TPU v7x, 32 devices: a whole 2x2x4 slice. The times are simulated.
32 devices in a mesh: ch: 8 (over z, x), seq: 4 (over y, core).
Axes of the slice: x: 2, y: 2, z: 4, core: 2. Of those that a mesh axis runs over, the one named last changes fastest.
Arguments:
- tokens: bfloat16 [4, 2048, 2, 1024], P('seq', 'ch'), may hold values from -6 to 6
- lengths: int32 [4, 2], P('seq'), may hold values from 257 to 2048, as said below
- in_weight: bfloat16 [1024, 3072], P(('ch', 'seq')), may hold values from -0.1875 to 0.1875
- out_weight: bfloat16 [1024, 1024], P(('ch', 'seq')), may hold values from -0.1875 to 0.1875
- up_weight: bfloat16 [1024, 4096], P(('ch', 'seq')), may hold values from -0.1875 to 0.1875
- down_weight: bfloat16 [4096, 1024], P(('ch', 'seq')), may hold values from -0.09375 to 0.09375
- gain_one: bfloat16 [1024], P(('ch', 'seq')), may hold values from 0.5 to 1.5
- gain_two: bfloat16 [1024], P(('ch', 'seq')), may hold values from 0.5 to 1.5
- conv_taps: float32 [3, 3, 1024], P(None, None, 'ch'), may hold values from -3.5 to 3.5
- skip_gain: float32 [1024], P('ch'), may hold values from -4 to 4
- filter_first: float32 [33, 64], replicated, may hold values from -1 to 1
- filter_bias: float32 [64], replicated, may hold values from -1 to 1
- frequency: float32 [64], replicated, may hold values from 0.5 to 2
- filter_second: float32 [64, 1024], P(None, 'ch'), may hold values from -0.046875 to 0.046875
- cotangent: bfloat16 [4, 2048, 2, 1024], P('seq', 'ch'), may hold values from -6 to 6
Outputs:
- output: bfloat16 [4, 2048, 2, 1024], P('seq', 'ch')
- grad_tokens: bfloat16 [4, 2048, 2, 1024], P('seq', 'ch')
- grad_in_weight: float32 [1024, 3072], P(('ch', 'seq'))
- grad_out_weight: float32 [1024, 1024], P(('ch', 'seq'))
- grad_up_weight: float32 [1024, 4096], P(('ch', 'seq'))
- grad_down_weight: float32 [4096, 1024], P(('ch', 'seq'))
- grad_gain_one: float32 [1024], P(('ch', 'seq'))
- grad_gain_two: float32 [1024], P(('ch', 'seq'))
- grad_conv_taps: float32 [3, 3, 1024], P(None, None, 'ch')
- grad_skip_gain: float32 [1024], P('ch')
- grad_filter_first: float32 [33, 64], replicated
- grad_filter_bias: float32 [64], replicated
- grad_frequency: float32 [64], replicated
- grad_filter_second: float32 [64, 1024], P(None, 'ch')
Inputs may be any that keep to these rules, and one draw needn't show every extreme that they name: `lengths`: in every group one bucket, which one drawn from the seed, holds a sequence of all 2048 positions.
All inputs are finite; a program needn't handle non-finite values.
Results may differ from a plain program's by a relative error of at most 0.012.
Values may be sent and summed in bfloat16 or wider, within the bound.
A program may use at most 256 MiB of HBM per device.

v0:
```python
import functools
import math

import jax
import jax.numpy as jnp
import numpy as np
from jax import lax
from jax.experimental import pallas as pl
from jax.experimental.pallas import tpu as pltpu
from jax.sharding import PartitionSpec as P

EPS = 1e-05
SLOW_RATE = math.log(100.0) / 1.5
FAST_RATE = math.log(100.0) / 0.3
HIGH = lax.Precision.HIGHEST
BF = jnp.bfloat16
F32 = jnp.float32
MESH = pl.DeviceIdType.MESH
VMEM_LIMIT = 56 << 20


def layer_norm(values, gain):
    centre = values - jnp.mean(values, axis=-1, keepdims=True)
    spread = jnp.mean(centre * centre, axis=-1, keepdims=True)
    return centre * lax.rsqrt(spread + EPS) * gain


def positions_table(length, features):
    steps = jnp.arange(length).astype(jnp.float32)
    scaled = steps / (length - 1)
    bands = (features - 1) // 2
    freqs = 0.0001 + (bands - 1 - 0.0001) * jnp.arange(bands).astype(jnp.float32) / (bands - 1)
    angles = freqs[None, :] * (2.0 * math.pi * steps / length)[:, None]
    return jnp.concatenate([scaled[:, None], jnp.cos(angles), -jnp.sin(angles)], axis=1)


def decay_table(length, chan_start, count, width):
    scaled = jnp.arange(length).astype(jnp.float32) / (length - 1)
    chans = (chan_start + jnp.arange(count)).astype(jnp.float32)
    rates = SLOW_RATE + (FAST_RATE - SLOW_RATE) * chans / (width - 1)
    return jnp.exp(-scaled[:, None] * rates[None, :])


def filter_hidden(filter_first, filter_bias, frequency, table):
    inner = jnp.dot(table, filter_first, precision=HIGH) + filter_bias
    return jnp.sin(frequency * inner)


def block_tables(size):
    k = np.arange(size)[:, None]
    t = np.arange(size)[None, :]
    angle = 2.0 * np.pi * ((k * t) % (2 * size)) / (2 * size)
    real = np.cos(angle)
    imag = -np.sin(angle)
    imag[0] = np.where(np.arange(size) % 2 == 0, 1.0, -1.0)
    full = np.concatenate([real, imag], axis=0).astype(np.float32)
    high = full.astype(jnp.bfloat16)
    low = (full - high.astype(np.float32)).astype(jnp.bfloat16)
    weight = np.full((size, 1), 1.0 / size, np.float32)
    weight[0] = 0.5 / size
    sign = np.where(np.arange(size) % 2 == 0, 1.0, -1.0).astype(np.float32)[:, None]
    lanes = np.zeros((size, 128), np.float32)
    lanes[:, 0:1] = weight
    lanes[:, 1:2] = sign
    lanes[:, 2] = 1.0
    lanes[0, 2] = 0.0
    return high, low, high.T.copy(), low.T.copy(), lanes


def split_high(values):
    high = values.astype(BF)
    return high, (values - high.astype(F32)).astype(BF)


def mm(a, b):
    return jnp.dot(a, b, preferred_element_type=F32)


def spectra(fh, fl, source, target, blocks, first=0):
    def step(i, carry):
        block = source[i]
        target[i] = mm(fh[...], block) + mm(fl[...], block)
        return carry

    lax.fori_loop(first, blocks, step, 0)


def filter_spectra(fh, fl, lanes, h_ref, abc, blocks, size):
    weight = lanes[:, 0:1]
    sign = lanes[:, 1:2]
    keep = lanes[:, 2:3]

    def step(j, carry):
        prev_re, prev_im = carry
        high, low = split_high(h_ref[j])
        now = mm(fh[...], high) + mm(fl[...], high) + mm(fh[...], low)
        now_re = now[:size]
        now_im = now[size:]
        g_re = (now_re + sign * prev_re) * weight
        g_im = (now_im + sign * prev_im) * weight
        abc[j, 0] = g_re
        abc[j, 1] = g_im * keep
        abc[j, 2] = jnp.where(keep > 0.5, g_re, g_im)
        return now_re, now_im

    zero = jnp.zeros((size, h_ref.shape[2]), F32)
    lax.fori_loop(0, blocks, step, (zero, zero))


def row_chunks(size, cols, body):
    width = min(128, cols)
    for lane in range(0, cols, width):

        def step(i, carry, lane=lane):
            body(pl.multiple_of(i * 8, 8), lane, width)
            return carry

        lax.fori_loop(0, size // 8, step, 0)


def products_forward(xs, abc, out, blocks, size):
    cols = xs.shape[2]

    def body(row, lane, width):
        re = [xs[i, pl.ds(row, 8), lane : lane + width] for i in range(blocks)]
        im = [xs[i, pl.ds(size + row, 8), lane : lane + width] for i in range(blocks)]
        a = [abc[j, 0, pl.ds(row, 8), lane : lane + width] for j in range(blocks)]
        b = [abc[j, 1, pl.ds(row, 8), lane : lane + width] for j in range(blocks)]
        c = [abc[j, 2, pl.ds(row, 8), lane : lane + width] for j in range(blocks)]
        for m in range(blocks):
            sum_re = re[0] * a[m] - im[0] * b[m]
            sum_im = re[0] * b[m] + im[0] * c[m]
            for i in range(1, m + 1):
                sum_re = sum_re + (re[i] * a[m - i] - im[i] * b[m - i])
                sum_im = sum_im + (re[i] * b[m - i] + im[i] * c[m - i])
            out[m, pl.ds(row, 8), lane : lane + width] = sum_re
            out[m, pl.ds(size + row, 8), lane : lane + width] = sum_im

    row_chunks(size, cols, body)


def products_backward(xs, ds, abc, out, lanes, blocks, size):
    cols = xs.shape[2]

    def body(row, lane, width):
        here = pl.ds(row, 8)
        there = pl.ds(size + row, 8)
        piece = slice(lane, lane + width)
        x_re = [xs[i, here, piece] for i in range(blocks)]
        x_im = [xs[i, there, piece] for i in range(blocks)]
        d_re = [ds[i, here, piece] for i in range(blocks)]
        d_im = [ds[i, there, piece] for i in range(blocks)]
        a = [abc[j, 0, here, piece] for j in range(blocks)]
        b = [abc[j, 1, here, piece] for j in range(blocks)]
        c = [abc[j, 2, here, piece] for j in range(blocks)]
        for i in range(blocks):
            sum_re = d_re[i] * a[0] + d_im[i] * b[0]
            sum_im = d_im[i] * c[0] - d_re[i] * b[0]
            for m in range(i + 1, blocks):
                sum_re = sum_re + (d_re[m] * a[m - i] + d_im[m] * b[m - i])
                sum_im = sum_im + (d_im[m] * c[m - i] - d_re[m] * b[m - i])
            out[i, here, piece] = sum_re
            out[i, there, piece] = sum_im
        weight = lanes[here, 0:1]
        sign = lanes[here, 1:2]
        keep = lanes[here, 2:3] > 0.5
        later_re = None
        later_im = None
        for j in range(blocks - 1, -1, -1):
            rr = d_re[j] * x_re[0]
            ii = d_im[j] * x_im[0]
            cross = d_im[j] * x_re[0] - d_re[j] * x_im[0]
            for i in range(1, blocks - j):
                rr = rr + d_re[i + j] * x_re[i]
                ii = ii + d_im[i + j] * x_im[i]
                cross = cross + (d_im[i + j] * x_re[i] - d_re[i + j] * x_im[i])
            g_re = jnp.where(keep, rr + ii, rr) * weight
            g_im = jnp.where(keep, cross, ii) * weight
            abc[j, 0, here, piece] = g_re if later_re is None else g_re + sign * later_re
            abc[j, 1, here, piece] = g_im if later_im is None else g_im + sign * later_im
            later_re, later_im = g_re, g_im

    row_chunks(size, cols, body)


def inverse_of(th, tl, values):
    high, low = split_high(values)
    return mm(th[...], high) + mm(tl[...], high) + mm(th[...], low)


def inverse_blocks(th, tl, source, target, blocks):
    def step(m, carry):
        target[m] = inverse_of(th, tl, source[m]).astype(target.dtype)
        return carry

    lax.fori_loop(0, blocks, step, 0)


def filter_gradient(th, tl, abc, out, blocks, size):
    def step(j, carry):
        re_high, re_low = split_high(abc[j, 0])
        im_high, im_low = split_high(abc[j, 1])
        left, right = th[:, :size], th[:, size:]
        total = mm(left, re_high) + mm(right, im_high) + mm(left, re_low) + mm(right, im_low)
        total = total + mm(tl[:, :size], re_high) + mm(tl[:, size:], im_high)
        out[j] = total
        return carry

    lax.fori_loop(0, blocks, step, 0)


def conv_forward_kernel(dims, x_ref, h_ref, fh, fl, th, tl, lanes, out, xs, abc):
    blocks, size, buckets, chans = dims
    filter_spectra(fh, fl, lanes, h_ref, abc, blocks, size)
    spectra(fh, fl, x_ref, xs, blocks)
    products_forward(xs, abc, xs, blocks, size)
    inverse_blocks(th, tl, xs, out, blocks)


def conv_backward_kernel(dims, d_ref, x_ref, h_ref, fh, fl, th, tl, lanes, out, dh_ref, xs, ds, abc):
    blocks, size, buckets, chans = dims
    filter_spectra(fh, fl, lanes, h_ref, abc, blocks, size)
    spectra(fh, fl, x_ref, xs, blocks)
    spectra(fh, fl, d_ref, ds, blocks)
    products_backward(xs, ds, abc, ds, lanes, blocks, size)
    inverse_blocks(th, tl, ds, out, blocks)
    filter_gradient(th, tl, abc, dh_ref, blocks, size)


VM = pl.BlockSpec(memory_space=pltpu.VMEM)
ANYWHERE = pl.BlockSpec(memory_space=pl.ANY)


def conv_call(kernel, dims, operands, kinds, spectra_count):
    blocks, size, buckets, chans = dims
    cols = buckets * chans
    scratch = [pltpu.VMEM((blocks, 2 * size, cols), F32)] * spectra_count
    return pl.pallas_call(
        functools.partial(kernel, dims),
        out_shape=[jax.ShapeDtypeStruct((blocks, size, cols), kind) for kind in kinds],
        in_specs=[VM] * len(operands),
        out_specs=[VM] * len(kinds),
        scratch_shapes=scratch + [pltpu.VMEM((blocks, 3, size, cols), F32)],
        compiler_params=pltpu.CompilerParams(vmem_limit_bytes=VMEM_LIMIT),
    )(*operands)


def rows_to_blocks(rows, dims):
    blocks, size, buckets, chans = dims
    moved = lax.all_to_all(rows.reshape(buckets, size, blocks, chans), "ch", split_axis=2, concat_axis=0)
    return jnp.transpose(moved, (0, 2, 1, 3)).reshape(blocks, size, buckets * chans)


def blocks_to_rows(values, dims):
    blocks, size, buckets, chans = dims
    moved = lax.all_to_all(values.reshape(blocks, size, buckets, chans), "ch", split_axis=0, concat_axis=0)
    return jnp.transpose(moved, (2, 1, 0, 3)).reshape(buckets * size, blocks * chans)


def conv_forward(rows, filt, tables, dims):
    kept = rows_to_blocks(rows, dims)
    (out,) = conv_call(conv_forward_kernel, dims, (kept, filt) + tables, (BF,), 1)
    return blocks_to_rows(out, dims), kept


def conv_backward(rows, kept, filt, tables, dims):
    moved = rows_to_blocks(rows, dims)
    out, dfilt = conv_call(conv_backward_kernel, dims, (moved, kept, filt) + tables, (BF, F32), 2)
    return blocks_to_rows(out, dims), dfilt


class Place:
    def __init__(self):
        self.ch = lax.axis_index("ch")
        self.seq = lax.axis_index("seq")
        self.z, self.x = self.ch // 2, lax.rem(self.ch, 2)
        self.y, self.core = self.seq // 2, lax.rem(self.seq, 2)
        self.sibling = {"seq": self.y * 2 + (1 - self.core)}
        self.along_y = {"seq": (1 - self.y) * 2 + self.core}
        self.along_x = {"ch": self.z * 2 + (1 - self.x)}
        self.others = [self.z + 1 - 2 * lax.rem(self.z, 2), lax.rem(self.z + 2, 4), 3 - self.z]
        self.along_z = [{"ch": one * 2 + self.x} for one in self.others]
        self.ch_ahead = [lax.rem(self.ch + d, 8) for d in range(1, 8)]
        self.seq_ahead = [lax.rem(self.seq + d, 4) for d in range(1, 4)]


def greet(ids):
    barrier = pltpu.get_barrier_semaphore()
    for one in ids:
        pl.semaphore_signal(barrier, inc=1, device_id=one, device_id_type=MESH)
    pl.semaphore_wait(barrier, len(ids))


def wait_all(copies):
    for copy in copies:
        copy.wait()


def push(src, dst, send, recv, device):
    copy = pltpu.make_async_remote_copy(
        src_ref=src, dst_ref=dst, send_sem=send, recv_sem=recv, device_id=device, device_id_type=MESH
    )
    copy.start()
    return copy


class Gather:
    SLOTS = 36

    def __init__(self, place, shards, fulls, send, recv, local):
        self.p, self.shards, self.fulls = place, shards, fulls
        self.send, self.recv, self.local = send, recv, local
        self.copies = {}

    def go(self, i, name, slot, src, dst, device):
        self.copies[(i, name)] = push(src, dst, self.send.at[i, slot], self.recv.at[i, slot], device)

    def start(self):
        p = self.p
        for i, shard in enumerate(self.shards):
            mine = self.fulls[i].at[p.z, p.x, p.y, p.core]
            for d in range(3):
                self.go(i, ("z", d), d, shard, mine, p.along_z[d])
            self.go(i, ("x", 0), 3, shard, mine, p.along_x)
            self.go(i, ("y", 0), 7, shard, mine, p.along_y)
            self.go(i, ("c", 0), 19, shard, mine, p.sibling)
            copy = pltpu.make_async_copy(shard, mine, self.local.at[i])
            copy.start()
            self.copies[(i, "own")] = copy

    def pass_column(self, d):
        p = self.p
        for i in range(len(self.shards)):
            self.copies[(i, ("z", d))].wait_recv()
            here = self.fulls[i].at[p.others[d], p.x, p.y, p.core]
            self.go(i, ("x", d + 1), 4 + d, here, here, p.along_x)
            self.go(i, ("y", d + 1), 8 + d, here, here, p.along_y)
            self.go(i, ("c", d + 1), 20 + d, here, here, p.sibling)

    def pass_sides(self, n):
        p = self.p
        zz = p.z if n == 0 else p.others[n - 1]
        for i in range(len(self.shards)):
            half = self.shards[i].shape[0] // 2
            full = self.fulls[i]
            self.copies[(i, ("x", n))].wait_recv()
            top = full.at[zz, 1 - p.x, p.y, p.core, pl.ds(0, half)]
            self.go(i, ("top", n), 11 + n, top, top, p.along_y)
            whole = full.at[zz, 1 - p.x, p.y, p.core]
            self.go(i, ("c", 4 + n), 23 + n, whole, whole, p.sibling)
            self.copies[(i, ("y", n))].wait_recv()
            low = full.at[zz, p.x, 1 - p.y, p.core, pl.ds(half, half)]
            self.go(i, ("low", n), 15 + n, low, low, p.along_x)
            whole = full.at[zz, p.x, 1 - p.y, p.core]
            self.go(i, ("c", 8 + n), 27 + n, whole, whole, p.sibling)

    def pass_last(self, n):
        p = self.p
        zz = p.z if n == 0 else p.others[n - 1]
        for i in range(len(self.shards)):
            self.copies[(i, ("top", n))].wait_recv()
            self.copies[(i, ("low", n))].wait_recv()
            whole = self.fulls[i].at[zz, 1 - p.x, 1 - p.y, p.core]
            self.go(i, ("c", 12 + n), 31 + n, whole, whole, p.sibling)

    def finish(self):
        for (i, name), copy in self.copies.items():
            if name == "own":
                copy.wait()
            else:
                copy.wait_send()
                if name[0] == "c":
                    copy.wait_recv()

    def rest(self):
        for d in range(3):
            self.pass_column(d)
            self.pass_sides(d)
        self.pass_sides(3)
        for n in range(4):
            self.pass_last(n)
        self.finish()

    @classmethod
    def scratch(cls, count):
        return [
            pltpu.SemaphoreType.DMA((count, cls.SLOTS)),
            pltpu.SemaphoreType.DMA((count, cls.SLOTS)),
            pltpu.SemaphoreType.DMA((count,)),
        ]


def everyone(p):
    ids = []
    for d in range(8):
        for e in range(4):
            if d or e:
                ids.append({"ch": lax.rem(p.ch + d, 8), "seq": lax.rem(p.seq + e, 4)})
    return ids


def start_kernel(pack, tail, shard, consts, halo, full, packs, send, recv, halo_sems, *gather_sems):
    p = Place()
    ids = everyone(p)
    greet(ids)
    copies = [push(pack, packs.at[p.ch, p.seq], send.at[n], recv.at[n], one) for n, one in enumerate(ids)]
    copies.append(push(tail, halo, halo_sems.at[0], halo_sems.at[1], {"ch": lax.rem(p.ch + 1, 8)}))
    gather = Gather(p, [shard], [full], *gather_sems)
    gather.start()
    packs[p.ch, p.seq] = pack[...]
    wait_all(copies)
    row = lax.broadcasted_iota(jnp.int32, (16, 128), 0)
    for c in range(8):
        first = packs[c, 0]
        total = first + packs[c, 1] + packs[c, 2] + packs[c, 3]
        consts[:, c * 128 : (c + 1) * 128] = jnp.where(row < 10, first, total)
    gather.rest()


def start_call(pack, tail, shard):
    rows, cols = shard.shape
    consts, halo, full = pl.pallas_call(
        start_kernel,
        out_shape=[
            jax.ShapeDtypeStruct((16, 1024), F32),
            jax.ShapeDtypeStruct(tail.shape, BF),
            jax.ShapeDtypeStruct((4, 2, 2, 2, rows, cols), BF),
        ],
        in_specs=[VM, VM, ANYWHERE],
        out_specs=[VM, VM, ANYWHERE],
        scratch_shapes=[
            pltpu.VMEM((8, 4, 16, 128), F32),
            pltpu.SemaphoreType.DMA((31,)),
            pltpu.SemaphoreType.DMA((31,)),
            pltpu.SemaphoreType.DMA((2,)),
        ]
        + Gather.scratch(1),
        compiler_params=pltpu.CompilerParams(collective_id=4, has_side_effects=True, vmem_limit_bytes=VMEM_LIMIT),
    )(pack, tail, shard)
    return consts, halo, full.reshape(rows * 32, cols)


def lagged(u, buf, b, stream, lane, size, width):
    at = pl.ds(pl.multiple_of(stream * width + lane, 128), 128)
    rows = size * 2
    buf[pl.ds(0, 16)] = u[pl.ds(rows + 16 * b, 16), at].astype(F32)
    buf[pl.ds(16, size)] = u[pl.ds(b * size, size), at].astype(F32)
    return buf[pl.ds(16, size)], buf[pl.ds(15, size)], buf[pl.ds(14, size)]


def short_conv(u, buf, consts, b, stream, lane, size, width):
    now, one, two = lagged(u, buf, b, stream, lane, size, width)
    at = pl.ds(lane, 128)
    return consts[stream : stream + 1, at] * now + consts[3 + stream : 4 + stream, at] * one + consts[
        6 + stream : 7 + stream, at
    ] * two


def send_pieces(p, pieces, blocks_ref, send, recv, local, make):
    copies = []
    for d in range(8):
        block = lax.rem(p.ch + d + 1, 8)
        make(block)
        for b in range(2):
            dst = blocks_ref.at[p.ch, :, pl.ds(b * 128, 128)]
            if d < 7:
                copies.append(push(pieces.at[block, b], dst, send.at[d, b], recv.at[d, b], {"ch": block}))
            else:
                copy = pltpu.make_async_copy(pieces.at[block, b], dst, local.at[b])
                copy.start()
                copies.append(copy)
    return copies


def send_blocks(p, ys, blocks_ref, send, recv, local):
    copies = []
    for d in range(7):
        copies.append(
            push(ys.at[p.ch_ahead[d]], blocks_ref.at[p.ch], send.at[d], recv.at[d], {"ch": p.ch_ahead[d]})
        )
    copy = pltpu.make_async_copy(ys.at[p.ch], blocks_ref.at[p.ch], local)
    copy.start()
    return copies + [copy]


def forward_kernel(
    size,
    u,
    consts,
    mask,
    h_ref,
    fh,
    fl,
    th,
    tl,
    lanes,
    mixer,
    kept,
    convolved,
    xs,
    abc,
    ys,
    pieces,
    gates,
    mixes,
    bufs,
    send,
    recv,
    local,
    send_back,
    recv_back,
    local_back,
):
    p = Place()
    width = 1024
    greet([{"ch": one} for one in p.ch_ahead])

    def make(block):
        lane = pl.multiple_of(block * 128, 128)

        def step(b, carry):
            gates[block, b] = short_conv(u, bufs.at[0], consts, b, 0, lane, size, width)
            key = short_conv(u, bufs.at[1], consts, b, 1, lane, size, width)
            mix = key * short_conv(u, bufs.at[2], consts, b, 2, lane, size, width)
            mixes[block, b] = mix
            pieces[block, b] = mix.astype(BF)
            return carry

        for b in range(2):
            step(b, 0)

    arriving = send_pieces(p, pieces, kept, send, recv, local, make)
    filter_spectra(fh, fl, lanes, h_ref, abc, 8, size)
    wait_all(arriving)
    spectra(fh, fl, kept, xs, 8)
    products_forward(xs, abc, xs, 8, size)
    inverse_blocks(th, tl, xs, ys, 8)
    wait_all(send_blocks(p, ys, convolved, send_back, recv_back, local_back))
    for c in range(8):
        at = slice(c * 128, (c + 1) * 128)
        for b in range(2):
            rows = slice(b * size, (b + 1) * size)
            long_part = convolved[c, :, b * 128 : (b + 1) * 128].astype(F32) + consts[9:10, at] * mixes[c, b]
            mixer[rows, at] = (gates[c, b] * long_part * mask[rows]).astype(BF)


def backward_kernel(
    size,
    u,
    consts,
    mask,
    grad_mixer,
    convolved,
    kept,
    h_ref,
    fh,
    fl,
    th,
    tl,
    lanes,
    du,
    dh_ref,
    sums,
    xs,
    ds,
    abc,
    ys,
    pieces,
    arrived,
    returned,
    keys,
    values,
    dlongs,
    dcs,
    edge_in,
    bufs,
    send,
    recv,
    local,
    send_back,
    recv_back,
    local_back,
    edge_sems,
):
    p = Place()
    width = 1024
    greet([{"ch": one} for one in p.ch_ahead])
    sums[...] = jnp.zeros_like(sums)

    def make(block):
        lane = pl.multiple_of(block * 128, 128)
        at = pl.ds(lane, 128)
        skip = consts[9:10, at]
        total = jnp.zeros((1, 128), F32)
        for b in range(2):
            rows = pl.ds(b * size, size)
            gate = short_conv(u, bufs.at[0], consts, b, 0, lane, size, width)
            key = short_conv(u, bufs.at[1], consts, b, 1, lane, size, width)
            value = short_conv(u, bufs.at[2], consts, b, 2, lane, size, width)
            keys[block, b] = key
            values[block, b] = value
            mix = key * value
            masked = grad_mixer[rows, at].astype(F32) * mask[rows]
            dlong = masked * gate
            dlongs[block, b] = dlong
            pieces[block, b] = dlong.astype(BF)
            total = total + jnp.sum(dlong * mix, axis=0, keepdims=True)
            long_part = convolved[block, :, b * 128 : (b + 1) * 128].astype(F32) + skip * mix
            dcs[0, b, pl.ds(0, size), at] = masked * long_part
        sums[9:10, at] = total

    arriving = send_pieces(p, pieces, arrived, send, recv, local, make)
    filter_spectra(fh, fl, lanes, h_ref, abc, 8, size)
    spectra(fh, fl, kept, xs, 8)
    wait_all(arriving)
    spectra(fh, fl, arrived, ds, 8)
    products_backward(xs, ds, abc, ds, lanes, 8, size)
    inverse_blocks(th, tl, ds, ys, 8)
    leaving = send_blocks(p, ys, returned, send_back, recv_back, local_back)
    filter_gradient(th, tl, abc, dh_ref, 8, size)
    wait_all(leaving)

    def products(c, carry):
        at = pl.ds(pl.multiple_of(c * 128, 128), 128)
        skip = consts[9:10, at]
        for b in range(2):
            dmixed = returned[c, :, b * 128 : (b + 1) * 128].astype(F32) + skip * dlongs[c, b]
            dcs[1, b, pl.ds(0, size), at] = dmixed * values[c, b]
            dcs[2, b, pl.ds(0, size), at] = dmixed * keys[c, b]
        return carry

    lax.fori_loop(0, 8, products, 0)
    edge = push(
        dcs.at[:, :, pl.ds(0, 8)], edge_in, edge_sems.at[0], edge_sems.at[1], {"ch": lax.rem(p.ch + 7, 8)}
    )

    def taps(c, carry):
        lane = pl.multiple_of(c * 128, 128)
        at = pl.ds(lane, 128)
        for stream in range(3):
            totals = [jnp.zeros((1, 128), F32)] * 3
            for b in range(2):
                parts = lagged(u, bufs.at[stream], b, stream, lane, size, width)
                grad = dcs[stream, b, pl.ds(0, size), at]
                for lag in range(3):
                    totals[lag] = totals[lag] + jnp.sum(grad * parts[lag], axis=0, keepdims=True)
            for lag in range(3):
                row = 3 * lag + stream
                sums[row : row + 1, at] = totals[lag]
        return carry

    lax.fori_loop(0, 8, taps, 0)
    edge.wait()
    inside = jnp.where(p.ch < 7, 1.0, 0.0)

    def streams(c, carry):
        lane = pl.multiple_of(c * 128, 128)
        at = pl.ds(lane, 128)
        for stream in range(3):
            out = pl.ds(pl.multiple_of(stream * width + lane, 128), 128)
            for b in range(2):
                dcs[stream, b, pl.ds(size, 8), at] = edge_in[stream, b, :, at] * inside
                total = consts[stream : stream + 1, at] * dcs[stream, b, pl.ds(0, size), at]
                total = total + consts[3 + stream : 4 + stream, at] * dcs[stream, b, pl.ds(1, size), at]
                total = total + consts[6 + stream : 7 + stream, at] * dcs[stream, b, pl.ds(2, size), at]
                du[pl.ds(b * size, size), out] = total.astype(BF)
        return carry

    lax.fori_loop(0, 8, streams, 0)


def exchange_sems():
    pieces = [pltpu.SemaphoreType.DMA((7, 2))] * 2 + [pltpu.SemaphoreType.DMA((2,))]
    return pieces + [pltpu.SemaphoreType.DMA((7,))] * 2 + [pltpu.SemaphoreType.DMA]


def forward_call(u, consts, mask, filt, tables, size):
    rows = 2 * size
    block = (8, size, 256)
    piece = (8, 2, size, 128)
    operands = (u, consts, mask, filt) + tables
    return pl.pallas_call(
        functools.partial(forward_kernel, size),
        out_shape=[jax.ShapeDtypeStruct((rows, 1024), BF)] + [jax.ShapeDtypeStruct(block, BF)] * 2,
        in_specs=[VM] * len(operands),
        out_specs=[VM] * 3,
        scratch_shapes=[
            pltpu.VMEM((8, 2 * size, 256), F32),
            pltpu.VMEM((8, 3, size, 256), F32),
            pltpu.VMEM(block, BF),
            pltpu.VMEM(piece, BF),
            pltpu.VMEM(piece, F32),
            pltpu.VMEM(piece, F32),
            pltpu.VMEM((3, size + 16, 128), F32),
        ]
        + exchange_sems(),
        compiler_params=pltpu.CompilerParams(collective_id=1, has_side_effects=True, vmem_limit_bytes=VMEM_LIMIT),
    )(*operands)


def backward_call(u, consts, mask, grad_mixer, convolved, kept, filt, tables, size):
    rows = 2 * size
    block = (8, size, 256)
    piece = (8, 2, size, 128)
    operands = (u, consts, mask, grad_mixer, convolved, kept, filt) + tables
    return pl.pallas_call(
        functools.partial(backward_kernel, size),
        out_shape=[
            jax.ShapeDtypeStruct((rows, 3072), BF),
            jax.ShapeDtypeStruct(block, F32),
            jax.ShapeDtypeStruct((16, 1024), F32),
        ],
        in_specs=[VM] * len(operands),
        out_specs=[VM] * 3,
        scratch_shapes=[
            pltpu.VMEM((8, 2 * size, 256), F32),
            pltpu.VMEM((8, 2 * size, 256), F32),
            pltpu.VMEM((8, 3, size, 256), F32),
            pltpu.VMEM(block, BF),
            pltpu.VMEM(piece, BF),
            pltpu.VMEM(block, BF),
            pltpu.VMEM(block, BF),
            pltpu.VMEM(piece, F32),
            pltpu.VMEM(piece, F32),
            pltpu.VMEM(piece, F32),
            pltpu.VMEM((3, 2, size + 8, 1024), F32),
            pltpu.VMEM((3, 2, 8, 1024), F32),
            pltpu.VMEM((3, size + 16, 128), F32),
        ]
        + exchange_sems()
        + [pltpu.SemaphoreType.DMA((2,))],
        compiler_params=pltpu.CompilerParams(collective_id=2, has_side_effects=True, vmem_limit_bytes=VMEM_LIMIT),
    )(*operands)


def add_rows(target, other):
    return (target.astype(F32) + other.astype(F32)).astype(BF)


def scatter_kernel(count, *refs):
    grads = refs[:count]
    small_vec, small_sec, small_fst = refs[count : count + 3]
    outs = refs[count + 3 : 2 * count + 3]
    small_out = refs[2 * count + 3]
    rest = refs[2 * count + 4 :]
    own = rest[:count]
    acc = rest[count : 2 * count]
    one_a = rest[2 * count : 3 * count]
    one_b = rest[3 * count : 4 * count]
    two_a = rest[4 * count : 5 * count]
    two_b = rest[5 * count : 6 * count]
    three = rest[6 * count : 7 * count]
    gathered, joined, send, recv, local, small_send, small_recv = rest[7 * count :]

    p = Place()
    ch, seq, z, x, y, core = p.ch, p.seq, p.z, p.x, p.y, p.core
    sibling, along_y, along_x, along_z, others = p.sibling, p.along_y, p.along_x, p.along_z, p.others
    ch_ahead, seq_ahead = p.ch_ahead, p.seq_ahead
    ch_count, seq_count = 8, 4
    greet([{"ch": one} for one in ch_ahead] + [{"seq": one} for one in seq_ahead])

    def remote(src, dst, slot, array, device):
        copy = pltpu.make_async_remote_copy(
            src_ref=src,
            dst_ref=dst,
            send_sem=send.at[array, slot],
            recv_sem=recv.at[array, slot],
            device_id=device,
            device_id_type=MESH,
        )
        copy.start()
        return copy

    core_copies, own_copies = [], []
    for i in range(count):
        core_copies.append(remote(grads[i].at[:, :, :, 1 - core], acc[i], 0, i, sibling))
        copy = pltpu.make_async_copy(grads[i].at[:, :, :, core], own[i], local.at[i])
        copy.start()
        own_copies.append(copy)

    vec_rows = small_vec.shape[0]
    fst_rows = small_fst.shape[0]
    sec_rows = small_sec.shape[0]
    small_copies = []
    for d in range(ch_count - 1):
        lane = pl.multiple_of(ch_ahead[d] * 128, 128)
        pairs = (
            (small_vec.at[:, pl.ds(lane, 128)], gathered.at[ch, pl.ds(0, vec_rows)]),
            (small_fst, gathered.at[ch, pl.ds(vec_rows, fst_rows)]),
        )
        for s in range(2):
            copy = pltpu.make_async_remote_copy(
                src_ref=pairs[s][0],
                dst_ref=pairs[s][1],
                send_sem=small_send.at[2 * d + s],
                recv_sem=small_recv.at[2 * d + s],
                device_id={"ch": ch_ahead[d]},
                device_id_type=MESH,
            )
            copy.start()
            small_copies.append(copy)
    gathered[ch, :vec_rows] = small_vec[:, pl.ds(pl.multiple_of(ch * 128, 128), 128)]
    gathered[ch, vec_rows:] = small_fst[...]

    one_copies = [None] * count
    two_copies = [None] * count
    three_copies = [None] * count

    def stage_core(i):
        own_copies[i].wait()
        core_copies[i].wait()

        def step(n, carry):
            zz, xy = n // 4, lax.rem(n, 4)
            xx, yy = xy // 2, lax.rem(xy, 2)
            acc[i][zz, xx, yy] = add_rows(acc[i][zz, xx, yy], own[i][zz, xx, yy])
            return carry

        lax.fori_loop(0, 16, step, 0)
        half = acc[i].shape[3] // 2
        one_copies[i] = (
            remote(acc[i].at[:, :, 1 - y, pl.ds(0, half)], one_a[i], 1, i, along_y),
            remote(acc[i].at[:, 1 - x, :, pl.ds(half, half)], one_b[i], 2, i, along_x),
        )

    def stage_one(i):
        wait_all(one_copies[i])
        half = acc[i].shape[3] // 2

        def step(n, carry):
            zz, w = n // 2, lax.rem(n, 2)
            acc[i][zz, w, y, :half] = add_rows(acc[i][zz, w, y, :half], one_a[i][zz, w])
            acc[i][zz, x, w, half:] = add_rows(acc[i][zz, x, w, half:], one_b[i][zz, w])
            return carry

        lax.fori_loop(0, 8, step, 0)
        two_copies[i] = (
            remote(acc[i].at[:, 1 - x, y, pl.ds(0, half)], two_a[i], 3, i, along_x),
            remote(acc[i].at[:, x, 1 - y, pl.ds(half, half)], two_b[i], 4, i, along_y),
        )

    def stage_two(i):
        wait_all(two_copies[i])
        half = acc[i].shape[3] // 2

        def step(zz, carry):
            acc[i][zz, x, y, :half] = add_rows(acc[i][zz, x, y, :half], two_a[i][zz])
            acc[i][zz, x, y, half:] = add_rows(acc[i][zz, x, y, half:], two_b[i][zz])
            return carry

        lax.fori_loop(0, 4, step, 0)
        three_copies[i] = [
            remote(acc[i].at[others[d], x, y], three[i].at[d], 5 + d, i, along_z[d]) for d in range(3)
        ]

    def stage_three(i):
        wait_all(three_copies[i])
        total = acc[i][z, x, y].astype(F32)
        for d in range(3):
            total = total + three[i][d].astype(F32)
        outs[i][...] = total

    stages = (stage_core, stage_one, stage_two, stage_three)
    for time in range(count + 3):
        for s in range(4):
            if 0 <= time - s < count:
                stages[s](time - s)
        if time == 0:
            wait_all(small_copies)
            total = gathered[0]
            for n in range(1, ch_count):
                total = total + gathered[n]
            joined[seq, : vec_rows + fst_rows] = total
            joined[seq, vec_rows + fst_rows :] = small_sec[...]
            small_copies = []
            for d in range(seq_count - 1):
                copy = pltpu.make_async_remote_copy(
                    src_ref=joined.at[seq],
                    dst_ref=joined.at[seq],
                    send_sem=small_send.at[14 + d],
                    recv_sem=small_recv.at[14 + d],
                    device_id={"seq": seq_ahead[d]},
                    device_id_type=MESH,
                )
                copy.start()
                small_copies.append(copy)
    wait_all(small_copies)
    total = joined[0]
    for n in range(1, seq_count):
        total = total + joined[n]
    small_out[...] = total


def scatter_sums(grads, vec, sec, fst):
    count = len(grads)
    views = []
    outs = []
    bufs = [[] for _ in range(7)]
    for grad in grads:
        rows, cols = grad.shape[0] // 32, grad.shape[1]
        half = rows // 2
        views.append(grad.reshape(4, 2, 2, 2, rows, cols))
        outs.append(jax.ShapeDtypeStruct((rows, cols), F32))
        for place, shape in enumerate(
            (
                (4, 2, 2, rows, cols),
                (4, 2, 2, rows, cols),
                (4, 2, half, cols),
                (4, 2, half, cols),
                (4, half, cols),
                (4, half, cols),
                (3, rows, cols),
            )
        ):
            bufs[place].append(pltpu.VMEM(shape, BF))
    small = vec.shape[0] + fst.shape[0]
    scratch = [one for group in bufs for one in group]
    scratch += [
        pltpu.VMEM((8, small, 128), F32),
        pltpu.VMEM((4, small + sec.shape[0], 128), F32),
        pltpu.SemaphoreType.DMA((count, 8)),
        pltpu.SemaphoreType.DMA((count, 8)),
        pltpu.SemaphoreType.DMA((count,)),
        pltpu.SemaphoreType.DMA((17,)),
        pltpu.SemaphoreType.DMA((17,)),
    ]
    outs.append(jax.ShapeDtypeStruct((small + sec.shape[0], 128), F32))
    return pl.pallas_call(
        functools.partial(scatter_kernel, count),
        out_shape=outs,
        in_specs=[ANYWHERE] * count + [VM] * 3,
        out_specs=[VM] * (count + 1),
        scratch_shapes=scratch,
        compiler_params=pltpu.CompilerParams(
            collective_id=3, has_side_effects=True, vmem_limit_bytes=VMEM_LIMIT
        ),
    )(*views, vec, sec, fst)


def general_body(
    tokens,
    lengths,
    in_weight,
    out_weight,
    up_weight,
    down_weight,
    gain_one,
    gain_two,
    conv_taps,
    skip_gain,
    filter_first,
    filter_bias,
    frequency,
    filter_second,
    cotangent,
):
    ch_count = lax.axis_size("ch")
    ch_place = lax.axis_index("ch")
    size = tokens.shape[1]
    buckets = tokens.shape[2]
    width = tokens.shape[3]
    chans = skip_gain.shape[0]
    length = size * ch_count
    rows = size * buckets
    dims = (ch_count, size, buckets, chans)
    tables = tuple(jnp.asarray(one) for one in block_tables(size))

    def gather(shard):
        return lax.all_gather(shard, ("ch", "seq"), axis=0, tiled=True)

    full_in = gather(in_weight)
    full_gain_one = gather(gain_one).astype(F32)
    full_gain_two = gather(gain_two).astype(F32)
    full_out = gather(out_weight)
    full_up = gather(up_weight)
    full_down = gather(down_weight)

    local = ch_place * size + jnp.arange(size, dtype=jnp.int32)
    mask = (local[None, :] < lengths[0][:, None]).astype(F32).reshape(rows, 1)
    before = ch_place * size - 2 + jnp.arange(2, dtype=jnp.int32)
    mask_before = (before[None, :] < lengths[0][:, None]).astype(F32).reshape(2 * buckets, 1)
    chain = [(i, i + 1) for i in range(ch_count - 1)]
    halo = lax.ppermute(tokens[0, size - 2 :], "ch", chain)
    x_zero = jnp.swapaxes(tokens[0], 0, 1).reshape(rows, width).astype(F32) * mask
    x_before = jnp.swapaxes(halo, 0, 1).reshape(2 * buckets, width).astype(F32) * mask_before

    taps_full = lax.all_gather(conv_taps.reshape(9, chans), "ch", axis=1, tiled=True).reshape(3, 3, width)
    skip_full = lax.all_gather(skip_gain.reshape(1, chans), "ch", axis=1, tiled=True)

    table = positions_table(length, filter_first.shape[0])
    hidden = filter_hidden(filter_first, filter_bias, frequency, table)
    decay = decay_table(length, ch_place * chans, chans, width)
    filt = jnp.dot(hidden, filter_second, precision=HIGH) * decay
    filt_blocks = jnp.tile(filt.reshape(ch_count, size, chans), (1, 1, buckets))

    normed_one = layer_norm(x_zero, full_gain_one).astype(BF)
    normed_before = layer_norm(x_before, full_gain_one).astype(BF)
    streams = jnp.dot(normed_one, full_in, preferred_element_type=F32).astype(BF)
    streams_before = jnp.dot(normed_before, full_in, preferred_element_type=F32).astype(BF)
    lag = jnp.concatenate(
        [streams_before.reshape(buckets, 2, 3, width), streams.reshape(buckets, size, 3, width)], axis=1
    ).astype(F32)
    lag_zero, lag_one, lag_two = lag[:, 2:], lag[:, 1:-1], lag[:, :-2]
    conv = taps_full[0] * lag_zero + taps_full[1] * lag_one + taps_full[2] * lag_two
    gate = conv[:, :, 0].reshape(rows, width)
    key_part = conv[:, :, 1].reshape(rows, width)
    value_part = conv[:, :, 2].reshape(rows, width)
    mixed = key_part * value_part

    convolved, kept = conv_forward(mixed.astype(BF), filt_blocks, tables, dims)
    long_part = convolved.astype(F32) + skip_full * mixed
    mixer = (gate * long_part * mask).astype(BF)
    after_mix = x_zero + jnp.dot(mixer, full_out, preferred_element_type=F32)
    normed_two = layer_norm(after_mix, full_gain_two).astype(BF)
    inner_act = jnp.dot(normed_two, full_up, preferred_element_type=F32)
    active = jax.nn.gelu(inner_act).astype(BF)
    result = (after_mix + jnp.dot(active, full_down, preferred_element_type=F32)).astype(BF)
    result = jnp.swapaxes(result.reshape(buckets, size, width), 0, 1).reshape(1, size, buckets, width)

    grad_result = jnp.swapaxes(cotangent[0], 0, 1).reshape(rows, width)
    grad_active = jnp.dot(grad_result, full_down.T, preferred_element_type=F32)
    _, gelu_pull = jax.vjp(jax.nn.gelu, inner_act)
    grad_inner = gelu_pull(grad_active)[0].astype(BF)
    grad_down = jnp.dot(active.T, grad_result, preferred_element_type=F32)
    grad_up = jnp.dot(normed_two.T, grad_inner, preferred_element_type=F32)
    grad_normed_two = jnp.dot(grad_inner, full_up.T, preferred_element_type=F32)
    _, norm_two_pull = jax.vjp(layer_norm, after_mix, full_gain_two)
    grad_after_part, grad_gain_two = norm_two_pull(grad_normed_two)
    grad_after = grad_result.astype(F32) + grad_after_part
    grad_mix = grad_after.astype(BF)
    grad_out = jnp.dot(mixer.T, grad_mix, preferred_element_type=F32)
    grad_mixer = jnp.dot(grad_mix, full_out.T, preferred_element_type=F32).astype(BF)
    grad_masked = grad_mixer.astype(F32) * mask
    grad_gate = grad_masked * long_part
    grad_long = grad_masked * gate
    grad_skip = jnp.sum(grad_long * mixed, axis=0)
    grad_convolved, grad_filt = conv_backward(grad_long.astype(BF), kept, filt_blocks, tables, dims)
    grad_mixed = grad_convolved.astype(F32) + skip_full * grad_long
    grad_conv = jnp.stack([grad_gate, grad_mixed * value_part, grad_mixed * key_part], axis=1)
    grad_conv = grad_conv.reshape(buckets, size, 3, width)
    grad_taps = jnp.stack(
        [
            jnp.sum(grad_conv * lag_zero, axis=(0, 1)),
            jnp.sum(grad_conv * lag_one, axis=(0, 1)),
            jnp.sum(grad_conv * lag_two, axis=(0, 1)),
        ],
        axis=0,
    )
    next_rows = lax.ppermute(grad_conv[:, :2], "ch", [(j, i) for i, j in chain])
    ahead = jnp.concatenate([grad_conv, next_rows], axis=1)
    grad_streams = taps_full[0] * ahead[:, :-2] + taps_full[1] * ahead[:, 1:-1] + taps_full[2] * ahead[:, 2:]
    grad_projected = grad_streams.astype(BF).reshape(rows, 3 * width)
    grad_in = jnp.dot(normed_one.T, grad_projected, preferred_element_type=F32)
    grad_normed_one = jnp.dot(grad_projected, full_in.T, preferred_element_type=F32)
    _, norm_one_pull = jax.vjp(layer_norm, x_zero, full_gain_one)
    grad_zero_part, grad_gain_one = norm_one_pull(grad_normed_one)
    grad_input = ((grad_after + grad_zero_part) * mask).astype(BF)
    grad_input = jnp.swapaxes(grad_input.reshape(buckets, size, width), 0, 1).reshape(1, size, buckets, width)

    grad_filt = jnp.sum(grad_filt.reshape(length, buckets, chans), axis=1)
    grad_raw = grad_filt * decay
    grad_second = jnp.dot(hidden.T, grad_raw, precision=HIGH)
    grad_hidden = jnp.dot(grad_raw, filter_second.T, precision=HIGH)

    def hidden_of(first_layer, first_shift, freq_values):
        return filter_hidden(first_layer, first_shift, freq_values, table)

    _, hidden_pull = jax.vjp(hidden_of, filter_first, filter_bias, frequency)
    grad_first, grad_bias, grad_freq = hidden_pull(grad_hidden)

    sum_in, sum_out, sum_up, sum_down, sum_gain_one, sum_gain_two = (
        lax.psum_scatter(one, ("ch", "seq"), scatter_dimension=0, tiled=True)
        for one in (grad_in, grad_out, grad_up, grad_down, grad_gain_one, grad_gain_two)
    )
    sum_second = lax.psum(grad_second, "seq")
    all_taps, all_skip, sum_first, sum_bias, sum_freq = lax.psum(
        (grad_taps, grad_skip, grad_first, grad_bias, grad_freq), ("ch", "seq")
    )
    sum_taps = lax.dynamic_slice_in_dim(all_taps, ch_place * chans, chans, 2)
    sum_skip = lax.dynamic_slice_in_dim(all_skip, ch_place * chans, chans, 0)
    return (
        result,
        grad_input,
        sum_in,
        sum_out,
        sum_up,
        sum_down,
        sum_gain_one,
        sum_gain_two,
        sum_taps,
        sum_skip,
        sum_first,
        sum_bias,
        sum_freq,
        sum_second,
    )


def slice_body(
    tokens,
    lengths,
    in_weight,
    out_weight,
    up_weight,
    down_weight,
    gain_one,
    gain_two,
    conv_taps,
    skip_gain,
    filter_first,
    filter_bias,
    frequency,
    filter_second,
    cotangent,
):
    ch_place = lax.axis_index("ch")
    seq_place = lax.axis_index("seq")
    size = tokens.shape[1]
    buckets = tokens.shape[2]
    width = tokens.shape[3]
    chans = skip_gain.shape[0]
    length = size * 8
    rows = size * buckets
    part = gain_one.shape[0]
    emb, filt_width = filter_first.shape
    tables = tuple(jnp.asarray(one) for one in block_tables(size))

    lane = jnp.arange(chans) // part == seq_place
    gains = jnp.stack([gain_one, gain_two]).astype(F32)
    gains = jnp.where(lane[None, :], jnp.tile(gains, (1, chans // part)), 0.0)
    pack = jnp.concatenate([conv_taps.reshape(9, chans), skip_gain[None], gains, jnp.zeros((4, chans), F32)])
    by_bucket = jnp.swapaxes(tokens[0], 0, 1)
    consts, halo, full_in = start_call(pack, by_bucket[:, size - 16 :], in_weight)

    def gather(shard):
        return lax.all_gather(shard, ("ch", "seq"), axis=0, tiled=True)

    full_out = gather(out_weight)
    full_up = gather(up_weight)
    full_down = gather(down_weight)
    full_gain_one = consts[10]
    full_gain_two = consts[11]

    local = ch_place * size + jnp.arange(size, dtype=jnp.int32)
    mask = (local[None, :] < lengths[0][:, None]).astype(F32).reshape(rows, 1)
    before = ch_place * size - 16 + jnp.arange(16, dtype=jnp.int32)
    inside = (before[None, :] < lengths[0][:, None]) & (before >= 0)[None, :]
    x_zero = by_bucket.reshape(rows, width).astype(F32) * mask
    x_before = halo.reshape(16 * buckets, width).astype(F32) * inside.astype(F32).reshape(16 * buckets, 1)
    normed_one = layer_norm(x_zero, full_gain_one).astype(BF)
    normed_before = layer_norm(x_before, full_gain_one).astype(BF)
    streams = jnp.dot(
        jnp.concatenate([normed_one, normed_before]), full_in, preferred_element_type=F32
    ).astype(BF)

    table = positions_table(length, emb)
    hidden = filter_hidden(filter_first, filter_bias, frequency, table)
    decay = decay_table(length, ch_place * chans, chans, width)
    filt = jnp.dot(hidden, filter_second, precision=HIGH) * decay
    filt_blocks = jnp.tile(filt.reshape(8, size, chans), (1, 1, buckets))

    wide_mask = jnp.broadcast_to(mask, (rows, 128))
    mixer, kept, convolved = forward_call(streams, consts, wide_mask, filt_blocks, tables, size)
    after_mix = x_zero + jnp.dot(mixer, full_out, preferred_element_type=F32)
    normed_two = layer_norm(after_mix, full_gain_two).astype(BF)
    inner_act = jnp.dot(normed_two, full_up, preferred_element_type=F32)
    active = jax.nn.gelu(inner_act).astype(BF)
    result = (after_mix + jnp.dot(active, full_down, preferred_element_type=F32)).astype(BF)
    result = jnp.swapaxes(result.reshape(buckets, size, width), 0, 1).reshape(1, size, buckets, width)

    grad_result = jnp.swapaxes(cotangent[0], 0, 1).reshape(rows, width)
    grad_active = jnp.dot(grad_result, full_down.T, preferred_element_type=F32)
    _, gelu_pull = jax.vjp(jax.nn.gelu, inner_act)
    grad_inner = gelu_pull(grad_active)[0].astype(BF)
    grad_down = jnp.dot(active.T, grad_result, preferred_element_type=F32).astype(BF)
    grad_up = jnp.dot(normed_two.T, grad_inner, preferred_element_type=F32).astype(BF)
    grad_normed_two = jnp.dot(grad_inner, full_up.T, preferred_element_type=F32)
    _, norm_two_pull = jax.vjp(layer_norm, after_mix, full_gain_two)
    grad_after_part, grad_gain_two = norm_two_pull(grad_normed_two)
    grad_after = grad_result.astype(F32) + grad_after_part
    grad_mix = grad_after.astype(BF)
    grad_out = jnp.dot(mixer.T, grad_mix, preferred_element_type=F32).astype(BF)
    grad_mixer = jnp.dot(grad_mix, full_out.T, preferred_element_type=F32).astype(BF)

    grad_projected, grad_filt, sums = backward_call(
        streams, consts, wide_mask, grad_mixer, convolved, kept, filt_blocks, tables, size
    )
    grad_in = jnp.dot(normed_one.T, grad_projected, preferred_element_type=F32).astype(BF)
    grad_normed_one = jnp.dot(grad_projected, full_in.T, preferred_element_type=F32)
    _, norm_one_pull = jax.vjp(layer_norm, x_zero, full_gain_one)
    grad_zero_part, grad_gain_one = norm_one_pull(grad_normed_one)
    grad_input = ((grad_after + grad_zero_part) * mask).astype(BF)
    grad_input = jnp.swapaxes(grad_input.reshape(buckets, size, width), 0, 1).reshape(1, size, buckets, width)

    grad_filt = grad_filt.reshape(length, buckets * chans)
    grad_raw = (grad_filt[:, :chans] + grad_filt[:, chans:]) * decay
    grad_second = jnp.dot(hidden.T, grad_raw, precision=HIGH)
    grad_hidden = jnp.dot(grad_raw, filter_second.T, precision=HIGH)

    def hidden_of(first_layer, first_shift, freq_values):
        return filter_hidden(first_layer, first_shift, freq_values, table)

    _, hidden_pull = jax.vjp(hidden_of, filter_first, filter_bias, frequency)
    grad_first, grad_bias, grad_freq = hidden_pull(grad_hidden)
    vec = jnp.concatenate([sums[:10], grad_gain_one[None], grad_gain_two[None], jnp.zeros((4, width), F32)])
    fst = jnp.concatenate([grad_first, grad_bias[None], grad_freq[None]])
    fst = jnp.pad(fst, ((0, -fst.shape[0] % 8), (0, 128 - filt_width)))
    sum_down, sum_up, sum_in, sum_out, small = scatter_sums((grad_down, grad_up, grad_in, grad_out), vec, grad_second, fst)
    gain_sums = lax.dynamic_slice_in_dim(small[10:12], seq_place * part, part, 1)
    return (
        result,
        grad_input,
        sum_in,
        sum_out,
        sum_up,
        sum_down,
        gain_sums[0],
        gain_sums[1],
        small[:9].reshape(3, 3, chans),
        small[9],
        small[16 : 16 + emb, :filt_width],
        small[16 + emb, :filt_width],
        small[17 + emb, :filt_width],
        small[16 + fst.shape[0] :],
    )


def solution(mesh):
    placed = (
        P("seq", "ch", None, None),
        P("seq", None),
        P(("ch", "seq"), None),
        P(("ch", "seq"), None),
        P(("ch", "seq"), None),
        P(("ch", "seq"), None),
        P(("ch", "seq")),
        P(("ch", "seq")),
        P(None, None, "ch"),
        P("ch"),
        P(),
        P(),
        P(),
        P(None, "ch"),
        P("seq", "ch", None, None),
    )
    custom = dict(mesh.shape) == {"ch": 8, "seq": 4}
    return jax.shard_map(
        slice_body if custom else general_body,
        mesh=mesh,
        in_specs=placed,
        out_specs=(
            P("seq", "ch", None, None),
            P("seq", "ch", None, None),
            P(("ch", "seq"), None),
            P(("ch", "seq"), None),
            P(("ch", "seq"), None),
            P(("ch", "seq"), None),
            P(("ch", "seq")),
            P(("ch", "seq")),
            P(None, None, "ch"),
            P("ch"),
            P(),
            P(),
            P(),
            P(None, "ch"),
        ),
        check_vma=False,
    )
```

profile of v0, /device:TPU:0, one launch (start us, length us, event | category | flops | bytes accessed | tf_op | source)
XLA Modules:
  0.0 621.3 jit_solution(6049047244015922816)
XLA Ops:
  8.0 0.7 all-gather.8.cloned.1.call-update
  9.5 0.7 and_convert_fusion
  11.0 0.7 fusion.33
  11.8 2.6 copy.61
  16.9 0.8 copy-done.8
  17.7 3.6 convolution_multiply_fusion
  21.3 2.1 tile.22
  23.5 4.2 tile.23.h_ref
  29.1 55.5 %shard_map.299 = (f32[16,1024]{1,0:T(8,128)}, bf16[2,16,1024]{2,1,0:T(8,128)(2,1)}, bf16[4,2,2,2,32,3072]{5,4,3,2,1,0:T(8,128)(2,1)}) custom-call(f32[16,128]{1,0:T(8,128)} %maximum_maximum_fusion.1.pack, bf16[2,16,1024]{2,1,0:T(8,128)(2,1)} %slice.60.tail, bf16[32,3072]{1,0:T(8,128)(2,1)} %shard.1), custom_call_target="tpu_custom_call" | custom-call | tf_op jit(solution)/shard_map/pallas_call | solution.py:422
  84.6 1.0 multiply_reduce_fusion.9
  85.7 1.0 multiply_reduce_fusion.8
  86.8 0.8 fusion.39
  87.7 0.9 fusion.26
  89.1 8.4 %convolution_convert_fusion.3.u = bf16[544,3072]{1,0:T(8,128)(2,1)} fusion(bf16[1024,3072]{1,0:T(8,128)(2,1)} %bitcast.161, bf16[32,1024]{1,0:T(8,128)(2,1)S(1)} %fusion.26, bf16[512,1024]{1,0:T(8,128)(2,1)S(1)} %multiply_convert_fusion.3), kind=kOutput, calls=%fused_computation.13 | convolution fusion | flops 3426451456 | bytes 10747904 | tf_op jit(solution)/shard_map/dot_general | solution.py:1152
  97.6 0.8 broadcast_in_dim.32.mask
  98.4 75.6 %shard_map.300 = (bf16[512,1024]{1,0:T(8,128)(2,1)}, bf16[8,256,256]{2,1,0:T(8,128)(2,1)}, bf16[8,256,256]{2,1,0:T(8,128)(2,1)}) custom-call(bf16[544,3072]{1,0:T(8,128)(2,1)} %convolution_convert_fusion.3.u, f32[16,1024]{1,0:T(8,128)} %get-tuple-element.28.consts, f32[512,128]{1,0:T(8,128)} %broadcast_in_dim.32.mask, f32[8,256,256]{2,1,0:T(8,128)} %tile.23.h_ref, ...), custom_call_target="tpu_custom_call" | custom-call | tf_op jit(solution)/shard_map/pallas_call | solution.py:682
  174.0 3.3 fusion.40
  177.3 1.3 copy-done.5
  179.0 9.8 %all-gather.8.cloned.1.call-done = bf16[4096,1024]{1,0:T(8,128)(2,1)} async-done(((bf16[128,1024]{1,0:T(8,128)(2,1)}), bf16[4096,1024]{1,0:T(8,128)(2,1)}) %all-gather.8.cloned.1.call-update) | async-done | bytes 8388624 | tf_op jit(solution)/shard_map/all_gather | solution.py:1136
  188.8 10.1 %fusion.41 = f32[512,4096]{1,0:T(8,128)} fusion(bf16[512,1024]{1,0:T(8,128)(2,1)S(1)} %bitcast.120, bf16[4096,1024]{1,0:T(8,128)(2,1)} %all-gather.8.cloned.1.call-done), kind=kOutput, calls=%fused_computation.118 | convolution fusion | flops 4294967296 | bytes 17825792 | tf_op jit(solution)/shard_map/dot_general | solution.py:1172
  198.8 74.9 %all-gather.6.cloned.1.call-done = bf16[1024,4096]{1,0:T(8,128)(2,1)} async-done(((bf16[32,4096]{1,0:T(8,128)(2,1)}), bf16[1024,4096]{1,0:T(8,128)(2,1)}) %all-gather.6.cloned.1.call-update) | async-done | bytes 8388624 | tf_op jit(solution)/shard_map/all_gather | solution.py:1136
  273.7 19.3 %fusion.6 = (bf16[512,4096]{1,0:T(8,128)(2,1)}, f32[512,4096]{1,0:T(8,128)}) fusion(f32[512,4096]{1,0:T(8,128)} %fusion.41, bf16[1024,4096]{1,0:T(8,128)(2,1)} %all-gather.6.cloned.1.call-done, f32[512,1024]{1,0:T(8,128)} %copy-done.5, f32[1024]{0:T(1024)S(1)} %bitcast.148, f32[512]{0:T(512)S(1)} %fusion.27, f32[512]{0:T(512)S(1)} %broadcast_multiply_fusion), kind=kOutput, calls=%fused_computation.8 | convolution fusion | flops 4339007488 | bytes 31465472 | tf_op jit(solution)/shard_map/dot_general | solution.py:1166
  293.1 7.2 %multiply_reduce_fusion = (f32[1024]{0:T(1024)S(1)}, f32[512]{0:T(512)S(1)}, f32[512,1024]{1,0:T(8,128)S(1)}) fusion(f32[512,1024]{1,0:T(8,128)S(1)} %copy-done.6, f32[512]{0:T(512)S(1)} %fusion.27, f32[512]{0:T(512)S(1)} %broadcast_multiply_fusion, f32[1024]{0:T(1024)S(1)} %bitcast.149, bf16[512,4096]{1,0:T(8,128)(2,1)} %get-tuple-element.66, ...), kind=kOutput, calls=%fused_computation.20 | convolution fusion | flops 4298635776 | bytes 16791552 | tf_op jit(solution)/shard_map/dot_general | solution.py:1177
  300.3 0.7 fusion.38
  301.8 0.9 copy-done.27
  302.8 2.6 convolution_convert_fusion.4
  305.4 2.3 convolution_convert_fusion.5.grad_mixer
  307.7 73.0 %shard_map.301 = (bf16[512,3072]{1,0:T(8,128)(2,1)}, f32[8,256,256]{2,1,0:T(8,128)}, f32[16,1024]{1,0:T(8,128)}) custom-call(bf16[544,3072]{1,0:T(8,128)(2,1)} %convolution_convert_fusion.3.u, f32[16,1024]{1,0:T(8,128)} %get-tuple-element.28.consts, f32[512,128]{1,0:T(8,128)} %broadcast_in_dim.32.mask, ...), custom_call_target="tpu_custom_call" | custom-call | tf_op jit(solution)/shard_map/pallas_call | solution.py:706
  380.7 5.0 fusion.18.refs_5_
  385.6 4.9 multiply_reduce_fusion.7
  390.6 7.4 %convolution_convert_fusion = bf16[1024,4096]{1,0:T(8,128)(2,1)} fusion(bf16[512,4096]{1,0:T(8,128)(2,1)S(1)} %copy-done.28, f32[512,1024]{1,0:T(8,128)S(1)} %copy-done.6, f32[1024]{0:T(1024)S(1)} %bitcast.151, f32[512]{0:T(512)S(1)} %fusion.27, f32[512]{0:T(512)S(1)} %broadcast_multiply_fusion), kind=kOutput, calls=%fused_computation.10 | convolution fusion | flops 4301258752 | bytes 14688256 | tf_op jit(solution)/shard_map/dot_general | solution.py:1176
  398.0 3.9 multiply_reduce_fusion.1
  401.9 5.9 convolution_convert_fusion.2
  408.5 12.6 %convolution_convert_fusion.1 = bf16[4096,1024]{1,0:T(8,128)(2,1)} fusion(bf16[512,1024]{1,0:T(8,128)(2,1)S(1)} %bitcast.121, f32[512,4096]{1,0:T(8,128)} %get-tuple-element.67), kind=kOutput, calls=%fused_computation.11 | convolution fusion | flops 4318035968 | bytes 17825792 | tf_op jit(solution)/shard_map/dot_general | solution.py:1175
  421.1 0.7 maximum_maximum_fusion.refs_4_
  422.5 159.0 %shard_map.302 = (f32[128,1024]{1,0:T(8,128)}, f32[32,4096]{1,0:T(8,128)}, f32[32,3072]{1,0:T(8,128)}, f32[32,1024]{1,0:T(8,128)}, f32[120,128]{1,0:T(8,128)}) custom-call(bf16[4,2,2,2,128,1024]{5,4,3,2,1,0:T(8,128)(2,1)} %bitcast.123, bf16[4,2,2,2,32,4096]{5,4,3,2,1,0:T(8,128)(2,1)} %bitcast.122, bf16[4,2,2,2,32,3072]{5,4,3,2,1,0:T(8,128)(2,1)} %bitcast.124, ...), custom_call_target="tpu_custom_call" | custom-call | tf_op jit(solution)/shard_map/pallas_call | solution.py:928
  581.4 1.2 slice_bitcast_fusion.2
  583.3 1.3 slice_bitcast_fusion
  584.6 0.7 slice.54
  585.3 1.3 slice.56
  586.6 1.4 slice.59
  588.0 2.2 fusion.37
  591.4 2.5 multiply_convert_fusion.1
  593.9 10.9 %add_convert_fusion = bf16[512,1024]{1,0:T(8,128)(2,1)S(1)} fusion(f32[512,1024]{1,0:T(8,128)S(1)} %copy-done.7, bf16[4096,1024]{1,0:T(8,128)(2,1)} %all-gather.8.cloned.1.call-done, f32[512,4096]{1,0:T(8,128)} %get-tuple-element.67), kind=kOutput, calls=%fused_computation.26 | convolution fusion | flops 4314890240 | bytes 19922944 | tf_op jit(solution)/shard_map/dot_general | solution.py:1168
  604.9 6.7 %copy_bitcast_fusion = (bf16[1,256,2,1024]{3,2,1,0:T(2,128)(2,1)}, bf16[1,256,2,1024]{3,2,1,0:T(2,128)(2,1)}) fusion(bf16[2,256,1024]{2,1,0:T(8,128)(2,1)S(1)} %bitcast.126, bf16[2,256,1024]{2,1,0:T(8,128)(2,1)S(1)} %bitcast.131), kind=kLoop, calls=%fused_computation.44 | loop fusion | bytes 4194304 | tf_op jit(solution)/shard_map/reshape | solution.py:1193
  611.6 0.7 copy.66
  613.0 0.8 copy.68
  613.8 0.8 copy.69
  (116 shorter events, 12.0 us)
Async XLA Ops:
  7.2 10.5 %copy-start = (f32[64,128]{1,0:T(8,128)S(1)}, f32[64,128]{1,0:T(8,128)}, u32[]{:S(2)}) copy-start(f32[64,128]{1,0:T(8,128)} %param.33) | copy-start | bytes 98308
  7.2 7.1 %copy-start.2 = (bf16[1,256,2,1024]{3,2,1,0:T(2,128)(2,1)S(1)}, bf16[1,256,2,1024]{3,2,1,0:T(2,128)(2,1)}, u32[]{:S(2)}) copy-start(bf16[1,256,2,1024]{3,2,1,0:T(2,128)(2,1)} %param.20) | copy-start | bytes 3145732
  7.2 166.8 %all-gather.4.cloned.1.call-start = ((), (), s32[]{:S(2)}) async-start(), calls=%async_computation | async-start | bytes 2162688 | tf_op jit(solution)/shard_map/all_gather | solution.py:1136
  7.9 180.8 %all-gather.8.cloned.1.call-start = ((), (), s32[]{:S(2)}) async-start(), calls=%async_computation.2 | async-start | bytes 8650752 | tf_op jit(solution)/shard_map/all_gather | solution.py:1136
  8.7 265.1 %all-gather.6.cloned.1.call-start = ((), (), s32[]{:S(2)}) async-start(), calls=%async_computation.1 | async-start | bytes 8650752 | tf_op jit(solution)/shard_map/all_gather | solution.py:1136
  11.8 3.6 copy-start.20
  11.8 3.6 copy-start.13
  14.3 1.9 copy-start.19
  14.3 1.9 copy-start.23
  14.8 3.0 copy-start.21
  15.6 173.1 %copy-start.3 = (bf16[2,256,1024]{2,1,0:T(8,128)(2,1)}, bf16[2,256,1024]{2,1,0:T(8,128)(2,1)S(1)}, u32[]{:S(2)}) copy-start(bf16[2,256,1024]{2,1,0:T(8,128)(2,1)S(1)} %copy.40) | copy-start | bytes 3145732
  16.9 0.8 copy-start.8
  23.5 4.2 copy-start.10
  23.5 5.0 copy-start.22
  89.1 8.5 %copy-start.11 = (bf16[512,1024]{1,0:T(8,128)(2,1)}, bf16[512,1024]{1,0:T(8,128)(2,1)S(1)}, u32[]{:S(2)}) copy-start(bf16[512,1024]{1,0:T(8,128)(2,1)S(1)} %multiply_convert_fusion.3) | copy-start | bytes 3145732
  177.3 1.3 copy-start.5
  273.7 19.3 %copy-start.6 = (f32[512,1024]{1,0:T(8,128)S(1)}, f32[512,1024]{1,0:T(8,128)}, u32[]{:S(2)}) copy-start(f32[512,1024]{1,0:T(8,128)} %copy-done.5) | copy-start | bytes 6291460
  273.7 19.3 %copy-start.24 = (bf16[1024,4096]{1,0:T(8,128)(2,1)S(1)}, bf16[1024,4096]{1,0:T(8,128)(2,1)}, u32[]{:S(2)}) copy-start(bf16[1024,4096]{1,0:T(8,128)(2,1)} %all-gather.6.cloned.1.call-done) | copy-start | bytes 25165828
  300.3 1.2 copy-start.4
  301.5 1.2 copy-start.27
  302.8 2.6 copy-start.26
  307.7 73.0 %copy-start.9 = (f32[2048,64]{0,1:T(8,128)S(1)}, f32[2048,64]{0,1:T(8,128)}, u32[]{:S(2)}) copy-start(f32[2048,64]{0,1:T(8,128)} %copy-done.8) | copy-start | bytes 1572868
  380.6 9.9 %copy-start.28 = (bf16[512,4096]{1,0:T(8,128)(2,1)S(1)}, bf16[512,4096]{1,0:T(8,128)(2,1)}, u32[]{:S(2)}) copy-start(bf16[512,4096]{1,0:T(8,128)(2,1)} %get-tuple-element.66) | copy-start | bytes 12582916
  385.6 12.4 %slice-start = ((s8[6291456]{0:T(1024)(128)(4,1)}), s8[4194304]{0:T(1024)(128)(4,1)S(1)}, s32[]{:S(2)}) async-start(s8[6291456]{0:T(1024)(128)(4,1)} %bitcast.162), calls=%async_computation.3 | async-start | bytes 8388608
  390.6 7.4 %slice-start.1 = ((s8[6291456]{0:T(1024)(128)(4,1)}), s8[2097152]{0:T(1024)(128)(4,1)S(1)}, s32[]{:S(2)}) async-start(s8[6291456]{0:T(1024)(128)(4,1)} %bitcast.162), calls=%async_computation.4 | async-start | bytes 4194304
  390.6 7.4 %copy-start.25 = (bf16[512,3072]{1,0:T(8,128)(2,1)S(1)}, bf16[512,3072]{1,0:T(8,128)(2,1)}, u32[]{:S(2)}) copy-start(bf16[512,3072]{1,0:T(8,128)(2,1)} %get-tuple-element.34) | copy-start | bytes 9437188
  398.0 3.9 copy-start.12
  408.5 12.6 %copy-start.18 = (f32[16,1024]{1,0:T(8,128)S(1)}, f32[16,1024]{1,0:T(8,128)}, u32[]{:S(2)}) copy-start(f32[16,1024]{1,0:T(8,128)} %get-tuple-element.35) | copy-start | bytes 196612
  591.4 2.5 copy-start.7
  604.9 6.7 %copy-start.16 = (f32[32,3072]{1,0:T(8,128)S(1)}, f32[32,3072]{1,0:T(8,128)}, u32[]{:S(2)}) copy-start(f32[32,3072]{1,0:T(8,128)} %get-tuple-element.89) | copy-start | bytes 1179652
  604.9 7.5 %copy-start.17 = (f32[32,1024]{1,0:T(8,128)S(1)}, f32[32,1024]{1,0:T(8,128)}, u32[]{:S(2)}) copy-start(f32[32,1024]{1,0:T(8,128)} %get-tuple-element.90) | copy-start | bytes 393220
  604.9 8.1 %copy-start.15 = (f32[32,4096]{1,0:T(8,128)S(1)}, f32[32,4096]{1,0:T(8,128)}, u32[]{:S(2)}) copy-start(f32[32,4096]{1,0:T(8,128)} %get-tuple-element.91) | copy-start | bytes 1572868
  604.9 9.7 %copy-start.1 = (f32[64,128]{1,0:T(8,128)S(1)}, f32[64,128]{1,0:T(8,128)}, u32[]{:S(2)}) copy-start(f32[64,128]{1,0:T(8,128)} %param.33) | copy-start | bytes 98308
  611.6 2.2 copy-start.14
Sparse Core Ops, SparseCore 0:
  10.9 71.4 all-gather.3
  85.3 103.4 all-gather.7
  191.6 82.0 all-gather.5
where the time goes:
time: 628 us; the launch traced here: 621 us
  Pallas kernels  363 us (58%)
  matrix products  109 us (17%)
  waiting for transfers between devices  86.8 us (14%)
  local copies, waits for them, and re-layouts  33 us (5%)
  other arithmetic  15.2 us (2%)
  between operations  14.4 us (2%)
    pallas_call x1, Pallas kernels, scatter_sums(): pl.pallas_call(functools.partial(scatter_kernel, count), out_shape=outs,...  159 us
    all_gather x3, waiting for transfers between devices, gather(): return lax.all_gather(shard, ('ch', 'seq'), axis=0, tiled=True)  84.7 us
    pallas_call x1, Pallas kernels, forward_call(): pl.pallas_call(functools.partial(forward_kernel, size), out_shape=[jax.Sh...  75.6 us
    pallas_call x1, Pallas kernels, backward_call(): pl.pallas_call(functools.partial(backward_kernel, size), out_shape=[jax.S...  73 us
    pallas_call x1, Pallas kernels, start_call(): pl.pallas_call(start_kernel, out_shape=[jax.ShapeDtypeStruct((16, 1024),...  55.5 us
    dot_general x1, matrix products, slice_body(): inner_act = jnp.dot(normed_two, full_up, preferred_element_type=F32)  19.3 us
    dot_general x1, matrix products, slice_body(): jnp.dot(active.T, grad_result, preferred_element_type=F32).astype(BF)  12.6 us
  transfers between devices with their start and end apart: 3, of which 2 were waited for; matrix products, arithmetic and copies ran while one was open for 7% of the time, Pallas kernels for 21%

commit v1 on v0

--- a/solution.py
+++ b/solution.py
@@ -16,7 +16,7 @@
 BF = jnp.bfloat16
 F32 = jnp.float32
 MESH = pl.DeviceIdType.MESH
-VMEM_LIMIT = 56 << 20
+VMEM_LIMIT = 62 << 20
 
 
 def layer_norm(values, gain):
@@ -88,7 +88,6 @@
 def filter_spectra(fh, fl, lanes, h_ref, abc, blocks, size):
     weight = lanes[:, 0:1]
     sign = lanes[:, 1:2]
-    keep = lanes[:, 2:3]
 
     def step(j, carry):
         prev_re, prev_im = carry
@@ -96,91 +95,101 @@
         now = mm(fh[...], high) + mm(fl[...], high) + mm(fh[...], low)
         now_re = now[:size]
         now_im = now[size:]
-        g_re = (now_re + sign * prev_re) * weight
-        g_im = (now_im + sign * prev_im) * weight
-        abc[j, 0] = g_re
-        abc[j, 1] = g_im * keep
-        abc[j, 2] = jnp.where(keep > 0.5, g_re, g_im)
+        abc[j, 0] = (now_re + sign * prev_re) * weight
+        abc[j, 1] = (now_im + sign * prev_im) * weight
         return now_re, now_im
 
     zero = jnp.zeros((size, h_ref.shape[2]), F32)
     lax.fori_loop(0, blocks, step, (zero, zero))
 
 
-def row_chunks(size, cols, body):
-    width = min(128, cols)
-    for lane in range(0, cols, width):
-
-        def step(i, carry, lane=lane):
-            body(pl.multiple_of(i * 8, 8), lane, width)
-            return carry
-
-        lax.fori_loop(0, size // 8, step, 0)
-
-
-def products_forward(xs, abc, out, blocks, size):
-    cols = xs.shape[2]
-
-    def body(row, lane, width):
-        re = [xs[i, pl.ds(row, 8), lane : lane + width] for i in range(blocks)]
-        im = [xs[i, pl.ds(size + row, 8), lane : lane + width] for i in range(blocks)]
-        a = [abc[j, 0, pl.ds(row, 8), lane : lane + width] for j in range(blocks)]
-        b = [abc[j, 1, pl.ds(row, 8), lane : lane + width] for j in range(blocks)]
-        c = [abc[j, 2, pl.ds(row, 8), lane : lane + width] for j in range(blocks)]
-        for m in range(blocks):
-            sum_re = re[0] * a[m] - im[0] * b[m]
-            sum_im = re[0] * b[m] + im[0] * c[m]
-            for i in range(1, m + 1):
-                sum_re = sum_re + (re[i] * a[m - i] - im[i] * b[m - i])
-                sum_im = sum_im + (re[i] * b[m - i] + im[i] * c[m - i])
-            out[m, pl.ds(row, 8), lane : lane + width] = sum_re
-            out[m, pl.ds(size + row, 8), lane : lane + width] = sum_im
-
-    row_chunks(size, cols, body)
-
-
-def products_backward(xs, ds, abc, out, lanes, blocks, size):
-    cols = xs.shape[2]
-
-    def body(row, lane, width):
-        here = pl.ds(row, 8)
-        there = pl.ds(size + row, 8)
+def row_chunks(size, body):
+    def step(i, carry):
+        body(pl.multiple_of(i * 8, 8))
+        return carry
+
+    lax.fori_loop(0, size // 8, step, 0)
+
+
+def load_filter(abc, lanes, here, blocks):
+    keep = lanes[here, 2:3]
+    a = [abc[j, 0, here] for j in range(blocks)]
+    raw = [abc[j, 1, here] for j in range(blocks)]
+    b = [one * keep for one in raw]
+    c = [jnp.where(keep > 0.5, one, two) for one, two in zip(a, raw)]
+    return a, b, c
+
+
+def products_forward(xs, abc, lanes, out, blocks, size):
+    width = abc.shape[3]
+    for lane in range(0, xs.shape[2], width):
         piece = slice(lane, lane + width)
-        x_re = [xs[i, here, piece] for i in range(blocks)]
-        x_im = [xs[i, there, piece] for i in range(blocks)]
-        d_re = [ds[i, here, piece] for i in range(blocks)]
-        d_im = [ds[i, there, piece] for i in range(blocks)]
-        a = [abc[j, 0, here, piece] for j in range(blocks)]
-        b = [abc[j, 1, here, piece] for j in range(blocks)]
-        c = [abc[j, 2, here, piece] for j in range(blocks)]
-        for i in range(blocks):
-            sum_re = d_re[i] * a[0] + d_im[i] * b[0]
-            sum_im = d_im[i] * c[0] - d_re[i] * b[0]
-            for m in range(i + 1, blocks):
-                sum_re = sum_re + (d_re[m] * a[m - i] + d_im[m] * b[m - i])
-                sum_im = sum_im + (d_im[m] * c[m - i] - d_re[m] * b[m - i])
-            out[i, here, piece] = sum_re
-            out[i, there, piece] = sum_im
-        weight = lanes[here, 0:1]
-        sign = lanes[here, 1:2]
-        keep = lanes[here, 2:3] > 0.5
-        later_re = None
-        later_im = None
-        for j in range(blocks - 1, -1, -1):
-            rr = d_re[j] * x_re[0]
-            ii = d_im[j] * x_im[0]
-            cross = d_im[j] * x_re[0] - d_re[j] * x_im[0]
-            for i in range(1, blocks - j):
-                rr = rr + d_re[i + j] * x_re[i]
-                ii = ii + d_im[i + j] * x_im[i]
-                cross = cross + (d_im[i + j] * x_re[i] - d_re[i + j] * x_im[i])
-            g_re = jnp.where(keep, rr + ii, rr) * weight
-            g_im = jnp.where(keep, cross, ii) * weight
-            abc[j, 0, here, piece] = g_re if later_re is None else g_re + sign * later_re
-            abc[j, 1, here, piece] = g_im if later_im is None else g_im + sign * later_im
-            later_re, later_im = g_re, g_im
-
-    row_chunks(size, cols, body)
+
+        def body(row, piece=piece):
+            here, there = pl.ds(row, 8), pl.ds(size + row, 8)
+            re = [xs[i, here, piece] for i in range(blocks)]
+            im = [xs[i, there, piece] for i in range(blocks)]
+            a, b, c = load_filter(abc, lanes, here, blocks)
+            for m in range(blocks):
+                sum_re = re[0] * a[m] - im[0] * b[m]
+                sum_im = re[0] * b[m] + im[0] * c[m]
+                for i in range(1, m + 1):
+                    sum_re = sum_re + (re[i] * a[m - i] - im[i] * b[m - i])
+                    sum_im = sum_im + (re[i] * b[m - i] + im[i] * c[m - i])
+                out[m, here, piece] = sum_re
+                out[m, there, piece] = sum_im
+
+        row_chunks(size, body)
+
+
+def products_backward(xs, ds, abc, gh, lanes, blocks, size):
+    width = abc.shape[3]
+    count = xs.shape[2] // width
+    for n in range(count):
+        piece = slice(n * width, (n + 1) * width)
+
+        def body(row, n=n, piece=piece):
+            here, there = pl.ds(row, 8), pl.ds(size + row, 8)
+            d_re = [ds[i, here, piece] for i in range(blocks)]
+            d_im = [ds[i, there, piece] for i in range(blocks)]
+            a, b, c = load_filter(abc, lanes, here, blocks)
+            for i in range(blocks):
+                sum_re = d_re[i] * a[0] + d_im[i] * b[0]
+                sum_im = d_im[i] * c[0] - d_re[i] * b[0]
+                for m in range(i + 1, blocks):
+                    sum_re = sum_re + (d_re[m] * a[m - i] + d_im[m] * b[m - i])
+                    sum_im = sum_im + (d_im[m] * c[m - i] - d_re[m] * b[m - i])
+                ds[i, here, piece] = sum_re
+                ds[i, there, piece] = sum_im
+            x_re = [xs[i, here, piece] for i in range(blocks)]
+            x_im = [xs[i, there, piece] for i in range(blocks)]
+            weight = lanes[here, 0:1]
+            sign = lanes[here, 1:2]
+            keep = lanes[here, 2:3] > 0.5
+            later_re = None
+            later_im = None
+            for j in range(blocks - 1, -1, -1):
+                rr = d_re[j] * x_re[0]
+                ii = d_im[j] * x_im[0]
+                cross = d_im[j] * x_re[0] - d_re[j] * x_im[0]
+                for i in range(1, blocks - j):
+                    rr = rr + d_re[i + j] * x_re[i]
+                    ii = ii + d_im[i + j] * x_im[i]
+                    cross = cross + (d_im[i + j] * x_re[i] - d_re[i + j] * x_im[i])
+                g_re = jnp.where(keep, rr + ii, rr) * weight
+                g_im = jnp.where(keep, cross, ii) * weight
+                if n:
+                    g_re = g_re + gh[j, 0, here]
+                    g_im = g_im + gh[j, 1, here]
+                if n == count - 1 and later_re is not None:
+                    gh[j, 0, here] = g_re + sign * later_re
+                    gh[j, 1, here] = g_im + sign * later_im
+                else:
+                    gh[j, 0, here] = g_re
+                    gh[j, 1, here] = g_im
+                later_re, later_im = g_re, g_im
+
+        row_chunks(size, body)
 
 
 def inverse_of(th, tl, values):
@@ -196,10 +205,10 @@
     lax.fori_loop(0, blocks, step, 0)
 
 
-def filter_gradient(th, tl, abc, out, blocks, size):
+def filter_gradient(th, tl, gh, out, blocks, size):
     def step(j, carry):
-        re_high, re_low = split_high(abc[j, 0])
-        im_high, im_low = split_high(abc[j, 1])
+        re_high, re_low = split_high(gh[j, 0])
+        im_high, im_low = split_high(gh[j, 1])
         left, right = th[:, :size], th[:, size:]
         total = mm(left, re_high) + mm(right, im_high) + mm(left, re_low) + mm(right, im_low)
         total = total + mm(tl[:, :size], re_high) + mm(tl[:, size:], im_high)
@@ -213,18 +222,18 @@
     blocks, size, buckets, chans = dims
     filter_spectra(fh, fl, lanes, h_ref, abc, blocks, size)
     spectra(fh, fl, x_ref, xs, blocks)
-    products_forward(xs, abc, xs, blocks, size)
+    products_forward(xs, abc, lanes, xs, blocks, size)
     inverse_blocks(th, tl, xs, out, blocks)
 
 
-def conv_backward_kernel(dims, d_ref, x_ref, h_ref, fh, fl, th, tl, lanes, out, dh_ref, xs, ds, abc):
+def conv_backward_kernel(dims, d_ref, x_ref, h_ref, fh, fl, th, tl, lanes, out, dh_ref, xs, ds, abc, gh):
     blocks, size, buckets, chans = dims
     filter_spectra(fh, fl, lanes, h_ref, abc, blocks, size)
     spectra(fh, fl, x_ref, xs, blocks)
     spectra(fh, fl, d_ref, ds, blocks)
-    products_backward(xs, ds, abc, ds, lanes, blocks, size)
+    products_backward(xs, ds, abc, gh, lanes, blocks, size)
     inverse_blocks(th, tl, ds, out, blocks)
-    filter_gradient(th, tl, abc, dh_ref, blocks, size)
+    filter_gradient(th, tl, gh, dh_ref, blocks, size)
 
 
 VM = pl.BlockSpec(memory_space=pltpu.VMEM)
@@ -240,7 +249,7 @@
         out_shape=[jax.ShapeDtypeStruct((blocks, size, cols), kind) for kind in kinds],
         in_specs=[VM] * len(operands),
         out_specs=[VM] * len(kinds),
-        scratch_shapes=scratch + [pltpu.VMEM((blocks, 3, size, cols), F32)],
+        scratch_shapes=scratch + [pltpu.VMEM((blocks, 2, size, cols), F32)] * spectra_count,
         compiler_params=pltpu.CompilerParams(vmem_limit_bytes=VMEM_LIMIT),
     )(*operands)
 
@@ -319,8 +328,8 @@
         p = self.p
         for i, shard in enumerate(self.shards):
             mine = self.fulls[i].at[p.z, p.x, p.y, p.core]
-            for d in range(3):
-                self.go(i, ("z", d), d, shard, mine, p.along_z[d])
+            self.go(i, ("z", 1), 1, shard, mine, p.along_z[1])
+            self.go(i, ("z", 0), 0, shard, mine, p.along_z[0])
             self.go(i, ("x", 0), 3, shard, mine, p.along_x)
             self.go(i, ("y", 0), 7, shard, mine, p.along_y)
             self.go(i, ("c", 0), 19, shard, mine, p.sibling)
@@ -333,6 +342,8 @@
         for i in range(len(self.shards)):
             self.copies[(i, ("z", d))].wait_recv()
             here = self.fulls[i].at[p.others[d], p.x, p.y, p.core]
+            if d == 1:
+                self.go(i, ("z", 2), 2, here, here, p.along_z[0])
             self.go(i, ("x", d + 1), 4 + d, here, here, p.along_x)
             self.go(i, ("y", d + 1), 8 + d, here, here, p.along_y)
             self.go(i, ("c", d + 1), 20 + d, here, here, p.sibling)
@@ -372,13 +383,17 @@
                 if name[0] == "c":
                     copy.wait_recv()
 
-    def rest(self):
-        for d in range(3):
-            self.pass_column(d)
-            self.pass_sides(d)
-        self.pass_sides(3)
-        for n in range(4):
-            self.pass_last(n)
+    def steps(self):
+        return (
+            [functools.partial(self.pass_column, 0), functools.partial(self.pass_column, 1)]
+            + [functools.partial(self.pass_sides, 0), functools.partial(self.pass_column, 2)]
+            + [functools.partial(self.pass_sides, n) for n in (1, 2, 3)]
+            + [functools.partial(self.pass_last, n) for n in range(4)]
+        )
+
+    def rest(self, first=0):
+        for step in self.steps()[first:]:
+            step()
         self.finish()
 
     @classmethod
@@ -458,15 +473,21 @@
 
 def send_pieces(p, pieces, blocks_ref, send, recv, local, make):
     copies = []
+
+    def piece(block, b):
+        if len(pieces.shape) == 4:
+            return pieces.at[block, b]
+        return pieces.at[block, :, pl.ds(b * 128, 128)]
+
     for d in range(8):
         block = lax.rem(p.ch + d + 1, 8)
         make(block)
         for b in range(2):
             dst = blocks_ref.at[p.ch, :, pl.ds(b * 128, 128)]
             if d < 7:
-                copies.append(push(pieces.at[block, b], dst, send.at[d, b], recv.at[d, b], {"ch": block}))
+                copies.append(push(piece(block, b), dst, send.at[d, b], recv.at[d, b], {"ch": block}))
             else:
-                copy = pltpu.make_async_copy(pieces.at[block, b], dst, local.at[b])
+                copy = pltpu.make_async_copy(piece(block, b), dst, local.at[b])
                 copy.start()
                 copies.append(copy)
     return copies
@@ -483,37 +504,17 @@
     return copies + [copy]
 
 
-def forward_kernel(
-    size,
-    u,
-    consts,
-    mask,
-    h_ref,
-    fh,
-    fl,
-    th,
-    tl,
-    lanes,
-    mixer,
-    kept,
-    convolved,
-    xs,
-    abc,
-    ys,
-    pieces,
-    gates,
-    mixes,
-    bufs,
-    send,
-    recv,
-    local,
-    send_back,
-    recv_back,
-    local_back,
-):
+def forward_kernel(size, *refs):
+    u, consts, mask, h_ref, fh, fl, th, tl, lanes = refs[:9]
+    shards = refs[9:12]
+    mixer, kept, convolved = refs[12:15]
+    fulls = refs[15:18]
+    xs, abc, ys, pieces, gates, mixes, bufs = refs[18:25]
+    send, recv, local, send_back, recv_back, local_back = refs[25:31]
     p = Place()
     width = 1024
-    greet([{"ch": one} for one in p.ch_ahead])
+    greet([{"ch": one} for one in p.ch_ahead] + [p.sibling, p.along_y])
+    gather = Gather(p, shards, fulls, *refs[31:])
 
     def make(block):
         lane = pl.multiple_of(block * 128, 128)
@@ -530,67 +531,52 @@
             step(b, 0)
 
     arriving = send_pieces(p, pieces, kept, send, recv, local, make)
+    gather.start()
+    steps = gather.steps()
     filter_spectra(fh, fl, lanes, h_ref, abc, 8, size)
     wait_all(arriving)
     spectra(fh, fl, kept, xs, 8)
-    products_forward(xs, abc, xs, 8, size)
+    steps[0]()
+    products_forward(xs, abc, lanes, xs, 8, size)
     inverse_blocks(th, tl, xs, ys, 8)
-    wait_all(send_blocks(p, ys, convolved, send_back, recv_back, local_back))
+    leaving = send_blocks(p, ys, convolved, send_back, recv_back, local_back)
+    for step in steps[1:4]:
+        step()
+    wait_all(leaving)
     for c in range(8):
         at = slice(c * 128, (c + 1) * 128)
         for b in range(2):
             rows = slice(b * size, (b + 1) * size)
             long_part = convolved[c, :, b * 128 : (b + 1) * 128].astype(F32) + consts[9:10, at] * mixes[c, b]
             mixer[rows, at] = (gates[c, b] * long_part * mask[rows]).astype(BF)
-
-
-def backward_kernel(
-    size,
-    u,
-    consts,
-    mask,
-    grad_mixer,
-    convolved,
-    kept,
-    h_ref,
-    fh,
-    fl,
-    th,
-    tl,
-    lanes,
-    du,
-    dh_ref,
-    sums,
-    xs,
-    ds,
-    abc,
-    ys,
-    pieces,
-    arrived,
-    returned,
-    keys,
-    values,
-    dlongs,
-    dcs,
-    edge_in,
-    bufs,
-    send,
-    recv,
-    local,
-    send_back,
-    recv_back,
-    local_back,
-    edge_sems,
-):
+    gather.rest(4)
+
+
+def backward_kernel(size, count, *refs):
+    u, consts, mask, grad_mixer, convolved, kept, h_ref, fh, fl, th, tl, lanes = refs[:12]
+    grads = refs[12 : 12 + count]
+    du, dh_ref, sums = refs[12 + count : 15 + count]
+    outs = refs[15 + count : 15 + 2 * count]
+    rest = refs[15 + 2 * count :]
+    xs, ds, abc, gh, pieces, arrived, returned, keys, values, dlongs, dcs, edge_out, edge_in, bufs = rest[:14]
+    send, recv, local, send_back, recv_back, local_back, edge_sems = rest[14:21]
     p = Place()
     width = 1024
-    greet([{"ch": one} for one in p.ch_ahead])
+    greet([{"ch": one} for one in p.ch_ahead] + [p.sibling, p.along_y])
+    scatter = Scatter(p, [(one, 0, one.shape[5]) for one in grads], outs, rest[21:])
+    scatter.start()
     sums[...] = jnp.zeros_like(sums)
+
+    def grad_parts(block, b, rows, skip):
+        at = pl.ds(pl.multiple_of(block * 128, 128), 128)
+        take = max(rows, 16)
+        masked = grad_mixer[pl.ds(b * size, take), at].astype(F32)[:rows] * mask[pl.ds(b * size, rows)]
+        conv = convolved[block, :take, b * 128 : (b + 1) * 128].astype(F32)[:rows]
+        return masked, conv + skip * (keys[block, b, :rows] * values[block, b, :rows])
 
     def make(block):
         lane = pl.multiple_of(block * 128, 128)
         at = pl.ds(lane, 128)
-        skip = consts[9:10, at]
         total = jnp.zeros((1, 128), F32)
         for b in range(2):
             rows = pl.ds(b * size, size)
@@ -599,74 +585,79 @@
             value = short_conv(u, bufs.at[2], consts, b, 2, lane, size, width)
             keys[block, b] = key
             values[block, b] = value
-            mix = key * value
-            masked = grad_mixer[rows, at].astype(F32) * mask[rows]
-            dlong = masked * gate
+            dlong = grad_mixer[rows, at].astype(F32) * mask[rows] * gate
             dlongs[block, b] = dlong
-            pieces[block, b] = dlong.astype(BF)
-            total = total + jnp.sum(dlong * mix, axis=0, keepdims=True)
-            long_part = convolved[block, :, b * 128 : (b + 1) * 128].astype(F32) + skip * mix
-            dcs[0, b, pl.ds(0, size), at] = masked * long_part
+            pieces[block, :, b * 128 : (b + 1) * 128] = dlong.astype(BF)
+            total = total + jnp.sum(dlong * (key * value), axis=0, keepdims=True)
         sums[9:10, at] = total
 
     arriving = send_pieces(p, pieces, arrived, send, recv, local, make)
     filter_spectra(fh, fl, lanes, h_ref, abc, 8, size)
     spectra(fh, fl, kept, xs, 8)
+    for i in range(count):
+        scatter.core(i)
     wait_all(arriving)
     spectra(fh, fl, arrived, ds, 8)
-    products_backward(xs, ds, abc, ds, lanes, 8, size)
-    inverse_blocks(th, tl, ds, ys, 8)
-    leaving = send_blocks(p, ys, returned, send_back, recv_back, local_back)
-    filter_gradient(th, tl, abc, dh_ref, 8, size)
+    products_backward(xs, ds, abc, gh, lanes, 8, size)
+    inverse_blocks(th, tl, ds, pieces, 8)
+    leaving = send_blocks(p, pieces, returned, send_back, recv_back, local_back)
+    filter_gradient(th, tl, gh, dh_ref, 8, size)
+    for i in range(count):
+        scatter.first(i)
     wait_all(leaving)
 
-    def products(c, carry):
+    def edges(c, carry):
         at = pl.ds(pl.multiple_of(c * 128, 128), 128)
         skip = consts[9:10, at]
         for b in range(2):
-            dmixed = returned[c, :, b * 128 : (b + 1) * 128].astype(F32) + skip * dlongs[c, b]
-            dcs[1, b, pl.ds(0, size), at] = dmixed * values[c, b]
-            dcs[2, b, pl.ds(0, size), at] = dmixed * keys[c, b]
+            masked, long_part = grad_parts(c, b, 8, skip)
+            back = returned[c, :16, b * 128 : (b + 1) * 128].astype(F32)[:8]
+            dmixed = back + skip * dlongs[c, b, :8]
+            edge_out[0, b, :, at] = masked * long_part
+            edge_out[1, b, :, at] = dmixed * values[c, b, :8]
+            edge_out[2, b, :, at] = dmixed * keys[c, b, :8]
         return carry
 
-    lax.fori_loop(0, 8, products, 0)
-    edge = push(
-        dcs.at[:, :, pl.ds(0, 8)], edge_in, edge_sems.at[0], edge_sems.at[1], {"ch": lax.rem(p.ch + 7, 8)}
-    )
-
-    def taps(c, carry):
+    lax.fori_loop(0, 8, edges, 0)
+    edge = push(edge_out, edge_in, edge_sems.at[0], edge_sems.at[1], {"ch": lax.rem(p.ch + 7, 8)})
+    for i in range(count):
+        scatter.second(i)
+    edge.wait()
+    inside = jnp.where(p.ch < 7, 1.0, 0.0)
+
+    def streams(c, carry):
         lane = pl.multiple_of(c * 128, 128)
         at = pl.ds(lane, 128)
+        skip = consts[9:10, at]
+        for b in range(2):
+            masked, long_part = grad_parts(c, b, size, skip)
+            dmixed = returned[c, :, b * 128 : (b + 1) * 128].astype(F32) + skip * dlongs[c, b]
+            dcs[0, b, pl.ds(0, size)] = masked * long_part
+            dcs[1, b, pl.ds(0, size)] = dmixed * values[c, b]
+            dcs[2, b, pl.ds(0, size)] = dmixed * keys[c, b]
         for stream in range(3):
+            out = pl.ds(pl.multiple_of(stream * width + lane, 128), 128)
             totals = [jnp.zeros((1, 128), F32)] * 3
             for b in range(2):
+                dcs[stream, b, pl.ds(size, 8)] = edge_in[stream, b, :, at] * inside
                 parts = lagged(u, bufs.at[stream], b, stream, lane, size, width)
-                grad = dcs[stream, b, pl.ds(0, size), at]
+                grad = dcs[stream, b, pl.ds(0, size)]
                 for lag in range(3):
                     totals[lag] = totals[lag] + jnp.sum(grad * parts[lag], axis=0, keepdims=True)
+                total = consts[stream : stream + 1, at] * grad
+                total = total + consts[3 + stream : 4 + stream, at] * dcs[stream, b, pl.ds(1, size)]
+                total = total + consts[6 + stream : 7 + stream, at] * dcs[stream, b, pl.ds(2, size)]
+                du[pl.ds(b * size, size), out] = total.astype(BF)
             for lag in range(3):
                 row = 3 * lag + stream
                 sums[row : row + 1, at] = totals[lag]
         return carry
 
-    lax.fori_loop(0, 8, taps, 0)
-    edge.wait()
-    inside = jnp.where(p.ch < 7, 1.0, 0.0)
-
-    def streams(c, carry):
-        lane = pl.multiple_of(c * 128, 128)
-        at = pl.ds(lane, 128)
-        for stream in range(3):
-            out = pl.ds(pl.multiple_of(stream * width + lane, 128), 128)
-            for b in range(2):
-                dcs[stream, b, pl.ds(size, 8), at] = edge_in[stream, b, :, at] * inside
-                total = consts[stream : stream + 1, at] * dcs[stream, b, pl.ds(0, size), at]
-                total = total + consts[3 + stream : 4 + stream, at] * dcs[stream, b, pl.ds(1, size), at]
-                total = total + consts[6 + stream : 7 + stream, at] * dcs[stream, b, pl.ds(2, size), at]
-                du[pl.ds(b * size, size), out] = total.astype(BF)
-        return carry
-
     lax.fori_loop(0, 8, streams, 0)
+    for i in range(count):
+        scatter.third(i)
+    for i in range(count):
+        scatter.last(i)
 
 
 def exchange_sems():
@@ -674,267 +665,274 @@
     return pieces + [pltpu.SemaphoreType.DMA((7,))] * 2 + [pltpu.SemaphoreType.DMA]
 
 
-def forward_call(u, consts, mask, filt, tables, size):
+def forward_call(u, consts, mask, filt, tables, shards, size):
     rows = 2 * size
     block = (8, size, 256)
     piece = (8, 2, size, 128)
     operands = (u, consts, mask, filt) + tables
-    return pl.pallas_call(
+    count = len(shards)
+    whole = [jax.ShapeDtypeStruct((4, 2, 2, 2) + one.shape, BF) for one in shards]
+    out = pl.pallas_call(
         functools.partial(forward_kernel, size),
-        out_shape=[jax.ShapeDtypeStruct((rows, 1024), BF)] + [jax.ShapeDtypeStruct(block, BF)] * 2,
-        in_specs=[VM] * len(operands),
-        out_specs=[VM] * 3,
+        out_shape=[jax.ShapeDtypeStruct((rows, 1024), BF)] + [jax.ShapeDtypeStruct(block, BF)] * 2 + whole,
+        in_specs=[VM] * len(operands) + [ANYWHERE] * count,
+        out_specs=[VM] * 3 + [ANYWHERE] * count,
         scratch_shapes=[
             pltpu.VMEM((8, 2 * size, 256), F32),
-            pltpu.VMEM((8, 3, size, 256), F32),
+            pltpu.VMEM((8, 2, size, 128), F32),
             pltpu.VMEM(block, BF),
             pltpu.VMEM(piece, BF),
             pltpu.VMEM(piece, F32),
             pltpu.VMEM(piece, F32),
             pltpu.VMEM((3, size + 16, 128), F32),
         ]
-        + exchange_sems(),
+        + exchange_sems()
+        + Gather.scratch(count),
         compiler_params=pltpu.CompilerParams(collective_id=1, has_side_effects=True, vmem_limit_bytes=VMEM_LIMIT),
-    )(*operands)
-
-
-def backward_call(u, consts, mask, grad_mixer, convolved, kept, filt, tables, size):
+    )(*operands, *shards)
+    return out[:3], [one.reshape(-1, one.shape[-1]) for one in out[3:]]
+
+
+def backward_call(u, consts, mask, grad_mixer, convolved, kept, filt, tables, grads, size):
     rows = 2 * size
     block = (8, size, 256)
     piece = (8, 2, size, 128)
     operands = (u, consts, mask, grad_mixer, convolved, kept, filt) + tables
-    return pl.pallas_call(
-        functools.partial(backward_kernel, size),
+    count = len(grads)
+    shapes = [(one.shape[0] // 32, one.shape[1]) for one in grads]
+    views = [one.reshape((4, 2, 2, 2) + shape) for one, shape in zip(grads, shapes)]
+    out = pl.pallas_call(
+        functools.partial(backward_kernel, size, count),
         out_shape=[
             jax.ShapeDtypeStruct((rows, 3072), BF),
-            jax.ShapeDtypeStruct(block, F32),
+            jax.ShapeDtypeStruct((8, size, 128), F32),
             jax.ShapeDtypeStruct((16, 1024), F32),
-        ],
-        in_specs=[VM] * len(operands),
-        out_specs=[VM] * 3,
+        ]
+        + [jax.ShapeDtypeStruct(shape, F32) for shape in shapes],
+        in_specs=[VM] * len(operands) + [ANYWHERE] * count,
+        out_specs=[VM] * (3 + count),
         scratch_shapes=[
             pltpu.VMEM((8, 2 * size, 256), F32),
             pltpu.VMEM((8, 2 * size, 256), F32),
-            pltpu.VMEM((8, 3, size, 256), F32),
+            pltpu.VMEM((8, 2, size, 128), F32),
+            pltpu.VMEM((8, 2, size, 128), F32),
             pltpu.VMEM(block, BF),
-            pltpu.VMEM(piece, BF),
             pltpu.VMEM(block, BF),
             pltpu.VMEM(block, BF),
             pltpu.VMEM(piece, F32),
             pltpu.VMEM(piece, F32),
             pltpu.VMEM(piece, F32),
-            pltpu.VMEM((3, 2, size + 8, 1024), F32),
+            pltpu.VMEM((3, 2, size + 8, 128), F32),
+            pltpu.VMEM((3, 2, 8, 1024), F32),
             pltpu.VMEM((3, 2, 8, 1024), F32),
             pltpu.VMEM((3, size + 16, 128), F32),
         ]
         + exchange_sems()
-        + [pltpu.SemaphoreType.DMA((2,))],
+        + [pltpu.SemaphoreType.DMA((2,))]
+        + Scatter.scratch(shapes),
         compiler_params=pltpu.CompilerParams(collective_id=2, has_side_effects=True, vmem_limit_bytes=VMEM_LIMIT),
-    )(*operands)
+    )(*operands, *views)
+    return out[:3], out[3:]
 
 
 def add_rows(target, other):
     return (target.astype(F32) + other.astype(F32)).astype(BF)
 
 
-def scatter_kernel(count, *refs):
-    grads = refs[:count]
-    small_vec, small_sec, small_fst = refs[count : count + 3]
-    outs = refs[count + 3 : 2 * count + 3]
-    small_out = refs[2 * count + 3]
-    rest = refs[2 * count + 4 :]
-    own = rest[:count]
-    acc = rest[count : 2 * count]
-    one_a = rest[2 * count : 3 * count]
-    one_b = rest[3 * count : 4 * count]
-    two_a = rest[4 * count : 5 * count]
-    two_b = rest[5 * count : 6 * count]
-    three = rest[6 * count : 7 * count]
-    gathered, joined, send, recv, local, small_send, small_recv = rest[7 * count :]
-
+class Scatter:
+    SLOTS = 11
+
+    def __init__(self, place, grads, outs, refs):
+        count = len(grads)
+        self.p, self.grads, self.outs = place, grads, outs
+        names = ("own", "acc", "one_a", "one_b", "two_a", "two_b", "three", "four")
+        for n, name in enumerate(names):
+            setattr(self, name, refs[n * count : (n + 1) * count])
+        self.send, self.recv, self.local = refs[8 * count : 8 * count + 3]
+        self.copies = {}
+
+    def go(self, i, slot, src, dst, device):
+        copy = push(src, dst, self.send.at[i, slot], self.recv.at[i, slot], device)
+        self.copies[(i, slot)] = copy
+
+    def done(self, i, *slots):
+        for slot in slots:
+            self.copies[(i, slot)].wait()
+
+    def part(self, i, zz, core):
+        ref, first, cols = self.grads[i]
+        if cols == ref.shape[5]:
+            return ref.at[zz, :, :, core]
+        return ref.at[zz, :, :, core, :, pl.ds(first, cols)]
+
+    def load(self, i, zz):
+        copy = pltpu.make_async_copy(self.part(i, zz, self.p.core), self.own[i].at[zz % 2], self.local.at[i, zz])
+        copy.start()
+        self.copies[(i, "own", zz)] = copy
+
+    def start(self):
+        for i in range(len(self.grads)):
+            for zz in range(4):
+                self.go(i, zz, self.part(i, zz, 1 - self.p.core), self.acc[i].at[zz], self.p.sibling)
+            self.load(i, 0)
+            self.load(i, 1)
+
+    def core(self, i):
+        p, acc, own = self.p, self.acc[i], self.own[i]
+        for zz in range(4):
+            self.copies[(i, "own", zz)].wait()
+            self.done(i, zz)
+
+            def step(n, carry, zz=zz):
+                xx, yy = n // 2, lax.rem(n, 2)
+                acc[zz, xx, yy] = add_rows(acc[zz, xx, yy], own[zz % 2, xx, yy])
+                return carry
+
+            lax.fori_loop(0, 4, step, 0)
+            if zz < 2:
+                self.load(i, zz + 2)
+        half = acc.shape[3] // 2
+        self.go(i, 4, acc.at[:, :, 1 - p.y, pl.ds(0, half)], self.one_a[i], p.along_y)
+        self.go(i, 5, acc.at[:, 1 - p.x, :, pl.ds(half, half)], self.one_b[i], p.along_x)
+
+    def first(self, i):
+        p, acc = self.p, self.acc[i]
+        half = acc.shape[3] // 2
+        self.done(i, 4, 5)
+
+        def step(n, carry):
+            zz, w = n // 2, lax.rem(n, 2)
+            acc[zz, w, p.y, :half] = add_rows(acc[zz, w, p.y, :half], self.one_a[i][zz, w])
+            acc[zz, p.x, w, half:] = add_rows(acc[zz, p.x, w, half:], self.one_b[i][zz, w])
+            return carry
+
+        lax.fori_loop(0, 8, step, 0)
+        self.go(i, 6, acc.at[:, 1 - p.x, p.y, pl.ds(0, half)], self.two_a[i], p.along_x)
+        self.go(i, 7, acc.at[:, p.x, 1 - p.y, pl.ds(half, half)], self.two_b[i], p.along_y)
+
+    def second(self, i):
+        p, acc = self.p, self.acc[i]
+        half = acc.shape[3] // 2
+        self.done(i, 6, 7)
+
+        def step(zz, carry):
+            acc[zz, p.x, p.y, :half] = add_rows(acc[zz, p.x, p.y, :half], self.two_a[i][zz])
+            acc[zz, p.x, p.y, half:] = add_rows(acc[zz, p.x, p.y, half:], self.two_b[i][zz])
+            return carry
+
+        lax.fori_loop(0, 4, step, 0)
+        self.go(i, 8, acc.at[p.others[2], p.x, p.y], self.three[i].at[0], p.along_z[0])
+        self.go(i, 9, acc.at[p.others[0], p.x, p.y], self.three[i].at[1], p.along_z[0])
+
+    def third(self, i):
+        p, acc = self.p, self.acc[i]
+        far = p.others[1]
+        self.done(i, 8, 9)
+        acc[far, p.x, p.y] = add_rows(acc[far, p.x, p.y], self.three[i][0])
+        self.go(i, 10, acc.at[far, p.x, p.y], self.four[i], p.along_z[1])
+
+    def last(self, i):
+        p, acc = self.p, self.acc[i]
+        self.done(i, 10)
+        total = acc[p.z, p.x, p.y].astype(F32) + self.three[i][1].astype(F32) + self.four[i][...].astype(F32)
+        cols = self.grads[i][2]
+        first = self.grads[i][1]
+        self.outs[i][:, first : first + cols] = total
+
+    @classmethod
+    def scratch(cls, shapes):
+        count = len(shapes)
+        bufs = [[] for _ in range(8)]
+        for rows, cols in shapes:
+            half = rows // 2
+            for place, shape in enumerate(
+                (
+                    (2, 2, 2, rows, cols),
+                    (4, 2, 2, rows, cols),
+                    (4, 2, half, cols),
+                    (4, 2, half, cols),
+                    (4, half, cols),
+                    (4, half, cols),
+                    (2, rows, cols),
+                    (rows, cols),
+                )
+            ):
+                bufs[place].append(pltpu.VMEM(shape, BF))
+        return [one for group in bufs for one in group] + [
+            pltpu.SemaphoreType.DMA((count, cls.SLOTS)),
+            pltpu.SemaphoreType.DMA((count, cls.SLOTS)),
+            pltpu.SemaphoreType.DMA((count, 4)),
+        ]
+
+
+PARTS = 3
+
+
+def scatter_kernel(grad, small_vec, small_sec, small_fst, out, small_out, gathered, joined, small_send, small_recv, *refs):
     p = Place()
-    ch, seq, z, x, y, core = p.ch, p.seq, p.z, p.x, p.y, p.core
-    sibling, along_y, along_x, along_z, others = p.sibling, p.along_y, p.along_x, p.along_z, p.others
-    ch_ahead, seq_ahead = p.ch_ahead, p.seq_ahead
-    ch_count, seq_count = 8, 4
-    greet([{"ch": one} for one in ch_ahead] + [{"seq": one} for one in seq_ahead])
-
-    def remote(src, dst, slot, array, device):
-        copy = pltpu.make_async_remote_copy(
-            src_ref=src,
-            dst_ref=dst,
-            send_sem=send.at[array, slot],
-            recv_sem=recv.at[array, slot],
-            device_id=device,
-            device_id_type=MESH,
-        )
-        copy.start()
-        return copy
-
-    core_copies, own_copies = [], []
-    for i in range(count):
-        core_copies.append(remote(grads[i].at[:, :, :, 1 - core], acc[i], 0, i, sibling))
-        copy = pltpu.make_async_copy(grads[i].at[:, :, :, core], own[i], local.at[i])
-        copy.start()
-        own_copies.append(copy)
+    greet([{"ch": one} for one in p.ch_ahead] + [{"seq": one} for one in p.seq_ahead])
+    cols = grad.shape[5] // PARTS
+    scatter = Scatter(p, [(grad, n * cols, cols) for n in range(PARTS)], [out] * PARTS, refs)
+    scatter.start()
 
     vec_rows = small_vec.shape[0]
     fst_rows = small_fst.shape[0]
-    sec_rows = small_sec.shape[0]
     small_copies = []
-    for d in range(ch_count - 1):
-        lane = pl.multiple_of(ch_ahead[d] * 128, 128)
+    for d in range(7):
+        lane = pl.multiple_of(p.ch_ahead[d] * 128, 128)
         pairs = (
-            (small_vec.at[:, pl.ds(lane, 128)], gathered.at[ch, pl.ds(0, vec_rows)]),
-            (small_fst, gathered.at[ch, pl.ds(vec_rows, fst_rows)]),
+            (small_vec.at[:, pl.ds(lane, 128)], gathered.at[p.ch, pl.ds(0, vec_rows)]),
+            (small_fst, gathered.at[p.ch, pl.ds(vec_rows, fst_rows)]),
         )
-        for s in range(2):
-            copy = pltpu.make_async_remote_copy(
-                src_ref=pairs[s][0],
-                dst_ref=pairs[s][1],
-                send_sem=small_send.at[2 * d + s],
-                recv_sem=small_recv.at[2 * d + s],
-                device_id={"ch": ch_ahead[d]},
-                device_id_type=MESH,
-            )
-            copy.start()
-            small_copies.append(copy)
-    gathered[ch, :vec_rows] = small_vec[:, pl.ds(pl.multiple_of(ch * 128, 128), 128)]
-    gathered[ch, vec_rows:] = small_fst[...]
-
-    one_copies = [None] * count
-    two_copies = [None] * count
-    three_copies = [None] * count
-
-    def stage_core(i):
-        own_copies[i].wait()
-        core_copies[i].wait()
-
-        def step(n, carry):
-            zz, xy = n // 4, lax.rem(n, 4)
-            xx, yy = xy // 2, lax.rem(xy, 2)
-            acc[i][zz, xx, yy] = add_rows(acc[i][zz, xx, yy], own[i][zz, xx, yy])
-            return carry
-
-        lax.fori_loop(0, 16, step, 0)
-        half = acc[i].shape[3] // 2
-        one_copies[i] = (
-            remote(acc[i].at[:, :, 1 - y, pl.ds(0, half)], one_a[i], 1, i, along_y),
-            remote(acc[i].at[:, 1 - x, :, pl.ds(half, half)], one_b[i], 2, i, along_x),
-        )
-
-    def stage_one(i):
-        wait_all(one_copies[i])
-        half = acc[i].shape[3] // 2
-
-        def step(n, carry):
-            zz, w = n // 2, lax.rem(n, 2)
-            acc[i][zz, w, y, :half] = add_rows(acc[i][zz, w, y, :half], one_a[i][zz, w])
-            acc[i][zz, x, w, half:] = add_rows(acc[i][zz, x, w, half:], one_b[i][zz, w])
-            return carry
-
-        lax.fori_loop(0, 8, step, 0)
-        two_copies[i] = (
-            remote(acc[i].at[:, 1 - x, y, pl.ds(0, half)], two_a[i], 3, i, along_x),
-            remote(acc[i].at[:, x, 1 - y, pl.ds(half, half)], two_b[i], 4, i, along_y),
-        )
-
-    def stage_two(i):
-        wait_all(two_copies[i])
-        half = acc[i].shape[3] // 2
-
-        def step(zz, carry):
-            acc[i][zz, x, y, :half] = add_rows(acc[i][zz, x, y, :half], two_a[i][zz])
-            acc[i][zz, x, y, half:] = add_rows(acc[i][zz, x, y, half:], two_b[i][zz])
-            return carry
-
-        lax.fori_loop(0, 4, step, 0)
-        three_copies[i] = [
-            remote(acc[i].at[others[d], x, y], three[i].at[d], 5 + d, i, along_z[d]) for d in range(3)
-        ]
-
-    def stage_three(i):
-        wait_all(three_copies[i])
-        total = acc[i][z, x, y].astype(F32)
-        for d in range(3):
-            total = total + three[i][d].astype(F32)
-        outs[i][...] = total
-
-    stages = (stage_core, stage_one, stage_two, stage_three)
-    for time in range(count + 3):
-        for s in range(4):
-            if 0 <= time - s < count:
-                stages[s](time - s)
+        for n, (src, dst) in enumerate(pairs):
+            slot = 2 * d + n
+            small_copies.append(push(src, dst, small_send.at[slot], small_recv.at[slot], {"ch": p.ch_ahead[d]}))
+    gathered[p.ch, :vec_rows] = small_vec[:, pl.ds(pl.multiple_of(p.ch * 128, 128), 128)]
+    gathered[p.ch, vec_rows:] = small_fst[...]
+
+    stages = (scatter.core, scatter.first, scatter.second, scatter.third, scatter.last)
+    for time in range(PARTS + len(stages) - 1):
+        for n, stage in enumerate(stages):
+            if 0 <= time - n < PARTS:
+                stage(time - n)
         if time == 0:
             wait_all(small_copies)
             total = gathered[0]
-            for n in range(1, ch_count):
+            for n in range(1, 8):
                 total = total + gathered[n]
-            joined[seq, : vec_rows + fst_rows] = total
-            joined[seq, vec_rows + fst_rows :] = small_sec[...]
-            small_copies = []
-            for d in range(seq_count - 1):
-                copy = pltpu.make_async_remote_copy(
-                    src_ref=joined.at[seq],
-                    dst_ref=joined.at[seq],
-                    send_sem=small_send.at[14 + d],
-                    recv_sem=small_recv.at[14 + d],
-                    device_id={"seq": seq_ahead[d]},
-                    device_id_type=MESH,
-                )
-                copy.start()
-                small_copies.append(copy)
+            joined[p.seq, : vec_rows + fst_rows] = total
+            joined[p.seq, vec_rows + fst_rows :] = small_sec[...]
+            small_copies = [
+                push(joined.at[p.seq], joined.at[p.seq], small_send.at[14 + d], small_recv.at[14 + d], {"seq": p.seq_ahead[d]})
+                for d in range(3)
+            ]
     wait_all(small_copies)
     total = joined[0]
-    for n in range(1, seq_count):
+    for n in range(1, 4):
         total = total + joined[n]
     small_out[...] = total
 
 
-def scatter_sums(grads, vec, sec, fst):
-    count = len(grads)
-    views = []
-    outs = []
-    bufs = [[] for _ in range(7)]
-    for grad in grads:
-        rows, cols = grad.shape[0] // 32, grad.shape[1]
-        half = rows // 2
-        views.append(grad.reshape(4, 2, 2, 2, rows, cols))
-        outs.append(jax.ShapeDtypeStruct((rows, cols), F32))
-        for place, shape in enumerate(
-            (
-                (4, 2, 2, rows, cols),
-                (4, 2, 2, rows, cols),
-                (4, 2, half, cols),
-                (4, 2, half, cols),
-                (4, half, cols),
-                (4, half, cols),
-                (3, rows, cols),
-            )
-        ):
-            bufs[place].append(pltpu.VMEM(shape, BF))
+def scatter_sums(grad, vec, sec, fst):
+    rows, cols = grad.shape[0] // 32, grad.shape[1]
     small = vec.shape[0] + fst.shape[0]
-    scratch = [one for group in bufs for one in group]
-    scratch += [
-        pltpu.VMEM((8, small, 128), F32),
-        pltpu.VMEM((4, small + sec.shape[0], 128), F32),
-        pltpu.SemaphoreType.DMA((count, 8)),
-        pltpu.SemaphoreType.DMA((count, 8)),
-        pltpu.SemaphoreType.DMA((count,)),
-        pltpu.SemaphoreType.DMA((17,)),
-        pltpu.SemaphoreType.DMA((17,)),
-    ]
-    outs.append(jax.ShapeDtypeStruct((small + sec.shape[0], 128), F32))
     return pl.pallas_call(
-        functools.partial(scatter_kernel, count),
-        out_shape=outs,
-        in_specs=[ANYWHERE] * count + [VM] * 3,
-        out_specs=[VM] * (count + 1),
-        scratch_shapes=scratch,
-        compiler_params=pltpu.CompilerParams(
-            collective_id=3, has_side_effects=True, vmem_limit_bytes=VMEM_LIMIT
-        ),
-    )(*views, vec, sec, fst)
+        scatter_kernel,
+        out_shape=[
+            jax.ShapeDtypeStruct((rows, cols), F32),
+            jax.ShapeDtypeStruct((small + sec.shape[0], 128), F32),
+        ],
+        in_specs=[ANYWHERE] + [VM] * 3,
+        out_specs=[VM] * 2,
+        scratch_shapes=[
+            pltpu.VMEM((8, small, 128), F32),
+            pltpu.VMEM((4, small + sec.shape[0], 128), F32),
+            pltpu.SemaphoreType.DMA((17,)),
+            pltpu.SemaphoreType.DMA((17,)),
+        ]
+        + Scatter.scratch([(rows, cols // PARTS)] * PARTS),
+        compiler_params=pltpu.CompilerParams(collective_id=3, has_side_effects=True, vmem_limit_bytes=VMEM_LIMIT),
+    )(grad.reshape(4, 2, 2, 2, rows, cols), vec, sec, fst)
 
 
 def general_body(
@@ -1132,12 +1130,6 @@
     by_bucket = jnp.swapaxes(tokens[0], 0, 1)
     consts, halo, full_in = start_call(pack, by_bucket[:, size - 16 :], in_weight)
 
-    def gather(shard):
-        return lax.all_gather(shard, ("ch", "seq"), axis=0, tiled=True)
-
-    full_out = gather(out_weight)
-    full_up = gather(up_weight)
-    full_down = gather(down_weight)
     full_gain_one = consts[10]
     full_gain_two = consts[11]
 
@@ -1157,10 +1149,12 @@
     hidden = filter_hidden(filter_first, filter_bias, frequency, table)
     decay = decay_table(length, ch_place * chans, chans, width)
     filt = jnp.dot(hidden, filter_second, precision=HIGH) * decay
-    filt_blocks = jnp.tile(filt.reshape(8, size, chans), (1, 1, buckets))
+    filt_blocks = filt.reshape(8, size, chans)
 
     wide_mask = jnp.broadcast_to(mask, (rows, 128))
-    mixer, kept, convolved = forward_call(streams, consts, wide_mask, filt_blocks, tables, size)
+    (mixer, kept, convolved), (full_out, full_up, full_down) = forward_call(
+        streams, consts, wide_mask, filt_blocks, tables, (out_weight, up_weight, down_weight), size
+    )
     after_mix = x_zero + jnp.dot(mixer, full_out, preferred_element_type=F32)
     normed_two = layer_norm(after_mix, full_gain_two).astype(BF)
     inner_act = jnp.dot(normed_two, full_up, preferred_element_type=F32)
@@ -1182,8 +1176,8 @@
     grad_out = jnp.dot(mixer.T, grad_mix, preferred_element_type=F32).astype(BF)
     grad_mixer = jnp.dot(grad_mix, full_out.T, preferred_element_type=F32).astype(BF)
 
-    grad_projected, grad_filt, sums = backward_call(
-        streams, consts, wide_mask, grad_mixer, convolved, kept, filt_blocks, tables, size
+    (grad_projected, grad_filt, sums), (sum_down, sum_up, sum_out) = backward_call(
+        streams, consts, wide_mask, grad_mixer, convolved, kept, filt_blocks, tables, (grad_down, grad_up, grad_out), size
     )
     grad_in = jnp.dot(normed_one.T, grad_projected, preferred_element_type=F32).astype(BF)
     grad_normed_one = jnp.dot(grad_projected, full_in.T, preferred_element_type=F32)
@@ -1192,8 +1186,7 @@
     grad_input = ((grad_after + grad_zero_part) * mask).astype(BF)
     grad_input = jnp.swapaxes(grad_input.reshape(buckets, size, width), 0, 1).reshape(1, size, buckets, width)
 
-    grad_filt = grad_filt.reshape(length, buckets * chans)
-    grad_raw = (grad_filt[:, :chans] + grad_filt[:, chans:]) * decay
+    grad_raw = grad_filt.reshape(length, chans) * decay
     grad_second = jnp.dot(hidden.T, grad_raw, precision=HIGH)
     grad_hidden = jnp.dot(grad_raw, filter_second.T, precision=HIGH)
 
@@ -1205,7 +1198,7 @@
     vec = jnp.concatenate([sums[:10], grad_gain_one[None], grad_gain_two[None], jnp.zeros((4, width), F32)])
     fst = jnp.concatenate([grad_first, grad_bias[None], grad_freq[None]])
     fst = jnp.pad(fst, ((0, -fst.shape[0] % 8), (0, 128 - filt_width)))
-    sum_down, sum_up, sum_in, sum_out, small = scatter_sums((grad_down, grad_up, grad_in, grad_out), vec, grad_second, fst)
+    sum_in, small = scatter_sums(grad_in, vec, grad_second, fst)
     gain_sums = lax.dynamic_slice_in_dim(small[10:12], seq_place * part, part, 1)
     return (
         result,

time: 628 us -> 527 us (0.84)
  waiting for transfers between devices: 86.8 us -> 0 us
  Pallas kernels: 363 us -> 377 us
  matrix products: 109 us -> 95.7 us
  between operations: 14.4 us -> 1.54 us
    all_gather x3 -> x0, waiting for transfers between devices: 84.7 us -> none  [gather(): return lax.all_gather(shard, ('ch', 'seq'), axis=0, tiled=True)]
    pallas_call x1, Pallas kernels: 75.6 us -> 124 us  [forward_call(): pl.pallas_call(functools.partial(forward_kernel, size), out_shape=[jax.Sh...]
    pallas_call x2, Pallas kernels: 232 us -> 206 us  [the longest x1 155 us: backward_call(): pl.pallas_call(functools.partial(backward_kernel, size, count), out_shape...]
    pallas_call x1, Pallas kernels: 55.5 us -> 46.9 us  [start_call(): pl.pallas_call(start_kernel, out_shape=[jax.ShapeDtypeStruct((16, 1024),...]
    another operation x2 -> x0, local copies, waits for them, and re-layouts: 6.34 us -> none  [slice_body(): filt_blocks = jnp.tile(filt.reshape(8, size, chans), (1, 1, buckets))]
  transfers between devices with their start and end apart: 3 -> 0, of which waited for: 2 -> 0; matrix products, arithmetic and copies ran while one was open for 7% -> 0% of each run, Pallas kernels for 21% -> 0%
where the time goes in v1:
time: 527 us; the launch traced here: 518 us
  Pallas kernels  377 us (72%)
  matrix products  95.7 us (18%)
  local copies, waits for them, and re-layouts  29.3 us (6%)
  other arithmetic  14.9 us (3%)
    pallas_call x1, Pallas kernels, backward_call(): pl.pallas_call(functools.partial(backward_kernel, size, count), out_shape...  155 us
    pallas_call x1, Pallas kernels, forward_call(): pl.pallas_call(functools.partial(forward_kernel, size), out_shape=[jax.Sh...  124 us
    pallas_call x1, Pallas kernels, scatter_sums(): pl.pallas_call(scatter_kernel, out_shape=[jax.ShapeDtypeStruct((rows, col...  51.2 us
    pallas_call x1, Pallas kernels, start_call(): pl.pallas_call(start_kernel, out_shape=[jax.ShapeDtypeStruct((16, 1024),...  46.9 us
    dot_general x1, matrix products, slice_body(): inner_act = jnp.dot(normed_two, full_up, preferred_element_type=F32)  14.5 us
    dot_general x1, matrix products, slice_body(): jnp.dot(active, full_down, preferred_element_type=F32)  13.5 us
    unnamed x70, local copies, waits for them, and re-layouts  10.7 us

profile of v1, /device:TPU:0, one launch (start us, length us, event | category | flops | bytes accessed | tf_op | source)
XLA Modules:
  0.0 518.3 jit_solution(5075460870865325681)
XLA Ops:
  0.8 0.8 and_convert_fusion
  1.8 0.7 maximum_convert_fusion
  2.5 0.7 fusion.35
  3.3 1.6 fusion.13
  4.9 1.8 multiply_reduce_fusion.5
  6.8 0.7 maximum_maximum_fusion.1.pack
  8.0 0.8 broadcast_in_dim.32.refs_2_
  9.5 1.2 copy.41
  10.7 4.6 convolution_multiply_fusion
  15.6 1.0 copy-done.6
  17.2 46.9 %shard_map.299 = (f32[16,1024]{1,0:T(8,128)}, bf16[2,16,1024]{2,1,0:T(8,128)(2,1)}, bf16[4,2,2,2,32,3072]{5,4,3,2,1,0:T(8,128)(2,1)}) custom-call(f32[16,128]{1,0:T(8,128)} %maximum_maximum_fusion.1.pack, bf16[2,16,1024]{2,1,0:T(8,128)(2,1)} %slice.52.tail, bf16[32,3072]{1,0:T(8,128)(2,1)} %shard.1), custom_call_target="tpu_custom_call" | custom-call | tf_op jit(solution)/shard_map/pallas_call | solution.py:437
  64.1 1.0 multiply_reduce_fusion.9
  65.1 1.0 multiply_reduce_fusion.8
  66.3 0.8 fusion.39
  67.1 0.9 fusion.28
  68.6 1.0 copy-done.7
  69.6 8.0 %convolution_convert_fusion.3.refs_0_ = bf16[544,3072]{1,0:T(8,128)(2,1)} fusion(bf16[1024,3072]{1,0:T(8,128)(2,1)} %bitcast.187, bf16[32,1024]{1,0:T(8,128)(2,1)S(1)} %fusion.28, bf16[512,1024]{1,0:T(8,128)(2,1)S(1)} %multiply_convert_fusion.3), kind=kOutput, calls=%fused_computation.18 | convolution fusion | flops 3426451456 | bytes 10747904 | tf_op jit(solution)/shard_map/dot_general | solution.py:1144
  77.5 124.0 %shard_map.300 = (bf16[512,1024]{1,0:T(8,128)(2,1)}, bf16[8,256,256]{2,1,0:T(8,128)(2,1)}, bf16[8,256,256]{2,1,0:T(8,128)(2,1)}, bf16[4,2,2,2,32,1024]{5,4,3,2,1...) custom-call(bf16[544,3072]{1,0:T(8,128)(2,1)} %convolution_convert_fusion.3.refs_0_, ...), custom_call_target="tpu_custom_call" | custom-call | tf_op jit(solution)/shard_map/pallas_call | solution.py:675
  201.6 3.7 fusion.40
  206.7 6.7 %fusion.41 = f32[4096,512]{0,1:T(8,128)} fusion(bf16[4096,1024]{1,0:T(8,128)(2,1)S(1)} %bitcast.186, bf16[512,1024]{1,0:T(8,128)(2,1)S(1)} %bitcast.139), kind=kOutput, calls=%fused_computation.122 | convolution fusion | flops 4294967296 | bytes 17825792 | tf_op jit(solution)/shard_map/dot_general | solution.py:1166
  213.5 14.5 %fusion.6 = (bf16[512,4096]{1,0:T(8,128)(2,1)S(1)}, f32[512,4096]{1,0:T(8,128)}) fusion(f32[4096,512]{0,1:T(8,128)} %fusion.41, bf16[1024,4096]{1,0:T(8,128)(2,1)S(1)} %bitcast.183, f32[512,1024]{1,0:T(8,128)S(1)} %get-tuple-element.71, f32[1024]{0:T(1024)S(1)} %bitcast.168, f32[512]{0:T(512)S(1)} %fusion.29, f32[512]{0:T(512)S(1)} %broadcast_multiply_fusion), kind=kOutput, calls=%fused_computation.8 | convolution fusion | flops 4339007488 | bytes 31465472 | tf_op jit(solution)/shard_map/dot_general | solution.py:1160
  228.0 13.5 %add_convert_fusion = bf16[512,1024]{1,0:T(8,128)(2,1)} fusion(f32[512,1024]{1,0:T(8,128)S(1)} %get-tuple-element.71, bf16[4096,1024]{1,0:T(8,128)(2,1)} %bitcast.185, f32[512,4096]{1,0:T(8,128)} %get-tuple-element.73), kind=kOutput, calls=%fused_computation.31 | convolution fusion | flops 4314890240 | bytes 19922944 | tf_op jit(solution)/shard_map/dot_general | solution.py:1162
  241.5 4.9 multiply_reduce_fusion
  246.4 0.7 fusion.38
  247.5 1.0 copy-done.2
  248.5 1.1 copy-done.23
  249.5 2.3 convolution_convert_fusion.5.refs_3_
  251.8 2.6 convolution_convert_fusion.4
  254.4 7.3 %convolution_convert_fusion = bf16[1024,4096]{1,0:T(8,128)(2,1)} fusion(bf16[512,4096]{1,0:T(8,128)(2,1)S(1)} %copy-done.26, f32[512,1024]{1,0:T(8,128)S(1)} %get-tuple-element.71, f32[1024]{0:T(1024)S(1)} %bitcast.171, f32[512]{0:T(512)S(1)} %fusion.29, f32[512]{0:T(512)S(1)} %broadcast_multiply_fusion), kind=kOutput, calls=%fused_computation.15 | convolution fusion | flops 4301258752 | bytes 14688256 | tf_op jit(solution)/shard_map/dot_general | solution.py:1170
  261.8 7.9 %convolution_convert_fusion.1 = bf16[4096,1024]{1,0:T(8,128)(2,1)} fusion(bf16[512,1024]{1,0:T(8,128)(2,1)S(1)} %bitcast.140, f32[512,4096]{1,0:T(8,128)S(1)} %bitcast.192), kind=kOutput, calls=%fused_computation.16 | convolution fusion | flops 4318035968 | bytes 17825792 | tf_op jit(solution)/shard_map/dot_general | solution.py:1169
  269.7 154.7 %shard_map.301 = (bf16[512,3072]{1,0:T(8,128)(2,1)}, f32[8,256,128]{2,1,0:T(8,128)}, f32[16,1024]{1,0:T(8,128)}, f32[128,1024]{1,0:T(8,128)}, f32[32,4096]{1,0:T(8,128)}, /*index=5*/f32[32,1024]{1,0:T(8,128)}) custom-call(bf16[544,3072]{1,0:T(8,128)(2,1)} %convolution_convert_fusion.3.refs_0_, f32[16,1024]{1,0:T(8,128)} %get-tuple-element.31.refs_1_, ...), custom_call_target="tpu_custom_call" | custom-call | tf_op jit(solution)/shard_map/pallas_call | solution.py:704
  424.3 7.1 %multiply_reduce_fusion.1 = (f32[1024]{0:T(1024)S(1)}, f32[512]{0:T(512)S(1)}, f32[512,1024]{1,0:T(8,128)S(1)}) fusion(f32[512]{0:T(512)S(1)} %rsqrt.33, f32[512]{0:T(512)S(1)} %bitcast.164, f32[512]{0:T(512)S(1)} %bitcast.160, bf16[1,256,2,1024]{3,2,1,0:T(2,128)(2,1)S(1)} %copy-done.1, f32[1024]{0:T(1024)S(1)} %bitcast.155, ...), kind=kOutput, calls=%fused_computation.26 | convolution fusion | flops 3225942528 | bytes 12599296 | tf_op jit(solution)/shard_map/dot_general | solution.py:1183
  431.5 0.9 fusion.37
  434.1 0.7 maximum_maximum_fusion.small_vec
  434.8 6.9 %copy_bitcast_fusion = (bf16[1,256,2,1024]{3,2,1,0:T(2,128)(2,1)}, bf16[1,256,2,1024]{3,2,1,0:T(2,128)(2,1)}) fusion(bf16[2,256,1024]{2,1,0:T(8,128)(2,1)S(1)} %bitcast.146, bf16[2,256,1024]{2,1,0:T(8,128)(2,1)S(1)} %bitcast.151), kind=kLoop, calls=%fused_computation.48 | loop fusion | bytes 4194304 | tf_op jit(solution)/shard_map/reshape | solution.py:1187
  442.1 3.1 fusion.20.small_sec
  445.2 2.9 multiply_reduce_fusion.7
  449.4 5.4 %convolution_convert_fusion.2 = bf16[1024,3072]{1,0:T(8,128)(2,1)} fusion(bf16[512,1024]{1,0:T(8,128)(2,1)S(1)} %copy-done.8, bf16[512,3072]{1,0:T(8,128)(2,1)S(1)} %copy-done.22), kind=kOutput, calls=%fused_computation.17 | convolution fusion | flops 3224371200 | bytes 10485760 | tf_op jit(solution)/shard_map/dot_general | solution.py:1182
  454.9 51.2 %shard_map.302 = (f32[32,3072]{1,0:T(8,128)}, f32[120,128]{1,0:T(8,128)}) custom-call(bf16[4,2,2,2,32,3072]{5,4,3,2,1,0:T(8,128)(2,1)} %bitcast.145, f32[16,1024]{1,0:T(8,128)} %maximum_maximum_fusion.small_vec, f32[64,128]{1,0:T(8,128)} %fusion.20.small_sec, f32[40,128]{1,0:T(8,128)} %select_maximum_fusion.small_fst), custom_call_target="tpu_custom_call" | custom-call | tf_op jit(solution)/shard_map/pallas_call | solution.py:919
  506.0 1.2 slice_bitcast_fusion.2
  507.3 0.7 slice.43
  508.5 1.3 slice_bitcast_fusion
  509.8 0.7 slice.46
  511.1 1.3 slice.48
  512.4 1.4 slice.51
  513.8 1.8 copy.69
  516.2 0.8 copy.71
  517.0 0.8 copy.72
  (107 shorter events, 10.2 us)
Async XLA Ops:
  0.6 10.1 %copy-start = (f32[64,128]{1,0:T(8,128)S(1)}, f32[64,128]{1,0:T(8,128)}, u32[]{:S(2)}) copy-start(f32[64,128]{1,0:T(8,128)} %param.33) | copy-start | bytes 98308
  0.7 8.8 %copy-start.10 = (bf16[1,256,2,1024]{3,2,1,0:T(2,128)(2,1)S(1)}, bf16[1,256,2,1024]{3,2,1,0:T(2,128)(2,1)}, u32[]{:S(2)}) copy-start(bf16[1,256,2,1024]{3,2,1,0:T(2,128)(2,1)} %param.34) | copy-start | bytes 3145732
  0.7 8.2 %copy-start.20 = (f32[64]{0:T(128)S(1)}, f32[64]{0:T(128)}, u32[]{:S(2)}) copy-start(f32[64]{0:T(128)} %param.31) | copy-start | bytes 772
  0.7 8.2 %copy-start.16 = (f32[33,64]{1,0:T(8,128)S(1)}, f32[33,64]{1,0:T(8,128)}, u32[]{:S(2)}) copy-start(f32[33,64]{1,0:T(8,128)} %param.30) | copy-start | bytes 25348
  0.7 6.1 %copy-start.19 = (f32[128]{0:T(128)S(1)}, f32[128]{0:T(128)}, u32[]{:S(2)}) copy-start(f32[128]{0:T(128)} %param.29) | copy-start | bytes 1540
  0.7 6.0 %copy-start.18 = (f32[3,3,128]{2,1,0:T(4,128)S(1)}, f32[3,3,128]{2,1,0:T(4,128)}, u32[]{:S(2)}) copy-start(f32[3,3,128]{2,1,0:T(4,128)} %param.28) | copy-start | bytes 13828
  4.9 5.8 %copy-start.17 = (f32[64]{0:T(128)S(1)}, f32[64]{0:T(128)}, u32[]{:S(2)}) copy-start(f32[64]{0:T(128)} %param.32) | copy-start | bytes 772
  8.8 6.5 %copy-start.1 = (bf16[1,256,2,1024]{3,2,1,0:T(2,128)(2,1)S(1)}, bf16[1,256,2,1024]{3,2,1,0:T(2,128)(2,1)}, u32[]{:S(2)}) copy-start(bf16[1,256,2,1024]{3,2,1,0:T(2,128)(2,1)} %param.20) | copy-start | bytes 3145732
  15.6 1.0 copy-start.6
  68.6 1.0 copy-start.7
  201.6 4.6 copy-start.21
  205.3 1.5 copy-start.4
  205.3 8.2 %slice-start = ((s8[8388608]{0:T(1024)(128)(4,1)}), s8[4194304]{0:T(1024)(128)(4,1)S(1)}, s32[]{:S(2)}) async-start(s8[8388608]{0:T(1024)(128)(4,1)} %bitcast.181), calls=%async_computation | async-start | bytes 8388608
  206.7 6.7 %slice-start.1 = ((s8[8388608]{0:T(1024)(128)(4,1)}), s8[4194304]{0:T(1024)(128)(4,1)S(1)}, s32[]{:S(2)}) async-start(s8[8388608]{0:T(1024)(128)(4,1)} %bitcast.181), calls=%async_computation.1 | async-start | bytes 8388608
  228.0 13.5 %copy-start.25 = (bf16[512,4096]{1,0:T(8,128)(2,1)}, bf16[512,4096]{1,0:T(8,128)(2,1)S(1)}, u32[]{:S(2)}) copy-start(bf16[512,4096]{1,0:T(8,128)(2,1)S(1)} %get-tuple-element.72) | copy-start | bytes 12582916
  247.2 1.3 copy-start.2
  247.2 2.3 copy-start.23
  249.5 2.3 copy-start.24
  251.8 2.6 copy-start.26
  251.8 10.0 %slice-start.2 = ((s8[8388608]{0:T(1024)(128)(4,1)}), s8[4194304]{0:T(1024)(128)(4,1)S(1)}, s32[]{:S(2)}) async-start(s8[8388608]{0:T(1024)(128)(4,1)} %bitcast.191), calls=%async_computation.2 | async-start | bytes 8388608
  254.4 7.4 %slice-start.3 = ((s8[8388608]{0:T(1024)(128)(4,1)}), s8[4194304]{0:T(1024)(128)(4,1)S(1)}, s32[]{:S(2)}) async-start(s8[8388608]{0:T(1024)(128)(4,1)} %bitcast.191), calls=%async_computation.3 | async-start | bytes 8388608
  431.4 1.6 copy-start.3
  431.4 1.8 copy-start.5
  433.3 0.8 copy-start.15
  433.3 1.5 copy-start.11
  434.8 6.9 %copy-start.9 = (f32[8,256,128]{2,1,0:T(8,128)S(1)}, f32[8,256,128]{2,1,0:T(8,128)}, u32[]{:S(2)}) copy-start(f32[8,256,128]{2,1,0:T(8,128)} %get-tuple-element.42) | copy-start | bytes 3145732
  442.1 7.3 %copy-start.8 = (bf16[512,1024]{1,0:T(8,128)(2,1)S(1)}, bf16[512,1024]{1,0:T(8,128)(2,1)}, u32[]{:S(2)}) copy-start(bf16[512,1024]{1,0:T(8,128)(2,1)} %copy-done.7) | copy-start | bytes 3145732
  442.1 7.3 %copy-start.22 = (bf16[512,3072]{1,0:T(8,128)(2,1)S(1)}, bf16[512,3072]{1,0:T(8,128)(2,1)}, u32[]{:S(2)}) copy-start(bf16[512,3072]{1,0:T(8,128)(2,1)} %get-tuple-element.40) | copy-start | bytes 9437188
  454.8 60.7 %copy-start.14 = (f32[32,1024]{1,0:T(8,128)S(1)}, f32[32,1024]{1,0:T(8,128)}, u32[]{:S(2)}) copy-start(f32[32,1024]{1,0:T(8,128)} %get-tuple-element.96) | copy-start | bytes 393220
  454.8 61.4 %copy-start.13 = (f32[32,4096]{1,0:T(8,128)S(1)}, f32[32,4096]{1,0:T(8,128)}, u32[]{:S(2)}) copy-start(f32[32,4096]{1,0:T(8,128)} %get-tuple-element.97) | copy-start | bytes 1572868
  506.0 11.0 %copy-start.12 = (f32[128,1024]{1,0:T(8,128)S(1)}, f32[128,1024]{1,0:T(8,128)}, u32[]{:S(2)}) copy-start(f32[128,1024]{1,0:T(8,128)} %get-tuple-element.98) | copy-start | bytes 1572868

commit v2 on v1

--- a/solution.py
+++ b/solution.py
@@ -17,6 +17,8 @@
 F32 = jnp.float32
 MESH = pl.DeviceIdType.MESH
 VMEM_LIMIT = 62 << 20
+SHARE = 0.72
+EARLY, LATE = range(0, 2), range(2, 4)
 
 
 def layer_norm(values, gain):
@@ -313,88 +315,44 @@
     return copy
 
 
-class Gather:
-    SLOTS = 36
-
-    def __init__(self, place, shards, fulls, send, recv, local):
-        self.p, self.shards, self.fulls = place, shards, fulls
+def split_columns(cols, share):
+    return int(cols * share / 128 + 0.5) * 128
+
+
+class Columns:
+    SLOTS = 3
+
+    def __init__(self, place, shards, columns, send, recv, local):
+        self.p, self.shards, self.columns = place, shards, columns
         self.send, self.recv, self.local = send, recv, local
         self.copies = {}
 
-    def go(self, i, name, slot, src, dst, device):
-        self.copies[(i, name)] = push(src, dst, self.send.at[i, slot], self.recv.at[i, slot], device)
+    def go(self, i, slot, src, dst, device):
+        self.copies[(i, slot)] = push(src, dst, self.send.at[i, slot], self.recv.at[i, slot], device)
 
     def start(self):
         p = self.p
         for i, shard in enumerate(self.shards):
-            mine = self.fulls[i].at[p.z, p.x, p.y, p.core]
-            self.go(i, ("z", 1), 1, shard, mine, p.along_z[1])
-            self.go(i, ("z", 0), 0, shard, mine, p.along_z[0])
-            self.go(i, ("x", 0), 3, shard, mine, p.along_x)
-            self.go(i, ("y", 0), 7, shard, mine, p.along_y)
-            self.go(i, ("c", 0), 19, shard, mine, p.sibling)
+            mine = self.columns[i].at[p.z]
+            self.go(i, 1, shard, mine, p.along_z[1])
+            self.go(i, 0, shard, mine, p.along_z[0])
             copy = pltpu.make_async_copy(shard, mine, self.local.at[i])
             copy.start()
-            self.copies[(i, "own")] = copy
-
-    def pass_column(self, d):
+            self.copies[(i, 3)] = copy
+
+    def pass_far(self):
         p = self.p
         for i in range(len(self.shards)):
-            self.copies[(i, ("z", d))].wait_recv()
-            here = self.fulls[i].at[p.others[d], p.x, p.y, p.core]
-            if d == 1:
-                self.go(i, ("z", 2), 2, here, here, p.along_z[0])
-            self.go(i, ("x", d + 1), 4 + d, here, here, p.along_x)
-            self.go(i, ("y", d + 1), 8 + d, here, here, p.along_y)
-            self.go(i, ("c", d + 1), 20 + d, here, here, p.sibling)
-
-    def pass_sides(self, n):
-        p = self.p
-        zz = p.z if n == 0 else p.others[n - 1]
-        for i in range(len(self.shards)):
-            half = self.shards[i].shape[0] // 2
-            full = self.fulls[i]
-            self.copies[(i, ("x", n))].wait_recv()
-            top = full.at[zz, 1 - p.x, p.y, p.core, pl.ds(0, half)]
-            self.go(i, ("top", n), 11 + n, top, top, p.along_y)
-            whole = full.at[zz, 1 - p.x, p.y, p.core]
-            self.go(i, ("c", 4 + n), 23 + n, whole, whole, p.sibling)
-            self.copies[(i, ("y", n))].wait_recv()
-            low = full.at[zz, p.x, 1 - p.y, p.core, pl.ds(half, half)]
-            self.go(i, ("low", n), 15 + n, low, low, p.along_x)
-            whole = full.at[zz, p.x, 1 - p.y, p.core]
-            self.go(i, ("c", 8 + n), 27 + n, whole, whole, p.sibling)
-
-    def pass_last(self, n):
-        p = self.p
-        zz = p.z if n == 0 else p.others[n - 1]
-        for i in range(len(self.shards)):
-            self.copies[(i, ("top", n))].wait_recv()
-            self.copies[(i, ("low", n))].wait_recv()
-            whole = self.fulls[i].at[zz, 1 - p.x, 1 - p.y, p.core]
-            self.go(i, ("c", 12 + n), 31 + n, whole, whole, p.sibling)
+            self.copies[(i, 1)].wait_recv()
+            here = self.columns[i].at[p.others[1]]
+            self.go(i, 2, here, here, p.along_z[0])
 
     def finish(self):
-        for (i, name), copy in self.copies.items():
-            if name == "own":
+        for (i, slot), copy in self.copies.items():
+            if slot == 1:
+                copy.wait_send()
+            else:
                 copy.wait()
-            else:
-                copy.wait_send()
-                if name[0] == "c":
-                    copy.wait_recv()
-
-    def steps(self):
-        return (
-            [functools.partial(self.pass_column, 0), functools.partial(self.pass_column, 1)]
-            + [functools.partial(self.pass_sides, 0), functools.partial(self.pass_column, 2)]
-            + [functools.partial(self.pass_sides, n) for n in (1, 2, 3)]
-            + [functools.partial(self.pass_last, n) for n in range(4)]
-        )
-
-    def rest(self, first=0):
-        for step in self.steps()[first:]:
-            step()
-        self.finish()
 
     @classmethod
     def scratch(cls, count):
@@ -405,6 +363,100 @@
         ]
 
 
+class Gather:
+    SLOTS = 32
+
+    def __init__(self, place, columns, fulls, share, send, recv, local, places=range(4), by_place=()):
+        self.p, self.columns, self.fulls, self.share = place, columns, fulls, share
+        self.places, self.by_place = places, by_place
+        self.send, self.recv, self.local = send, recv, local
+        self.copies = {}
+        self.seen = set()
+
+    def go(self, i, slot, src, dst, device):
+        self.copies[(i, slot)] = push(src, dst, self.send.at[i, slot], self.recv.at[i, slot], device)
+
+    def place(self, n):
+        return self.p.z if n == 0 else self.p.others[n - 1]
+
+    def arrays(self, n):
+        return [i for i in range(len(self.fulls)) if i not in self.by_place or n in self.places]
+
+    def plane(self, i, n):
+        if i in self.by_place:
+            return self.fulls[i].at[n - self.places[0]]
+        return self.fulls[i].at[self.place(n)]
+
+    def ends(self, i, n):
+        p, zz = self.p, self.place(n)
+        return self.columns[i].at[zz], self.plane(i, n).at[p.x, p.y, p.core]
+
+    def start_y(self, places=range(4)):
+        for n in places:
+            for i in self.arrays(n):
+                src, dst = self.ends(i, n)
+                self.go(i, 4 + n, src, dst, self.p.along_y)
+                self.go(i, 16 + n, src, dst, self.p.sibling)
+                copy = pltpu.make_async_copy(src, dst, self.local.at[i, n])
+                copy.start()
+                self.copies[(i, 32 + n)] = copy
+
+    def start_x(self, places=range(4)):
+        for n in places:
+            for i in self.arrays(n):
+                src, dst = self.ends(i, n)
+                self.go(i, n, src, dst, self.p.along_x)
+
+    def pass_sides(self, n):
+        p = self.p
+        for i in self.arrays(n):
+            full = self.plane(i, n)
+            cols = full.shape[4]
+            part = split_columns(cols, self.share)
+            self.copies[(i, n)].wait_recv()
+            whole = full.at[1 - p.x, p.y, p.core]
+            some = full.at[1 - p.x, p.y, p.core, :, pl.ds(0, part)]
+            self.go(i, 8 + n, some, some, p.along_y)
+            self.go(i, 20 + n, whole, whole, p.sibling)
+            self.copies[(i, 4 + n)].wait_recv()
+            whole = full.at[p.x, 1 - p.y, p.core]
+            some = full.at[p.x, 1 - p.y, p.core, :, pl.ds(part, cols - part)]
+            self.go(i, 12 + n, some, some, p.along_x)
+            self.go(i, 24 + n, whole, whole, p.sibling)
+
+    def pass_last(self, n):
+        p = self.p
+        for i in self.arrays(n):
+            self.copies[(i, 8 + n)].wait_recv()
+            self.copies[(i, 12 + n)].wait_recv()
+            whole = self.plane(i, n).at[1 - p.x, 1 - p.y, p.core]
+            self.go(i, 28 + n, whole, whole, p.sibling)
+
+    def arrived(self, n):
+        for i in range(len(self.fulls)):
+            for slot in (16, 20, 24, 28):
+                self.copies[(i, slot + n)].wait_recv()
+            self.copies.pop((i, 32 + n)).wait()
+            self.seen.add((i, n))
+
+    def finish(self):
+        for (i, slot), copy in self.copies.items():
+            if slot >= 32:
+                copy.wait()
+            else:
+                copy.wait_send()
+                if slot >= 16 and (i, slot % 4) not in self.seen:
+                    copy.wait_recv()
+
+    @classmethod
+    def scratch(cls, count):
+        return [
+            pltpu.SemaphoreType.DMA((count, cls.SLOTS)),
+            pltpu.SemaphoreType.DMA((count, cls.SLOTS)),
+            pltpu.SemaphoreType.DMA((count, 4)),
+        ]
+
+
 def everyone(p):
     ids = []
     for d in range(8):
@@ -414,45 +466,79 @@
     return ids
 
 
-def start_kernel(pack, tail, shard, consts, halo, full, packs, send, recv, halo_sems, *gather_sems):
+def start_kernel(count, *refs):
+    pack, tail = refs[:2]
+    shards = refs[2 : 2 + count]
+    consts, halo, full = refs[2 + count : 5 + count]
+    columns = refs[5 + count : 4 + 2 * count]
+    packs, send, recv, halo_sems, column_in = refs[4 + 2 * count : 9 + 2 * count]
+    column_sems = refs[9 + 2 * count : 12 + 2 * count]
+    gather_sems = refs[12 + 2 * count :]
+    columns = [column_in] + list(columns)
     p = Place()
     ids = everyone(p)
     greet(ids)
+    column = Columns(p, shards, columns, *column_sems)
+    gather = Gather(p, columns[:1], [full], 0.5, *gather_sems)
+    column.start()
     copies = [push(pack, packs.at[p.ch, p.seq], send.at[n], recv.at[n], one) for n, one in enumerate(ids)]
     copies.append(push(tail, halo, halo_sems.at[0], halo_sems.at[1], {"ch": lax.rem(p.ch + 1, 8)}))
-    gather = Gather(p, [shard], [full], *gather_sems)
-    gather.start()
     packs[p.ch, p.seq] = pack[...]
+    column.copies.pop((0, 3)).wait()
+    gather.start_x([0])
+    gather.start_y([0])
+    column.copies[(0, 0)].wait_recv()
+    gather.start_x([1])
+    gather.start_y([1])
+    column.pass_far()
+    gather.start_x([2])
+    gather.start_y([2])
+    gather.pass_sides(0)
+    gather.pass_sides(1)
+    column.copies[(0, 2)].wait_recv()
+    gather.start_x([3])
+    gather.start_y([3])
     wait_all(copies)
     row = lax.broadcasted_iota(jnp.int32, (16, 128), 0)
     for c in range(8):
         first = packs[c, 0]
         total = first + packs[c, 1] + packs[c, 2] + packs[c, 3]
         consts[:, c * 128 : (c + 1) * 128] = jnp.where(row < 10, first, total)
-    gather.rest()
-
-
-def start_call(pack, tail, shard):
-    rows, cols = shard.shape
-    consts, halo, full = pl.pallas_call(
-        start_kernel,
+    gather.pass_sides(2)
+    gather.pass_sides(3)
+    for n in range(4):
+        gather.pass_last(n)
+    gather.finish()
+    for slot in (0, 2):
+        column.copies.pop((0, slot)).wait_send()
+    column.finish()
+
+
+def start_call(pack, tail, shards):
+    rows, cols = shards[0].shape
+    count = len(shards)
+    out = pl.pallas_call(
+        functools.partial(start_kernel, count),
         out_shape=[
             jax.ShapeDtypeStruct((16, 1024), F32),
             jax.ShapeDtypeStruct(tail.shape, BF),
             jax.ShapeDtypeStruct((4, 2, 2, 2, rows, cols), BF),
-        ],
-        in_specs=[VM, VM, ANYWHERE],
-        out_specs=[VM, VM, ANYWHERE],
+        ]
+        + [jax.ShapeDtypeStruct((4,) + one.shape, BF) for one in shards[1:]],
+        in_specs=[VM, VM] + [VM] * count,
+        out_specs=[VM, VM, ANYWHERE] + [VM] * (count - 1),
         scratch_shapes=[
             pltpu.VMEM((8, 4, 16, 128), F32),
             pltpu.SemaphoreType.DMA((31,)),
             pltpu.SemaphoreType.DMA((31,)),
             pltpu.SemaphoreType.DMA((2,)),
+            pltpu.VMEM((4, rows, cols), BF),
         ]
+        + Columns.scratch(count)
         + Gather.scratch(1),
         compiler_params=pltpu.CompilerParams(collective_id=4, has_side_effects=True, vmem_limit_bytes=VMEM_LIMIT),
-    )(pack, tail, shard)
-    return consts, halo, full.reshape(rows * 32, cols)
+    )(pack, tail, *shards)
+    return out[0], out[1], out[2].reshape(rows * 32, cols), out[3:]
 
 
 def lagged(u, buf, b, stream, lane, size, width):
@@ -506,7 +592,7 @@
 
 def forward_kernel(size, *refs):
     u, consts, mask, h_ref, fh, fl, th, tl, lanes = refs[:9]
-    shards = refs[9:12]
+    columns = refs[9:12]
     mixer, kept, convolved = refs[12:15]
     fulls = refs[15:18]
     xs, abc, ys, pieces, gates, mixes, bufs = refs[18:25]
@@ -514,7 +600,8 @@
     p = Place()
     width = 1024
     greet([{"ch": one} for one in p.ch_ahead] + [p.sibling, p.along_y])
-    gather = Gather(p, shards, fulls, *refs[31:])
+    gather = Gather(p, columns, fulls, SHARE, *refs[31:], places=EARLY, by_place=(2,))
+    gather.start_y()
 
     def make(block):
         lane = pl.multiple_of(block * 128, 128)
@@ -531,17 +618,15 @@
             step(b, 0)
 
     arriving = send_pieces(p, pieces, kept, send, recv, local, make)
-    gather.start()
-    steps = gather.steps()
+    gather.start_x()
     filter_spectra(fh, fl, lanes, h_ref, abc, 8, size)
     wait_all(arriving)
     spectra(fh, fl, kept, xs, 8)
-    steps[0]()
     products_forward(xs, abc, lanes, xs, 8, size)
     inverse_blocks(th, tl, xs, ys, 8)
     leaving = send_blocks(p, ys, convolved, send_back, recv_back, local_back)
-    for step in steps[1:4]:
-        step()
+    for n in range(4):
+        gather.pass_sides(n)
     wait_all(leaving)
     for c in range(8):
         at = slice(c * 128, (c + 1) * 128)
@@ -549,7 +634,9 @@
             rows = slice(b * size, (b + 1) * size)
             long_part = convolved[c, :, b * 128 : (b + 1) * 128].astype(F32) + consts[9:10, at] * mixes[c, b]
             mixer[rows, at] = (gates[c, b] * long_part * mask[rows]).astype(BF)
-    gather.rest(4)
+    for n in range(4):
+        gather.pass_last(n)
+    gather.finish()
 
 
 def backward_kernel(size, count, *refs):
@@ -563,8 +650,11 @@
     p = Place()
     width = 1024
     greet([{"ch": one} for one in p.ch_ahead] + [p.sibling, p.along_y])
-    scatter = Scatter(p, [(one, 0, one.shape[5]) for one in grads], outs, rest[21:])
-    scatter.start()
+    whole = [grads[0]] + [(one, 0, one.shape[5]) for one in grads[1:]]
+    stops = [None] + list(outs[1:])
+    scatter = Scatter(p, whole, [outs[0]] + [None] * (count - 1), stops, SHARE, rest[21:])
+    scatter.start(1)
+    scatter.start(2)
     sums[...] = jnp.zeros_like(sums)
 
     def grad_parts(block, b, rows, skip):
@@ -592,18 +682,19 @@
         sums[9:10, at] = total
 
     arriving = send_pieces(p, pieces, arrived, send, recv, local, make)
+    scatter.turn(0)
+    scatter.core(1)
     filter_spectra(fh, fl, lanes, h_ref, abc, 8, size)
+    scatter.core(2)
     spectra(fh, fl, kept, xs, 8)
-    for i in range(count):
-        scatter.core(i)
     wait_all(arriving)
     spectra(fh, fl, arrived, ds, 8)
     products_backward(xs, ds, abc, gh, lanes, 8, size)
     inverse_blocks(th, tl, ds, pieces, 8)
     leaving = send_blocks(p, pieces, returned, send_back, recv_back, local_back)
     filter_gradient(th, tl, gh, dh_ref, 8, size)
-    for i in range(count):
-        scatter.first(i)
+    scatter.third(0)
+    scatter.first(1)
     wait_all(leaving)
 
     def edges(c, carry):
@@ -620,8 +711,7 @@
 
     lax.fori_loop(0, 8, edges, 0)
     edge = push(edge_out, edge_in, edge_sems.at[0], edge_sems.at[1], {"ch": lax.rem(p.ch + 7, 8)})
-    for i in range(count):
-        scatter.second(i)
+    scatter.first(2)
     edge.wait()
     inside = jnp.where(p.ch < 7, 1.0, 0.0)
 
@@ -654,10 +744,238 @@
         return carry
 
     lax.fori_loop(0, 8, streams, 0)
-    for i in range(count):
-        scatter.third(i)
-    for i in range(count):
-        scatter.last(i)
+    scatter.second(1)
+    scatter.second(2)
+    scatter.last(0)
+
+
+def nt(a, b):
+    return lax.dot_general(a, b, (((1,), (1,)), ((), ())), preferred_element_type=F32)
+
+
+def tn(a, b):
+    return lax.dot_general(a, b, (((0,), (0,)), ((), ())), preferred_element_type=F32)
+
+
+GELU_ONE = math.sqrt(2.0 / math.pi)
+GELU_THREE = GELU_ONE * 0.044715
+
+
+class Planes:
+    def __init__(self, place, column, acc, one_a, one_b, two_a, two_b, send, recv):
+        self.p, self.column = place, column
+        self.acc, self.one_a, self.one_b, self.two_a, self.two_b = acc, one_a, one_b, two_a, two_b
+        self.send, self.recv = send, recv
+        self.copies = {}
+        cols = acc.shape[4]
+        half = split_columns(cols, 0.5)
+        self.low, self.high = pl.ds(0, half), pl.ds(half, cols - half)
+
+    def go(self, n, slot, src, dst, device):
+        self.copies[(n, slot)] = push(src, dst, self.send.at[n, slot], self.recv.at[n, slot], device)
+
+    def done(self, n, *slots):
+        for slot in slots:
+            self.copies[(n, slot)].wait()
+
+    def core(self, n, made):
+        self.go(n, 0, made.at[:, :, 1 - self.p.core], self.acc.at[n], self.p.sibling)
+
+    def sides(self, n, made):
+        p, acc = self.p, self.acc.at[n]
+        self.done(n, 0)
+
+        def step(k, carry):
+            xx, yy = k // 2, lax.rem(k, 2)
+            acc[xx, yy] = add_rows(acc[xx, yy], made[xx, yy, p.core])
+            return carry
+
+        lax.fori_loop(0, 4, step, 0)
+        self.go(n, 1, acc.at[:, 1 - p.y, :, self.low], self.one_a.at[n], p.along_y)
+        self.go(n, 2, acc.at[1 - p.x, :, :, self.high], self.one_b.at[n], p.along_x)
+
+    def cross(self, n):
+        p, acc = self.p, self.acc.at[n]
+        low, high = self.low, self.high
+        self.done(n, 1, 2)
+        for k in range(2):
+            acc[k, p.y, :, low] = add_rows(acc[k, p.y, :, low], self.one_a[n, k])
+            acc[p.x, k, :, high] = add_rows(acc[p.x, k, :, high], self.one_b[n, k])
+        self.go(n, 3, acc.at[1 - p.x, p.y, :, low], self.two_a.at[n], p.along_x)
+        self.go(n, 4, acc.at[p.x, 1 - p.y, :, high], self.two_b.at[n], p.along_y)
+
+    def last(self, n, zz):
+        p, acc = self.p, self.acc.at[n]
+        low, high = self.low, self.high
+        self.done(n, 3, 4)
+        self.column[zz, :, low] = add_rows(acc[p.x, p.y, :, low], self.two_a[n])
+        self.column[zz, :, high] = add_rows(acc[p.x, p.y, :, high], self.two_b[n])
+
+    @staticmethod
+    def scratch(rows, cols):
+        half = split_columns(cols, 0.5)
+        return [
+            pltpu.VMEM((4, 2, 2, rows, cols), BF),
+            pltpu.VMEM((4, 2, rows, half), BF),
+            pltpu.VMEM((4, 2, rows, cols - half), BF),
+            pltpu.VMEM((4, rows, half), BF),
+            pltpu.VMEM((4, rows, cols - half), BF),
+            pltpu.SemaphoreType.DMA((4, 5)),
+            pltpu.SemaphoreType.DMA((4, 5)),
+        ]
+
+
+def feed_forward_kernel(*refs):
+    mixer, tokens, mask, cot, consts, w_out, w_up, early, column = refs[:9]
+    result, grad_after, grad_mixer, grad_gain, grad_out, sum_column, grad_up = refs[9:16]
+    up, planes, late, total, unit, scale, normed, turned, da, pre, dact, act, dpre, kept_down, kept_up = refs[16:31]
+    up_sem, plane_sems, out_sems = refs[31:34]
+    gather_sems, scatter_refs = refs[34:37], refs[37:]
+    p = Place()
+    greet([p.along_x, p.along_y, p.sibling])
+    gather = Gather(p, [column], [late], 0.5, *gather_sems, places=LATE, by_place=(0,))
+    gather.start_x()
+    gather.start_y()
+    sums = Planes(p, sum_column, *scatter_refs)
+    loads = [pltpu.make_async_copy(w_up, up, up_sem)]
+    loads += [pltpu.make_async_copy(early.at[n], planes.at[n], plane_sems.at[n]) for n in EARLY]
+    for load in loads:
+        load.start()
+    gain = consts[11:12, :]
+    total[...] = mm(mixer[...], w_out[...])
+
+    def norm(i, carry):
+        rows = pl.ds(pl.multiple_of(i * 32, 32), 32)
+        zero = tokens[rows].astype(F32) * mask[rows, 0:1]
+        value = zero + total[rows]
+        total[rows] = value
+        centre = value - jnp.mean(value, axis=1, keepdims=True)
+        inverse = lax.rsqrt(jnp.mean(centre * centre, axis=1, keepdims=True) + EPS)
+        one = centre * inverse
+        unit[rows] = one
+        scale[rows] = jnp.broadcast_to(inverse, (32, 128))
+        normed[rows] = (one * gain).astype(BF)
+        return carry
+
+    lax.fori_loop(0, 16, norm, 0)
+    turned[...] = normed[...].T
+    wait_all(loads)
+    writes = [None] * 4
+    for n in range(4):
+        zz = gather.place(n)
+        cols = pl.ds(pl.multiple_of(zz * 1024, 1024), 1024)
+        slot = n % 2
+        made = kept_down.at[slot]
+        pre[...] = mm(normed[...], up[:, cols])
+        if n < 2:
+            gather.pass_sides(n + 2)
+            plane = planes.at[n]
+        else:
+            gather.arrived(n)
+            plane = late.at[n - 2]
+        if n > 0:
+            sums.sides(n - 1, kept_down.at[1 - slot])
+        dact[...] = nt(cot[...], plane[...].reshape(1024, 1024))
+
+        def gelu(i, carry):
+            rows = pl.ds(pl.multiple_of(i * 16, 16), 16)
+            x = pre[rows]
+            square = x * x
+            t = jnp.tanh(x * (GELU_ONE + GELU_THREE * square))
+            half = 0.5 + 0.5 * t
+            value = x * half
+            act[rows] = value.astype(BF)
+            slope = half + value * (1.0 - t) * (GELU_ONE + 3.0 * GELU_THREE * square)
+            dpre[rows] = (dact[rows] * slope).astype(BF)
+            return carry
+
+        lax.fori_loop(0, 32, gelu, 0)
+        if n > 1:
+            wait_all(writes[n - 2])
+        made[...] = tn(act[...], cot[...]).astype(BF).reshape(2, 2, 2, 128, 1024)
+        sums.core(n, made)
+        total[...] += mm(act[...], plane[...].reshape(1024, 1024))
+        if n > 1:
+            sums.cross(n - 2)
+        else:
+            gather.pass_last(n + 2)
+        back = nt(dpre[...], up[:, cols])
+        da[...] = back if n == 0 else da[...] + back
+        kept_up[slot] = mm(turned[...], dpre[...]).astype(BF)
+        writes[n] = [pltpu.make_async_copy(kept_up.at[slot], grad_up.at[:, cols], out_sems.at[n])]
+        for copy in writes[n]:
+            copy.start()
+    sums.sides(3, kept_down.at[1])
+    sums.cross(2)
+    sums.last(0, gather.place(0))
+
+    def finish(i, gain_sum):
+        rows = pl.ds(pl.multiple_of(i * 32, 32), 32)
+        result[rows] = total[rows].astype(BF)
+        one = unit[rows]
+        back = da[rows]
+        e = back * gain
+        inner = e - jnp.mean(e, axis=1, keepdims=True) - one * jnp.mean(e * one, axis=1, keepdims=True)
+        after = cot[rows].astype(F32) + scale[rows, 0:1] * inner
+        grad_after[rows] = after
+        normed[rows] = after.astype(BF)
+        return gain_sum + jnp.sum(back * one, axis=0, keepdims=True)
+
+    grad_gain[...] = lax.fori_loop(0, 16, finish, jnp.zeros((1, 1024), F32))
+    grad_mixer[...] = nt(normed[...], w_out[...]).astype(BF)
+    sums.cross(3)
+    sums.last(1, gather.place(1))
+    sums.last(2, gather.place(2))
+    grad_out[...] = tn(mixer[...], normed[...]).astype(BF)
+    for n in (2, 3):
+        wait_all(writes[n])
+    gather.finish()
+    sums.last(3, gather.place(3))
+
+
+def feed_forward_call(mixer, tokens, mask, cot, consts, w_out, w_up, early, column):
+    rows, width = mixer.shape
+    hidden = w_up.shape[1]
+    wide = (rows, width)
+    square = (width, width)
+    part = column.shape[1:]
+    return pl.pallas_call(
+        feed_forward_kernel,
+        out_shape=[
+            jax.ShapeDtypeStruct(wide, BF),
+            jax.ShapeDtypeStruct(wide, F32),
+            jax.ShapeDtypeStruct(wide, BF),
+            jax.ShapeDtypeStruct((1, width), F32),
+            jax.ShapeDtypeStruct(square, BF),
+            jax.ShapeDtypeStruct((4,) + part, BF),
+            jax.ShapeDtypeStruct((width, hidden), BF),
+        ],
+        in_specs=[VM] * 6 + [ANYWHERE] * 3,
+        out_specs=[VM] * 6 + [ANYWHERE],
+        scratch_shapes=[
+            pltpu.VMEM((width, hidden), BF),
+            pltpu.VMEM((len(EARLY), 2, 2, 2) + part, BF),
+            pltpu.VMEM((len(LATE), 2, 2, 2) + part, BF),
+            pltpu.VMEM(wide, F32),
+            pltpu.VMEM(wide, F32),
+            pltpu.VMEM((rows, 128), F32),
+            pltpu.VMEM(wide, BF),
+            pltpu.VMEM((width, rows), BF),
+            pltpu.VMEM(wide, F32),
+            pltpu.VMEM(wide, F32),
+            pltpu.VMEM(wide, F32),
+            pltpu.VMEM(wide, BF),
+            pltpu.VMEM(wide, BF),
+            pltpu.VMEM((2, 2, 2, 2) + part, BF),
+            pltpu.VMEM((2,) + square, BF),
+            pltpu.SemaphoreType.DMA,
+            pltpu.SemaphoreType.DMA((len(EARLY),)),
+            pltpu.SemaphoreType.DMA((4,)),
+        ]
+        + Gather.scratch(1)
+        + Planes.scratch(*part),
+        compiler_params=pltpu.CompilerParams(collective_id=5, has_side_effects=True, vmem_limit_bytes=VMEM_LIMIT),
+    )(mixer, tokens, mask, cot, consts, w_out, w_up, early, column)
 
 
 def exchange_sems():
@@ -665,17 +983,18 @@
     return pieces + [pltpu.SemaphoreType.DMA((7,))] * 2 + [pltpu.SemaphoreType.DMA]
 
 
-def forward_call(u, consts, mask, filt, tables, shards, size):
+def forward_call(u, consts, mask, filt, tables, columns, size):
     rows = 2 * size
     block = (8, size, 256)
     piece = (8, 2, size, 128)
     operands = (u, consts, mask, filt) + tables
-    count = len(shards)
-    whole = [jax.ShapeDtypeStruct((4, 2, 2, 2) + one.shape, BF) for one in shards]
+    count = len(columns)
+    whole = [jax.ShapeDtypeStruct((4, 2, 2, 2) + one.shape[1:], BF) for one in columns[:2]]
+    whole.append(jax.ShapeDtypeStruct((len(EARLY), 2, 2, 2) + columns[2].shape[1:], BF))
     out = pl.pallas_call(
         functools.partial(forward_kernel, size),
         out_shape=[jax.ShapeDtypeStruct((rows, 1024), BF)] + [jax.ShapeDtypeStruct(block, BF)] * 2 + whole,
-        in_specs=[VM] * len(operands) + [ANYWHERE] * count,
+        in_specs=[VM] * (len(operands) + count),
         out_specs=[VM] * 3 + [ANYWHERE] * count,
         scratch_shapes=[
             pltpu.VMEM((8, 2 * size, 256), F32),
@@ -689,8 +1008,8 @@
         + exchange_sems()
         + Gather.scratch(count),
         compiler_params=pltpu.CompilerParams(collective_id=1, has_side_effects=True, vmem_limit_bytes=VMEM_LIMIT),
-    )(*operands, *shards)
-    return out[:3], [one.reshape(-1, one.shape[-1]) for one in out[3:]]
+    )(*operands, *columns)
+    return out[:3], [one.reshape(-1, one.shape[-1]) for one in out[3:5]] + [out[5]]
 
 
 def backward_call(u, consts, mask, grad_mixer, convolved, kept, filt, tables, grads, size):
@@ -699,8 +1018,8 @@
     piece = (8, 2, size, 128)
     operands = (u, consts, mask, grad_mixer, convolved, kept, filt) + tables
     count = len(grads)
-    shapes = [(one.shape[0] // 32, one.shape[1]) for one in grads]
-    views = [one.reshape((4, 2, 2, 2) + shape) for one, shape in zip(grads, shapes)]
+    shapes = [grads[0].shape[1:]] + [(one.shape[0] // 32, one.shape[1]) for one in grads[1:]]
+    views = [grads[0]] + [one.reshape((4, 2, 2, 2) + shape) for one, shape in zip(grads[1:], shapes[1:])]
     out = pl.pallas_call(
         functools.partial(backward_kernel, size, count),
         out_shape=[
@@ -708,8 +1027,9 @@
             jax.ShapeDtypeStruct((8, size, 128), F32),
             jax.ShapeDtypeStruct((16, 1024), F32),
         ]
-        + [jax.ShapeDtypeStruct(shape, F32) for shape in shapes],
-        in_specs=[VM] * len(operands) + [ANYWHERE] * count,
+        + [jax.ShapeDtypeStruct(shapes[0], F32)]
+        + [jax.ShapeDtypeStruct((4,) + shape, BF) for shape in shapes[1:]],
+        in_specs=[VM] * (len(operands) + 1) + [ANYWHERE] * (count - 1),
         out_specs=[VM] * (3 + count),
         scratch_shapes=[
             pltpu.VMEM((8, 2 * size, 256), F32),
@@ -729,7 +1049,7 @@
         ]
         + exchange_sems()
         + [pltpu.SemaphoreType.DMA((2,))]
-        + Scatter.scratch(shapes),
+        + Scatter.scratch([shape + (n > 0, n > 0) for n, shape in enumerate(shapes)], SHARE),
         compiler_params=pltpu.CompilerParams(collective_id=2, has_side_effects=True, vmem_limit_bytes=VMEM_LIMIT),
     )(*operands, *views)
     return out[:3], out[3:]
@@ -742,14 +1062,22 @@
 class Scatter:
     SLOTS = 11
 
-    def __init__(self, place, grads, outs, refs):
+    def __init__(self, place, grads, outs, columns, share, refs):
+        self.p, self.grads, self.outs, self.columns, self.share = place, grads, outs, columns, share
         count = len(grads)
-        self.p, self.grads, self.outs = place, grads, outs
-        names = ("own", "acc", "one_a", "one_b", "two_a", "two_b", "three", "four")
-        for n, name in enumerate(names):
-            setattr(self, name, refs[n * count : (n + 1) * count])
-        self.send, self.recv, self.local = refs[8 * count : 8 * count + 3]
+        self.bufs = []
+        at = 0
+        for one, column in zip(grads, columns):
+            names = Scatter.names(isinstance(one, tuple), column is not None)
+            self.bufs.append(dict(zip(names, refs[at : at + len(names)])))
+            at += len(names)
+        self.send, self.recv, self.local = refs[at : at + 3]
         self.copies = {}
+
+    @staticmethod
+    def names(whole, stops):
+        before = ("own", "acc", "one_a", "one_b", "two_a", "two_b") if whole else ()
+        return before + (() if stops else ("three", "four"))
 
     def go(self, i, slot, src, dst, device):
         copy = push(src, dst, self.send.at[i, slot], self.recv.at[i, slot], device)
@@ -766,19 +1094,24 @@
         return ref.at[zz, :, :, core, :, pl.ds(first, cols)]
 
     def load(self, i, zz):
-        copy = pltpu.make_async_copy(self.part(i, zz, self.p.core), self.own[i].at[zz % 2], self.local.at[i, zz])
+        own = self.bufs[i]["own"]
+        copy = pltpu.make_async_copy(self.part(i, zz, self.p.core), own.at[zz % 2], self.local.at[i, zz])
         copy.start()
         self.copies[(i, "own", zz)] = copy
 
-    def start(self):
-        for i in range(len(self.grads)):
-            for zz in range(4):
-                self.go(i, zz, self.part(i, zz, 1 - self.p.core), self.acc[i].at[zz], self.p.sibling)
-            self.load(i, 0)
-            self.load(i, 1)
+    def start(self, i):
+        for zz in range(4):
+            self.go(i, zz, self.part(i, zz, 1 - self.p.core), self.bufs[i]["acc"].at[zz], self.p.sibling)
+        self.load(i, 0)
+        self.load(i, 1)
+
+    def halves(self, i):
+        cols = self.grads[i][2]
+        part = split_columns(cols, self.share)
+        return pl.ds(0, part), pl.ds(part, cols - part)
 
     def core(self, i):
-        p, acc, own = self.p, self.acc[i], self.own[i]
+        p, acc, own = self.p, self.bufs[i]["acc"], self.bufs[i]["own"]
         for zz in range(4):
             self.copies[(i, "own", zz)].wait()
             self.done(i, zz)
@@ -791,74 +1124,88 @@
             lax.fori_loop(0, 4, step, 0)
             if zz < 2:
                 self.load(i, zz + 2)
-        half = acc.shape[3] // 2
-        self.go(i, 4, acc.at[:, :, 1 - p.y, pl.ds(0, half)], self.one_a[i], p.along_y)
-        self.go(i, 5, acc.at[:, 1 - p.x, :, pl.ds(half, half)], self.one_b[i], p.along_x)
+        low, high = self.halves(i)
+        self.go(i, 4, acc.at[:, :, 1 - p.y, :, low], self.bufs[i]["one_a"], p.along_y)
+        self.go(i, 5, acc.at[:, 1 - p.x, :, :, high], self.bufs[i]["one_b"], p.along_x)
 
     def first(self, i):
-        p, acc = self.p, self.acc[i]
-        half = acc.shape[3] // 2
+        p, acc = self.p, self.bufs[i]["acc"]
+        one_a, one_b = self.bufs[i]["one_a"], self.bufs[i]["one_b"]
+        low, high = self.halves(i)
         self.done(i, 4, 5)
 
         def step(n, carry):
             zz, w = n // 2, lax.rem(n, 2)
-            acc[zz, w, p.y, :half] = add_rows(acc[zz, w, p.y, :half], self.one_a[i][zz, w])
-            acc[zz, p.x, w, half:] = add_rows(acc[zz, p.x, w, half:], self.one_b[i][zz, w])
+            acc[zz, w, p.y, :, low] = add_rows(acc[zz, w, p.y, :, low], one_a[zz, w])
+            acc[zz, p.x, w, :, high] = add_rows(acc[zz, p.x, w, :, high], one_b[zz, w])
             return carry
 
         lax.fori_loop(0, 8, step, 0)
-        self.go(i, 6, acc.at[:, 1 - p.x, p.y, pl.ds(0, half)], self.two_a[i], p.along_x)
-        self.go(i, 7, acc.at[:, p.x, 1 - p.y, pl.ds(half, half)], self.two_b[i], p.along_y)
+        self.go(i, 6, acc.at[:, 1 - p.x, p.y, :, low], self.bufs[i]["two_a"], p.along_x)
+        self.go(i, 7, acc.at[:, p.x, 1 - p.y, :, high], self.bufs[i]["two_b"], p.along_y)
 
     def second(self, i):
-        p, acc = self.p, self.acc[i]
-        half = acc.shape[3] // 2
+        p, acc = self.p, self.bufs[i]["acc"]
+        two_a, two_b = self.bufs[i]["two_a"], self.bufs[i]["two_b"]
+        low, high = self.halves(i)
         self.done(i, 6, 7)
+        column = self.columns[i]
 
         def step(zz, carry):
-            acc[zz, p.x, p.y, :half] = add_rows(acc[zz, p.x, p.y, :half], self.two_a[i][zz])
-            acc[zz, p.x, p.y, half:] = add_rows(acc[zz, p.x, p.y, half:], self.two_b[i][zz])
+            here = acc.at[zz, p.x, p.y] if column is None else column.at[zz]
+            here[:, low] = add_rows(acc[zz, p.x, p.y, :, low], two_a[zz])
+            here[:, high] = add_rows(acc[zz, p.x, p.y, :, high], two_b[zz])
             return carry
 
         lax.fori_loop(0, 4, step, 0)
-        self.go(i, 8, acc.at[p.others[2], p.x, p.y], self.three[i].at[0], p.along_z[0])
-        self.go(i, 9, acc.at[p.others[0], p.x, p.y], self.three[i].at[1], p.along_z[0])
+        if column is None:
+            self.turn(i)
+
+    def sums(self, i, zz):
+        if isinstance(self.grads[i], tuple):
+            return self.bufs[i]["acc"].at[zz, self.p.x, self.p.y]
+        return self.grads[i].at[zz]
+
+    def turn(self, i):
+        p, three = self.p, self.bufs[i]["three"]
+        self.go(i, 8, self.sums(i, p.others[2]), three.at[0], p.along_z[0])
+        self.go(i, 9, self.sums(i, p.others[0]), three.at[1], p.along_z[0])
 
     def third(self, i):
-        p, acc = self.p, self.acc[i]
-        far = p.others[1]
+        p, three = self.p, self.bufs[i]["three"]
         self.done(i, 8, 9)
-        acc[far, p.x, p.y] = add_rows(acc[far, p.x, p.y], self.three[i][0])
-        self.go(i, 10, acc.at[far, p.x, p.y], self.four[i], p.along_z[1])
+        far = self.sums(i, p.others[1])
+        three[0] = add_rows(far[...], three[0])
+        self.go(i, 10, three.at[0], self.bufs[i]["four"], p.along_z[1])
 
     def last(self, i):
-        p, acc = self.p, self.acc[i]
+        three, four = self.bufs[i]["three"], self.bufs[i]["four"]
         self.done(i, 10)
-        total = acc[p.z, p.x, p.y].astype(F32) + self.three[i][1].astype(F32) + self.four[i][...].astype(F32)
-        cols = self.grads[i][2]
-        first = self.grads[i][1]
-        self.outs[i][:, first : first + cols] = total
+        total = self.sums(i, self.p.z)[...].astype(F32) + three[1].astype(F32) + four[...].astype(F32)
+        if isinstance(self.grads[i], tuple):
+            _, first, cols = self.grads[i]
+            self.outs[i][:, first : first + cols] = total
+        else:
+            self.outs[i][...] = total
 
     @classmethod
-    def scratch(cls, shapes):
-        count = len(shapes)
-        bufs = [[] for _ in range(8)]
-        for rows, cols in shapes:
-            half = rows // 2
-            for place, shape in enumerate(
-                (
-                    (2, 2, 2, rows, cols),
-                    (4, 2, 2, rows, cols),
-                    (4, 2, half, cols),
-                    (4, 2, half, cols),
-                    (4, half, cols),
-                    (4, half, cols),
-                    (2, rows, cols),
-                    (rows, cols),
-                )
-            ):
-                bufs[place].append(pltpu.VMEM(shape, BF))
-        return [one for group in bufs for one in group] + [
+    def scratch(cls, kinds, share):
+        count = len(kinds)
+        bufs = []
+        for rows, cols, whole, stops in kinds:
+            part = split_columns(cols, share)
+            shapes = {
+                "own": (2, 2, 2, rows, cols),
+                "acc": (4, 2, 2, rows, cols),
+                "one_a": (4, 2, rows, part),
+                "one_b": (4, 2, rows, cols - part),
+                "two_a": (4, rows, part),
+                "two_b": (4, rows, cols - part),
+                "three": (2, rows, cols),
+                "four": (rows, cols),
+            }
+            bufs += [pltpu.VMEM(shapes[name], BF) for name in cls.names(whole, stops)]
+        return bufs + [
             pltpu.SemaphoreType.DMA((count, cls.SLOTS)),
             pltpu.SemaphoreType.DMA((count, cls.SLOTS)),
             pltpu.SemaphoreType.DMA((count, 4)),
@@ -868,12 +1215,23 @@
 PARTS = 3
 
 
-def scatter_kernel(grad, small_vec, small_sec, small_fst, out, small_out, gathered, joined, small_send, small_recv, *refs):
+def scatter_kernel(count, *refs):
+    grad, small_vec, small_sec, small_fst = refs[:4]
+    columns = refs[4 : 4 + count]
+    out, small_out = refs[4 + count : 6 + count]
+    outs = refs[6 + count : 6 + 2 * count]
+    gathered, joined, small_send, small_recv = refs[6 + 2 * count : 10 + 2 * count]
     p = Place()
     greet([{"ch": one} for one in p.ch_ahead] + [{"seq": one} for one in p.seq_ahead])
     cols = grad.shape[5] // PARTS
-    scatter = Scatter(p, [(grad, n * cols, cols) for n in range(PARTS)], [out] * PARTS, refs)
-    scatter.start()
+    parts = [(grad, n * cols, cols) for n in range(PARTS)]
+    scatter = Scatter(
+        p, parts + list(columns), [out] * PARTS + list(outs), [None] * (PARTS + count), 0.5, refs[10 + 2 * count :]
+    )
+    for n in range(PARTS):
+        scatter.start(n)
+    for n in range(count):
+        scatter.turn(PARTS + n)
 
     vec_rows = small_vec.shape[0]
     fst_rows = small_fst.shape[0]
@@ -891,6 +1249,7 @@
     gathered[p.ch, vec_rows:] = small_fst[...]
 
     stages = (scatter.core, scatter.first, scatter.second, scatter.third, scatter.last)
+    later = [functools.partial(stage, PARTS + n) for stage in (scatter.third, scatter.last) for n in range(count)]
     for time in range(PARTS + len(stages) - 1):
         for n, stage in enumerate(stages):
             if 0 <= time - n < PARTS:
@@ -906,6 +1265,10 @@
                 push(joined.at[p.seq], joined.at[p.seq], small_send.at[14 + d], small_recv.at[14 + d], {"seq": p.seq_ahead[d]})
                 for d in range(3)
             ]
+        if time > 0 and later:
+            later.pop(0)()
+    for step in later:
+        step()
     wait_all(small_copies)
     total = joined[0]
     for n in range(1, 4):
@@ -913,26 +1276,30 @@
     small_out[...] = total
 
 
-def scatter_sums(grad, vec, sec, fst):
+def scatter_sums(grad, vec, sec, fst, columns):
     rows, cols = grad.shape[0] // 32, grad.shape[1]
     small = vec.shape[0] + fst.shape[0]
-    return pl.pallas_call(
-        scatter_kernel,
+    count = len(columns)
+    kinds = [(rows, cols // PARTS, True, False)] * PARTS + [one.shape[1:] + (False, False) for one in columns]
+    out = pl.pallas_call(
+        functools.partial(scatter_kernel, count),
         out_shape=[
             jax.ShapeDtypeStruct((rows, cols), F32),
             jax.ShapeDtypeStruct((small + sec.shape[0], 128), F32),
-        ],
-        in_specs=[ANYWHERE] + [VM] * 3,
-        out_specs=[VM] * 2,
+        ]
+        + [jax.ShapeDtypeStruct(one.shape[1:], F32) for one in columns],
+        in_specs=[ANYWHERE] + [VM] * (3 + count),
+        out_specs=[VM] * (2 + count),
         scratch_shapes=[
             pltpu.VMEM((8, small, 128), F32),
             pltpu.VMEM((4, small + sec.shape[0], 128), F32),
             pltpu.SemaphoreType.DMA((17,)),
             pltpu.SemaphoreType.DMA((17,)),
         ]
-        + Scatter.scratch([(rows, cols // PARTS)] * PARTS),
+        + Scatter.scratch(kinds, 0.5),
         compiler_params=pltpu.CompilerParams(collective_id=3, has_side_effects=True, vmem_limit_bytes=VMEM_LIMIT),
-    )(grad.reshape(4, 2, 2, 2, rows, cols), vec, sec, fst)
+    )(grad.reshape(4, 2, 2, 2, rows, cols), vec, sec, fst, *columns)
+    return out[0], out[1], out[2:]
 
 
 def general_body(
@@ -1128,10 +1495,11 @@
     gains = jnp.where(lane[None, :], jnp.tile(gains, (1, chans // part)), 0.0)
     pack = jnp.concatenate([conv_taps.reshape(9, chans), skip_gain[None], gains, jnp.zeros((4, chans), F32)])
     by_bucket = jnp.swapaxes(tokens[0], 0, 1)
-    consts, halo, full_in = start_call(pack, by_bucket[:, size - 16 :], in_weight)
+    consts, halo, full_in, columns = start_call(
+        pack, by_bucket[:, size - 16 :], (in_weight, out_weight, up_weight, down_weight)
+    )
 
     full_gain_one = consts[10]
-    full_gain_two = consts[11]
 
     local = ch_place * size + jnp.arange(size, dtype=jnp.int32)
     mask = (local[None, :] < lengths[0][:, None]).astype(F32).reshape(rows, 1)
@@ -1152,32 +1520,17 @@
     filt_blocks = filt.reshape(8, size, chans)
 
     wide_mask = jnp.broadcast_to(mask, (rows, 128))
-    (mixer, kept, convolved), (full_out, full_up, full_down) = forward_call(
-        streams, consts, wide_mask, filt_blocks, tables, (out_weight, up_weight, down_weight), size
+    (mixer, kept, convolved), (full_out, full_up, early) = forward_call(
+        streams, consts, wide_mask, filt_blocks, tables, columns, size
     )
-    after_mix = x_zero + jnp.dot(mixer, full_out, preferred_element_type=F32)
-    normed_two = layer_norm(after_mix, full_gain_two).astype(BF)
-    inner_act = jnp.dot(normed_two, full_up, preferred_element_type=F32)
-    active = jax.nn.gelu(inner_act).astype(BF)
-    result = (after_mix + jnp.dot(active, full_down, preferred_element_type=F32)).astype(BF)
+    grad_result = jnp.swapaxes(cotangent[0], 0, 1).reshape(rows, width)
+    result, grad_after, grad_mixer, grad_gain_two, grad_out, column_down, grad_up = feed_forward_call(
+        mixer, by_bucket.reshape(rows, width), wide_mask, grad_result, consts, full_out, full_up, early, columns[2]
+    )
     result = jnp.swapaxes(result.reshape(buckets, size, width), 0, 1).reshape(1, size, buckets, width)
 
-    grad_result = jnp.swapaxes(cotangent[0], 0, 1).reshape(rows, width)
-    grad_active = jnp.dot(grad_result, full_down.T, preferred_element_type=F32)
-    _, gelu_pull = jax.vjp(jax.nn.gelu, inner_act)
-    grad_inner = gelu_pull(grad_active)[0].astype(BF)
-    grad_down = jnp.dot(active.T, grad_result, preferred_element_type=F32).astype(BF)
-    grad_up = jnp.dot(normed_two.T, grad_inner, preferred_element_type=F32).astype(BF)
-    grad_normed_two = jnp.dot(grad_inner, full_up.T, preferred_element_type=F32)
-    _, norm_two_pull = jax.vjp(layer_norm, after_mix, full_gain_two)
-    grad_after_part, grad_gain_two = norm_two_pull(grad_normed_two)
-    grad_after = grad_result.astype(F32) + grad_after_part
-    grad_mix = grad_after.astype(BF)
-    grad_out = jnp.dot(mixer.T, grad_mix, preferred_element_type=F32).astype(BF)
-    grad_mixer = jnp.dot(grad_mix, full_out.T, preferred_element_type=F32).astype(BF)
-
-    (grad_projected, grad_filt, sums), (sum_down, sum_up, sum_out) = backward_call(
-        streams, consts, wide_mask, grad_mixer, convolved, kept, filt_blocks, tables, (grad_down, grad_up, grad_out), size
+    (grad_projected, grad_filt, sums), (sum_down, *late) = backward_call(
+        streams, consts, wide_mask, grad_mixer, convolved, kept, filt_blocks, tables, (column_down, grad_up, grad_out), size
     )
     grad_in = jnp.dot(normed_one.T, grad_projected, preferred_element_type=F32).astype(BF)
     grad_normed_one = jnp.dot(grad_projected, full_in.T, preferred_element_type=F32)
@@ -1195,10 +1548,10 @@
 
     _, hidden_pull = jax.vjp(hidden_of, filter_first, filter_bias, frequency)
     grad_first, grad_bias, grad_freq = hidden_pull(grad_hidden)
-    vec = jnp.concatenate([sums[:10], grad_gain_one[None], grad_gain_two[None], jnp.zeros((4, width), F32)])
+    vec = jnp.concatenate([sums[:10], grad_gain_one[None], grad_gain_two, jnp.zeros((4, width), F32)])
     fst = jnp.concatenate([grad_first, grad_bias[None], grad_freq[None]])
     fst = jnp.pad(fst, ((0, -fst.shape[0] % 8), (0, 128 - filt_width)))
-    sum_in, small = scatter_sums(grad_in, vec, grad_second, fst)
+    sum_in, small, (sum_up, sum_out) = scatter_sums(grad_in, vec, grad_second, fst, late)
     gain_sums = lax.dynamic_slice_in_dim(small[10:12], seq_place * part, part, 1)
     return (
         result,

time: 527 us -> 451 us (0.86); the launches traced: 518 us -> 448 us
  matrix products: 95.7 us -> 32.5 us
    pallas_call x2 -> x3, Pallas kernels: 98.1 us -> 202 us  [the longest x1 69.1 us: start_call(): pl.pallas_call(functools.partial(start_kernel, count), out_shape=[jax.Sha...]
    pallas_call x1, Pallas kernels: 155 us -> 85.3 us  [backward_call(): pl.pallas_call(functools.partial(backward_kernel, size, count), out_shape...]
    dot_general x9 -> x0, matrix products: 63.4 us -> none  [the longest x1 14.5 us: slice_body(): inner_act = jnp.dot(normed_two, full_up, preferred_element_type=F32)]
    pallas_call x1, Pallas kernels: 124 us -> 86.8 us  [forward_call(): pl.pallas_call(functools.partial(forward_kernel, size), out_shape=[jax.Sh...]
    unnamed x70 -> x46, local copies, waits for them, and re-layouts: 10.7 us -> 8.29 us
where the time goes in v2:
time: 451 us; the launch traced here: 448 us
  Pallas kernels  374 us (83%)
  matrix products  32.5 us (7%)
  local copies, waits for them, and re-layouts  26.9 us (6%)
  other arithmetic  13.2 us (3%)
    pallas_call x1, Pallas kernels, forward_call(): pl.pallas_call(functools.partial(forward_kernel, size), out_shape=[jax.Sh...  86.8 us
    pallas_call x1, Pallas kernels, backward_call(): pl.pallas_call(functools.partial(backward_kernel, size, count), out_shape...  85.3 us
    pallas_call x1, Pallas kernels, start_call(): pl.pallas_call(functools.partial(start_kernel, count), out_shape=[jax.Sha...  69.1 us
    pallas_call x1, Pallas kernels, feed_forward_call(): pl.pallas_call(feed_forward_kernel, out_shape=[jax.ShapeDtypeStruct(wide,...  67 us
    pallas_call x1, Pallas kernels, scatter_sums(): pl.pallas_call(functools.partial(scatter_kernel, count), out_shape=[jax.S...  65.7 us

profile of v2, /device:TPU:0, one launch (start us, length us, event | category | flops | bytes accessed | tf_op | source)
XLA Modules:
  0.0 447.9 jit_solution(10665408630271160938)
XLA Ops:
  0.8 0.8 and_convert_fusion
  1.8 0.7 maximum_convert_fusion
  2.5 0.7 fusion.21
  3.3 1.6 fusion
  4.9 1.8 multiply_reduce_fusion.2
  6.8 0.7 maximum_maximum_fusion.1.refs_0_
  7.4 0.5 multiply_cosine_fusion
  8.0 0.8 broadcast_in_dim.28.refs_2_
  8.8 0.6 convolution_add_fusion
  9.8 0.6 slice.48.refs_1_
  10.4 4.7 %convolution_multiply_fusion = f32[2048,128]{1,0:T(8,128)} fusion(f32[64,128]{1,0:T(8,128)S(1)} %copy-done, f32[128]{0:T(128)S(1)} %multiply_add_fusion, f32[2048]{0:T(1024)S(1)} %multiply_negate_fusion, f32[2048,64]{0,1:T(8,128)S(1)} %convolution_add_fusion, f32[64]{0:T(128)S(1)} %copy-done.13), kind=kOutput, calls=%fused_computation.3 | convolution fusion | flops 201981952 | bytes 1614592 | tf_op jit(solution)/shard_map/dot_general | solution.py:1519
  15.1 1.3 copy.39
  16.4 69.1 %shard_map.299 = (f32[16,1024]{1,0:T(8,128)}, bf16[2,16,1024]{2,1,0:T(8,128)(2,1)}, bf16[4,2,2,2,32,3072]{5,4,3,2,1,0:T(8,128)(2,1)}, bf16[4,32,1024]{2,1,0:T(8,...) custom-call(f32[16,128]{1,0:T(8,128)} %maximum_maximum_fusion.1.refs_0_, ...), custom_call_target="tpu_custom_call" | custom-call | tf_op jit(solution)/shard_map/pallas_call | solution.py:520
  85.5 1.0 multiply_reduce_fusion.6
  86.5 1.0 multiply_reduce_fusion.5
  87.7 0.8 slice.37
  88.4 0.9 fusion.15
  89.4 0.5 multiply_convert_fusion.1
  89.9 1.0 copy-done.5
  90.9 8.1 %convolution_convert_fusion.1.refs_0_ = bf16[544,3072]{1,0:T(8,128)(2,1)} fusion(bf16[1024,3072]{1,0:T(8,128)(2,1)} %bitcast.120, bf16[32,1024]{1,0:T(8,128)(2,1)S(1)} %fusion.15, bf16[512,1024]{1,0:T(8,128)(2,1)S(1)} %multiply_convert_fusion.1), kind=kOutput, calls=%fused_computation.1 | convolution fusion | flops 3426451456 | bytes 10747904 | tf_op jit(solution)/shard_map/dot_general | solution.py:1512
  99.0 86.8 %shard_map.300 = (bf16[512,1024]{1,0:T(8,128)(2,1)}, bf16[8,256,256]{2,1,0:T(8,128)(2,1)}, bf16[8,256,256]{2,1,0:T(8,128)(2,1)}, bf16[4,2,2,2,32,1024]{5,4,3,2,1...) custom-call(bf16[544,3072]{1,0:T(8,128)(2,1)} %convolution_convert_fusion.1.refs_0_, ...), custom_call_target="tpu_custom_call" | custom-call | tf_op jit(solution)/shard_map/pallas_call | solution.py:994
  185.8 67.0 %shard_map.301 = (bf16[512,1024]{1,0:T(8,128)(2,1)}, f32[512,1024]{1,0:T(8,128)}, bf16[512,1024]{1,0:T(8,128)(2,1)}, f32[1,1024]{1,0:T(1,128)}, bf16[1024,1024]{...) custom-call(bf16[512,1024]{1,0:T(8,128)(2,1)} %get-tuple-element.49.refs_0_, ...), custom_call_target="tpu_custom_call" | custom-call | tf_op jit(solution)/shard_map/pallas_call | solution.py:942
  252.8 85.3 %shard_map.302 = (bf16[512,3072]{1,0:T(8,128)(2,1)}, f32[8,256,128]{2,1,0:T(8,128)}, f32[16,1024]{1,0:T(8,128)}, f32[128,1024]{1,0:T(8,128)}, bf16[4,32,4096]{2,...) custom-call(bf16[544,3072]{1,0:T(8,128)(2,1)} %convolution_convert_fusion.1.refs_0_, ...), custom_call_target="tpu_custom_call" | custom-call | tf_op jit(solution)/shard_map/pallas_call | solution.py:1023
  338.2 6.9 %multiply_reduce_fusion = (f32[1024]{0:T(1024)S(1)}, f32[512]{0:T(512)S(1)}, f32[512,1024]{1,0:T(8,128)S(1)}) fusion(f32[512]{0:T(512)S(1)} %rsqrt.22, f32[512]{0:T(512)S(1)} %bitcast.108, f32[512]{0:T(512)S(1)} %bitcast.104, bf16[1,256,2,1024]{3,1,2,0:T(8,128)(2,1)S(1)} %copy-done.2, f32[1024]{0:T(1024)S(1)} %bitcast.100, ...), kind=kOutput, calls=%fused_computation.6 | convolution fusion | flops 3225942528 | bytes 12599296 | tf_op jit(solution)/shard_map/dot_general | solution.py:1536
  345.1 0.9 fusion.22
  346.0 0.7 maximum_maximum_fusion.refs_1_
  346.7 0.3 multiply_convert_fusion
  347.1 0.9 copy-done.9
  348.0 6.9 %copy_bitcast_fusion = (bf16[1,256,2,1024]{3,2,1,0:T(2,128)(2,1)}, bf16[1,256,2,1024]{3,2,1,0:T(2,128)(2,1)}) fusion(bf16[2,256,1024]{2,1,0:T(8,128)(2,1)S(1)} %bitcast.92, bf16[2,256,1024]{2,1,0:T(8,128)(2,1)S(1)} %bitcast.96), kind=kLoop, calls=%fused_computation.19 | loop fusion | bytes 4194304 | tf_op jit(solution)/shard_map/reshape | solution.py:1540
  354.9 0.3 bitcast_multiply_fusion
  355.2 3.1 fusion.7.refs_2_
  358.3 2.9 multiply_reduce_fusion.4
  361.3 0.6 fusion.5
  361.9 0.6 select_maximum_fusion.refs_3_
  362.5 5.5 %convolution_convert_fusion = bf16[1024,3072]{1,0:T(8,128)(2,1)} fusion(bf16[512,1024]{1,0:T(8,128)(2,1)S(1)} %copy-done.6, bf16[512,3072]{1,0:T(8,128)(2,1)S(1)} %copy-done.18), kind=kOutput, calls=%fused_computation | convolution fusion | flops 3224371200 | bytes 10485760 | tf_op jit(solution)/shard_map/dot_general | solution.py:1535
  368.1 65.7 %shard_map.303 = (f32[32,3072]{1,0:T(8,128)}, f32[120,128]{1,0:T(8,128)}, f32[32,4096]{1,0:T(8,128)}, f32[32,1024]{1,0:T(8,128)}) custom-call(bf16[4,2,2,2,32,3072]{5,4,3,2,1,0:T(8,128)(2,1)} %bitcast.90, f32[16,1024]{1,0:T(8,128)} %maximum_maximum_fusion.refs_1_, f32[64,128]{1,0:T(8,128)} %fusion.7.refs_2_, f32[40,128]{1,0:T(8,128)} %select_maximum_fusion.refs_3_, ...), custom_call_target="tpu_custom_call" | custom-call | tf_op jit(solution)/shard_map/pallas_call | solution.py:1284
  433.8 1.2 slice_bitcast_fusion.2
  435.0 0.7 slice.39
  435.8 0.5 slice_bitcast_fusion.3
  436.3 1.3 slice_bitcast_fusion
  437.6 0.7 slice.42
  438.3 0.6 reshape.330
  438.9 1.3 slice.44
  440.2 1.4 slice.47
  441.6 1.8 copy.56
  443.4 1.6 copy.57
  444.9 1.9 copy.58
  446.8 0.8 copy.59
  (66 shorter events, 1.0 us)
Async XLA Ops:
  0.6 9.8 %copy-start = (f32[64,128]{1,0:T(8,128)S(1)}, f32[64,128]{1,0:T(8,128)}, u32[]{:S(2)}) copy-start(f32[64,128]{1,0:T(8,128)} %param.33) | copy-start | bytes 98308
  0.7 8.8 %copy-start.3 = (bf16[1,256,2,1024]{3,2,1,0:T(2,128)(2,1)S(1)}, bf16[1,256,2,1024]{3,2,1,0:T(2,128)(2,1)}, u32[]{:S(2)}) copy-start(bf16[1,256,2,1024]{3,2,1,0:T(2,128)(2,1)} %param.20) | copy-start | bytes 3145732
  0.7 8.2 %copy-start.17 = (f32[64]{0:T(128)S(1)}, f32[64]{0:T(128)}, u32[]{:S(2)}) copy-start(f32[64]{0:T(128)} %param.31) | copy-start | bytes 772
  0.7 8.2 %copy-start.12 = (f32[33,64]{1,0:T(8,128)S(1)}, f32[33,64]{1,0:T(8,128)}, u32[]{:S(2)}) copy-start(f32[33,64]{1,0:T(8,128)} %param.30) | copy-start | bytes 25348
  0.7 6.1 %copy-start.16 = (f32[128]{0:T(128)S(1)}, f32[128]{0:T(128)}, u32[]{:S(2)}) copy-start(f32[128]{0:T(128)} %param.29) | copy-start | bytes 1540
  0.7 6.0 %copy-start.14 = (f32[3,3,128]{2,1,0:T(4,128)S(1)}, f32[3,3,128]{2,1,0:T(4,128)}, u32[]{:S(2)}) copy-start(f32[3,3,128]{2,1,0:T(4,128)} %param.28) | copy-start | bytes 13828
  4.9 5.5 %copy-start.13 = (f32[64]{0:T(128)S(1)}, f32[64]{0:T(128)}, u32[]{:S(2)}) copy-start(f32[64]{0:T(128)} %param.32) | copy-start | bytes 772
  9.5 5.7 %copy-start.8 = (bf16[1,256,2,1024]{3,2,1,0:T(2,128)(2,1)S(1)}, bf16[1,256,2,1024]{3,2,1,0:T(2,128)(2,1)}, u32[]{:S(2)}) copy-start(bf16[1,256,2,1024]{3,2,1,0:T(2,128)(2,1)} %param.34) | copy-start | bytes 3145732
  9.8 79.6 %copy-start.1 = (bf16[1,256,2,1024]{3,1,2,0:T(8,128)(2,1)}, bf16[1,256,2,1024]{3,1,2,0:T(8,128)(2,1)S(1)}, u32[]{:S(2)}) copy-start(bf16[1,256,2,1024]{3,1,2,0:T(8,128)(2,1)S(1)} %copy.51) | copy-start | bytes 3145732
  89.9 1.1 copy-start.5
  252.8 85.3 %copy-start.2 = (bf16[1,256,2,1024]{3,1,2,0:T(8,128)(2,1)S(1)}, bf16[1,256,2,1024]{3,1,2,0:T(8,128)(2,1)}, u32[]{:S(2)}) copy-start(bf16[1,256,2,1024]{3,1,2,0:T(8,128)(2,1)} %copy-done.1) | copy-start | bytes 3145732
  345.1 0.9 copy-start.11
  345.1 0.9 copy-start.15
  345.1 1.6 copy-start.4
  346.7 1.2 copy-start.9
  348.0 6.9 %copy-start.7 = (f32[8,256,128]{2,1,0:T(8,128)S(1)}, f32[8,256,128]{2,1,0:T(8,128)}, u32[]{:S(2)}) copy-start(f32[8,256,128]{2,1,0:T(8,128)} %get-tuple-element.64) | copy-start | bytes 3145732
  355.2 7.3 %copy-start.6 = (bf16[512,1024]{1,0:T(8,128)(2,1)S(1)}, bf16[512,1024]{1,0:T(8,128)(2,1)}, u32[]{:S(2)}) copy-start(bf16[512,1024]{1,0:T(8,128)(2,1)} %copy-done.5) | copy-start | bytes 3145732
  355.2 7.3 %copy-start.18 = (bf16[512,3072]{1,0:T(8,128)(2,1)S(1)}, bf16[512,3072]{1,0:T(8,128)(2,1)}, u32[]{:S(2)}) copy-start(bf16[512,3072]{1,0:T(8,128)(2,1)} %get-tuple-element.61) | copy-start | bytes 9437188
  433.8 13.0 %copy-start.10 = (f32[128,1024]{1,0:T(8,128)S(1)}, f32[128,1024]{1,0:T(8,128)}, u32[]{:S(2)}) copy-start(f32[128,1024]{1,0:T(8,128)} %get-tuple-element.113) | copy-start | bytes 1572868
